TPU v7x, 256 devices: a whole 4x4x8 slice. The times are simulated.
256 devices in a mesh: tm: 32 (over y, z), tile: 8 (over x, core).
Axes of the slice: x: 4, y: 4, z: 8, core: 2. Of those that a mesh axis runs over, the one named last changes fastest.
Arguments:
- features: bfloat16 [256, 2, 256, 256], P('tile', None, 'tm'), may hold values from -6 to 6
- cotangent: bfloat16 [256, 2, 256, 256], P('tile', None, 'tm'), may hold values from -6 to 6
- valid_dates: int32 [256, 256], P('tile', 'tm'), may hold values from 0 to 1, as said below
- gain_first: float32 [256], replicated, may hold values from 0.1 to 1.9
- qkv_weight: bfloat16 [256, 768], replicated, may hold values from -0.75625 to 0.75625
- out_weight: bfloat16 [256, 256], replicated, may hold values from -0.375 to 0.375
- gain_second: float32 [256], replicated, may hold values from 0.1 to 1.9
- up_weight: bfloat16 [256, 1024], replicated, may hold values from -0.375 to 0.375
- down_weight: bfloat16 [1024, 256], replicated, may hold values from -0.1875 to 0.1875
Outputs:
- feature_grad: bfloat16 [256, 2, 256, 256], P('tile', None, 'tm')
- qkv_grad: float32 [256, 768], replicated
- out_grad: float32 [256, 256], replicated
- up_grad: float32 [256, 1024], replicated
- down_grad: float32 [1024, 256], replicated
Inputs may be any that keep to these rules, and one draw needn't show every extreme that they name: `valid_dates`: for every block and every index of tm, between 1 and 4 of the 8 dates that this index holds are valid; in every tile group some block has exactly 4 valid dates on every index of tm.
All inputs are finite; a program needn't handle non-finite values.
Results may differ from a plain program's by a relative error of at most 0.01.
The roundings to bfloat16 on the way count: a program that leaves them out, or rounds other values in their place, can miss the bound.
Values may be sent and summed in bfloat16 or wider, within the bound.
No kernel may reach another device: no remote copies, remote signals or barrier semaphores. Data moves between devices by JAX's collectives and lax.ppermute only.
A program may use at most 64 MiB of HBM per device.

v0:
```python
import jax
import jax.numpy as jnp
from jax import lax
from jax.sharding import PartitionSpec as P

HEADS = 16


EPS = 1e-05
GELU_C = 0.7978845608028654
GELU_A = 0.044715


def gelu_tanh(inputs):
    inner = GELU_C * (inputs + GELU_A * inputs * inputs * inputs)
    return 0.5 * inputs * (1.0 + jnp.tanh(inner))


def gelu_slope(inputs):
    inner = GELU_C * (inputs + GELU_A * inputs * inputs * inputs)
    tangent = jnp.tanh(inner)
    return 0.5 * (1.0 + tangent) + 0.5 * inputs * (1.0 - tangent * tangent) * GELU_C * (
        1.0 + 3.0 * GELU_A * inputs * inputs
    )


def norm_rows(hidden):
    centre = hidden - jnp.mean(hidden, axis=-1, keepdims=True)
    inverse = lax.rsqrt(jnp.mean(centre * centre, axis=-1, keepdims=True) + EPS)
    return (centre * inverse, inverse)


def norm_back(normed, inverse, gain, upstream):
    scaled = upstream * gain
    return inverse * (
        scaled
        - jnp.mean(scaled, axis=-1, keepdims=True)
        - normed * jnp.mean(scaled * normed, axis=-1, keepdims=True)
    )


def outer_rows(left, right):
    return lax.dot_general(
        left, right, (((0,), (0,)), ((), ())), preferred_element_type=jnp.float32
    )


def back_dot(left, weight):
    return lax.dot_general(
        left, weight, (((1,), (1,)), ((), ())), preferred_element_type=jnp.float32
    )


def masked_scores(query_blk, key_blk, keep_row, factor):
    scores = (
        jnp.einsum("lhe,mhe->hlm", query_blk, key_blk, preferred_element_type=jnp.float32) * factor
    )
    return jnp.where(keep_row[None, None, :] > 0, scores, -1e30)


def layer_backward(
    features,
    cotangent,
    keep_mask,
    gain_first,
    qkv_weight,
    out_weight,
    gain_second,
    up_weight,
    down_weight,
    head_count,
):
    seq_count, length, model_width = features.shape
    head_dim = model_width // head_count
    factor = float(head_dim) ** (-0.5)
    row_count = seq_count * length
    keep_col = keep_mask.reshape(row_count, 1).astype(jnp.float32)
    inputs = features.reshape(row_count, model_width).astype(jnp.float32)
    upstream = (cotangent.reshape(row_count, model_width).astype(jnp.float32) * keep_col).astype(
        jnp.bfloat16
    )
    normed_one, inverse_one = norm_rows(inputs)
    first_in = (normed_one * gain_first).astype(jnp.bfloat16)
    projected = jnp.dot(first_in, qkv_weight, preferred_element_type=jnp.float32).astype(
        jnp.bfloat16
    )
    projected = projected.reshape(seq_count, length, 3, head_count, head_dim)
    queries = projected[:, :, 0]
    key_rows = projected[:, :, 1]
    value_rows = projected[:, :, 2]

    def attend_block(pieces):
        query_blk, key_blk, value_blk, keep_row = pieces
        scores = masked_scores(query_blk, key_blk, keep_row, factor)
        highest = jnp.max(scores, axis=-1, keepdims=True)
        powered = jnp.exp(scores - highest)
        denominator = jnp.sum(powered, axis=-1, keepdims=True)
        attn_probs = (powered / denominator).astype(jnp.bfloat16)
        attended = jnp.einsum(
            "hlm,mhe->lhe", attn_probs, value_blk, preferred_element_type=jnp.float32
        ).astype(jnp.bfloat16)
        return (attended, highest, denominator)

    attended, highest, denominator = lax.map(
        attend_block, (queries, key_rows, value_rows, keep_mask)
    )
    attended_rows = attended.reshape(row_count, model_width)
    residual = inputs + jnp.dot(attended_rows, out_weight, preferred_element_type=jnp.float32)
    normed_two, inverse_two = norm_rows(residual)
    second_in = (normed_two * gain_second).astype(jnp.bfloat16)
    pre_act = jnp.dot(second_in, up_weight, preferred_element_type=jnp.float32)
    activated = gelu_tanh(pre_act).astype(jnp.bfloat16)
    down_grad = outer_rows(activated, upstream)
    hidden_grad = (back_dot(upstream, down_weight) * gelu_slope(pre_act)).astype(jnp.bfloat16)
    up_grad = outer_rows(second_in, hidden_grad)
    resid_grad = upstream.astype(jnp.float32) + norm_back(
        normed_two, inverse_two, gain_second, back_dot(hidden_grad, up_weight)
    )
    resid_half = resid_grad.astype(jnp.bfloat16)
    out_grad = outer_rows(attended_rows, resid_half)
    attended_grad = (
        back_dot(resid_half, out_weight)
        .astype(jnp.bfloat16)
        .reshape(seq_count, length, head_count, head_dim)
    )

    def attend_back(pieces):
        query_blk, key_blk, value_blk, keep_row, highest_blk, denom_blk, grad_blk = pieces
        scores = masked_scores(query_blk, key_blk, keep_row, factor)
        attn_full = jnp.exp(scores - highest_blk) / denom_blk
        attn_probs = attn_full.astype(jnp.bfloat16)
        prob_grad = jnp.einsum(
            "lhe,mhe->hlm", grad_blk, value_blk, preferred_element_type=jnp.float32
        )
        score_grad = (
            attn_full
            * (prob_grad - jnp.sum(attn_full * prob_grad, axis=-1, keepdims=True))
            * factor
        ).astype(jnp.bfloat16)
        query_grad = jnp.einsum(
            "hlm,mhe->lhe", score_grad, key_blk, preferred_element_type=jnp.float32
        )
        key_grad = jnp.einsum(
            "hlm,lhe->mhe", score_grad, query_blk, preferred_element_type=jnp.float32
        )
        value_grad = jnp.einsum(
            "hlm,lhe->mhe", attn_probs, grad_blk, preferred_element_type=jnp.float32
        )
        return jnp.stack([query_grad, key_grad, value_grad], axis=1).astype(jnp.bfloat16)

    proj_grad = lax.map(
        attend_back, (queries, key_rows, value_rows, keep_mask, highest, denominator, attended_grad)
    )
    proj_grad = proj_grad.reshape(row_count, 3 * model_width)
    qkv_grad = outer_rows(first_in, proj_grad)
    feature_grad = (
        resid_grad + norm_back(normed_one, inverse_one, gain_first, back_dot(proj_grad, qkv_weight))
    ) * keep_col
    feature_grad = feature_grad.astype(jnp.bfloat16).reshape(seq_count, length, model_width)
    return (feature_grad, (qkv_grad, out_grad, up_grad, down_grad))


def per_device(
    features,
    cotangent,
    valid_dates,
    gain_first,
    qkv_weight,
    out_weight,
    gain_second,
    up_weight,
    down_weight,
):
    block_count, pix_count, date_count, model_width = features.shape
    time_devices = lax.axis_size("tm")
    tile_devices = lax.axis_size("tile")
    keep_local = valid_dates.astype(jnp.bfloat16)
    sent_keep = keep_local[:, None, :]
    got_feat, got_cot, got_keep = (
        lax.all_to_all(features, "tm", split_axis=0, concat_axis=2, tiled=True),
        lax.all_to_all(cotangent, "tm", split_axis=0, concat_axis=2, tiled=True),
        lax.all_to_all(sent_keep, "tm", split_axis=0, concat_axis=2, tiled=True),
    )
    own_blocks = got_feat.shape[0]
    seq_len = got_feat.shape[2]
    keep_rows = jnp.broadcast_to(got_keep, (own_blocks, pix_count, seq_len)).reshape(
        own_blocks * pix_count, seq_len
    )
    block_grad, partials = layer_backward(
        got_feat.reshape(own_blocks * pix_count, seq_len, model_width),
        got_cot.reshape(own_blocks * pix_count, seq_len, model_width),
        keep_rows,
        gain_first,
        qkv_weight,
        out_weight,
        gain_second,
        up_weight,
        down_weight,
        HEADS,
    )
    returned = lax.all_to_all(
        block_grad.reshape(own_blocks, pix_count, seq_len, model_width),
        "tm",
        split_axis=2,
        concat_axis=0,
        tiled=True,
    )
    grad_scale = float(block_count * tile_devices * pix_count * date_count * time_devices) ** (-0.5)
    scaled = tuple((partial_term * grad_scale for partial_term in partials))
    summed = lax.psum(scaled, ("tm", "tile"))
    qkv_grad, out_grad, up_grad, down_grad = summed
    return (returned, qkv_grad, out_grad, up_grad, down_grad)


def solution(mesh):
    in_specs = (
        P("tile", None, "tm", None),
        P("tile", None, "tm", None),
        P("tile", "tm"),
        P(),
        P(),
        P(),
        P(),
        P(),
        P(),
    )
    out_specs = (P("tile", None, "tm", None), P(), P(), P(), P())
    return jax.shard_map(
        per_device, mesh=mesh, in_specs=in_specs, out_specs=out_specs, check_vma=False
    )
```

profile of v0, /device:TPU:1, one launch (start us, length us, event | category | flops | bytes accessed | tf_op | source)
XLA Modules:
  0.0 404.7 jit_solution(2547918679555537822)
XLA Ops:
  8.1 20.5 %all_to_all.45 = bf16[32,1,8]{2,1,0:T(2,128)(2,1)S(1)} all-to-all(bf16[32,1,8]{2,1,0:T(2,128)(2,1)S(1)} %copy.69), channel_id=1, replica_groups=mesh['tm'=32,'tile'=8] {'tm'}, dimensions={0} | all-to-all | bytes 1024 | tf_op jit(solution)/shard_map/all_to_all | solution.py:182
  28.5 3.9 all-to-all-start.2
  32.6 9.5 %all-to-all-done.2 = bf16[32,2,8,256]{3,2,1,0:T(8,128)(2,1)S(1)} async-done(((bf16[32,2,8,256]{3,2,1,0:T(8,128)(2,1)}), bf16[32,2,8,256]{3,2,1,0:T(8,128)(2,1)S(1)}, u32[]{:S(2)}, u32[]{:S(2)}) %all-to-all-start.2) | async-done | bytes 262176 | tf_op jit(solution)/shard_map/all_to_all | solution.py:180
  42.1 5.1 %all-to-all-start = ((bf16[32,2,8,256]{3,2,1,0:T(8,128)(2,1)}), bf16[32,2,8,256]{3,2,1,0:T(8,128)(2,1)S(1)}, u32[]{:S(2)}, u32[]{:S(2)}) async-start(bf16[32,2,8,256]{3,2,1,0:T(8,128)(2,1)} %param.14), calls=%async_computation | async-start | bytes 524288 | tf_op jit(solution)/shard_map/all_to_all | solution.py:181
  48.4 8.5 %all-to-all-done = bf16[32,2,8,256]{3,2,1,0:T(8,128)(2,1)S(1)} async-done(((bf16[32,2,8,256]{3,2,1,0:T(8,128)(2,1)}), bf16[32,2,8,256]{3,2,1,0:T(8,128)(2,1)S(1)}, u32[]{:S(2)}, u32[]{:S(2)}) %all-to-all-start) | async-done | bytes 262176 | tf_op jit(solution)/shard_map/all_to_all | solution.py:181
  59.6 7.8 %while.24 = (s32[]{:T(128)}, bf16[2,256,16,16]{1,3,2,0:T(8,128)(2,1)}, f32[2,16,256,1]{2,1,3,0:T(8,128)}, f32[2,16,256,1]{2,1,3,0:T(8,128)}, bf16[2,256,16,16]{1...) while((s32[]{:T(128)}, ...), condition=%wide.region_5.6_spmd, body=%wide.region_2.5_spmd.sunk | while | flops 79749888 | bytes 15356069 | solution.py:104
  70.1 1.9 convolution_multiply_fusion
  71.9 1.4 fusion.79
  74.0 1.6 convolution_multiply_fusion.1
  77.5 44.4 %while.25 = (s32[]{:T(128)}, bf16[2,256,3,16,16]{1,4,3,2,0:T(8,128)(2,1)}, bf16[2,256,16,16]{1,3,2,0:T(8,128)(2,1)S(1)}, bf16[2,256]{1,0:T(2,128)(2,1)S(1)}, bf1...) while((s32[]{:T(128)}, ...), condition=%wide.region_12.13_spmd, body=%wide.region_10.12_spmd.sunk | while | flops 184886528 | bytes 71405008 | solution.py:151
  79.8 1.9 copy-done.1
  82.3 2.7 fusion.145
  85.1 6.9 %fusion.147 = bf16[1,256,1,16,16]{1,4,3,2,0:T(8,128)(2,1)S(1)} fusion(f32[16,256,256]{1,2,0:T(8,128)} %copy-done.1, f32[16,256,256]{1,2,0:T(8,128)} %fusion.145, bf16[2,256,16,16]{1,3,2,0:T(8,128)(2,1)S(1)} %get-tuple-element.397, s32[]{:T(128)S(6)} %copy.119), kind=kOutput, calls=%fused_computation.39.clone.1 | convolution fusion | flops 38867200 | bytes 17039364 | tf_op jit(solution)/shard_map/while/body/eval_jaxpr/hlm,mhe->lhe/dot_general | solution.py:140
  92.0 6.8 %fusion.146 = bf16[1,256,1,16,16]{1,4,3,2,0:T(8,128)(2,1)S(1)} fusion(f32[16,256,256]{1,2,0:T(8,128)} %copy-done.1, f32[16,256,256]{1,2,0:T(8,128)} %fusion.145, bf16[2,256,16,16]{1,3,2,0:T(8,128)(2,1)S(1)} %get-tuple-element.399, s32[]{:T(128)S(6)} %copy.119), kind=kOutput, calls=%fused_computation.38.clone.1 | convolution fusion | flops 38867200 | bytes 17039364 | tf_op jit(solution)/shard_map/while/body/eval_jaxpr/hlm,lhe->mhe/dot_general | solution.py:143
  101.8 1.9 copy-done.1
  104.4 2.7 fusion.145
  107.1 6.9 %fusion.147 = bf16[1,256,1,16,16]{1,4,3,2,0:T(8,128)(2,1)S(1)} fusion(f32[16,256,256]{1,2,0:T(8,128)} %copy-done.1, f32[16,256,256]{1,2,0:T(8,128)} %fusion.145, bf16[2,256,16,16]{1,3,2,0:T(8,128)(2,1)S(1)} %get-tuple-element.397, s32[]{:T(128)S(6)} %copy.119), kind=kOutput, calls=%fused_computation.39.clone.1 | convolution fusion | flops 38867200 | bytes 17039364 | tf_op jit(solution)/shard_map/while/body/eval_jaxpr/hlm,mhe->lhe/dot_general | solution.py:140
  114.1 6.8 %fusion.146 = bf16[1,256,1,16,16]{1,4,3,2,0:T(8,128)(2,1)S(1)} fusion(f32[16,256,256]{1,2,0:T(8,128)} %copy-done.1, f32[16,256,256]{1,2,0:T(8,128)} %fusion.145, bf16[2,256,16,16]{1,3,2,0:T(8,128)(2,1)S(1)} %get-tuple-element.399, s32[]{:T(128)S(6)} %copy.119), kind=kOutput, calls=%fused_computation.38.clone.1 | convolution fusion | flops 38867200 | bytes 17039364 | tf_op jit(solution)/shard_map/while/body/eval_jaxpr/hlm,lhe->mhe/dot_general | solution.py:143
  121.8 2.0 copy.81
  127.7 14.1 %all_to_all.46 = bf16[1,2,256,256]{3,1,0,2:T(2,128)(2,1)S(1)} all-to-all(bf16[1,2,256,256]{3,1,0,2:T(2,128)(2,1)S(1)} %copy.82), channel_id=1, replica_groups=mesh['tm'=32,'tile'=8] {'tm'}, dimensions={2} | all-to-all | bytes 524288 | tf_op jit(solution)/shard_map/all_to_all | solution.py:201
  142.6 248.2 %all-reduce.3.cloned.1.call-done = (f32[256,768]{1,0:T(8,128)}, f32[256,256]{1,0:T(8,128)}, f32[256,1024]{1,0:T(8,128)}, f32[1024,256]{1,0:T(8,128)}) async-done(((f32[256,768]{1,0:T(8,128)}, f32[256,256]{1,0:T(8,128)}, f32[256,1024]{1,0:T(8,128)}, f32[1024,256]{1,0:T(8,128)}), (f32[256,768]{1,0:T(8,128)}, f32[256,256]{1,0:T(8,128)}, f32[256,1024]{1,0:T(8,128)}, ...) | async-done | bytes 3145744 | tf_op jit(solution)/shard_map/psum | solution.py:210
  390.7 2.2 copy.129
  392.9 1.7 copy.130
  394.5 2.3 copy.131
  (116 shorter events, 30.4 us)
Async XLA Ops:
  7.2 62.4 %copy-start = (bf16[256,1024]{1,0:T(8,128)(2,1)S(1)}, bf16[256,1024]{1,0:T(8,128)(2,1)}, u32[]{:S(2)}) copy-start(bf16[256,1024]{1,0:T(8,128)(2,1)} %param.20) | copy-start | bytes 1572868
  7.2 50.7 %copy-start.7 = (bf16[256,768]{1,0:T(8,128)(2,1)S(1)}, bf16[256,768]{1,0:T(8,128)(2,1)}, u32[]{:S(2)}) copy-start(bf16[256,768]{1,0:T(8,128)(2,1)} %param.17) | copy-start | bytes 1179652
  28.5 13.6 %all-to-all-start.2 = ((bf16[32,2,8,256]{3,2,1,0:T(8,128)(2,1)}), bf16[32,2,8,256]{3,2,1,0:T(8,128)(2,1)S(1)}, u32[]{:S(2)}, u32[]{:S(2)}) async-start(bf16[32,2,8,256]{3,2,1,0:T(8,128)(2,1)} %param.13), calls=%async_computation.2 | async-start | bytes 524288 | tf_op jit(solution)/shard_map/all_to_all | solution.py:180
  42.1 14.8 %all-to-all-start = ((bf16[32,2,8,256]{3,2,1,0:T(8,128)(2,1)}), bf16[32,2,8,256]{3,2,1,0:T(8,128)(2,1)S(1)}, u32[]{:S(2)}, u32[]{:S(2)}) async-start(bf16[32,2,8,256]{3,2,1,0:T(8,128)(2,1)} %param.14), calls=%async_computation | async-start | bytes 524288 | tf_op jit(solution)/shard_map/all_to_all | solution.py:181
  47.2 343.5 %all-reduce.3.cloned.1.call-start = ((), (), s32[]{:S(2)}) async-start(), calls=%async_computation.4 | async-start | bytes 6291456 | tf_op jit(solution)/shard_map/psum | solution.py:210
  47.4 0.6 copy-start.5
  47.8 0.6 copy-start.9
  59.6 9.1 %copy-start.6 = (bf16[256,256]{1,0:T(8,128)(2,1)S(1)}, bf16[256,256]{1,0:T(8,128)(2,1)}, u32[]{:S(2)}) copy-start(bf16[256,256]{1,0:T(8,128)(2,1)} %param.18) | copy-start | bytes 393220
  59.7 2.0 copy-start.10
  62.8 0.7 copy-start.11
  63.5 2.0 copy-start.10
  66.7 0.7 copy-start.11
  67.4 2.1 copy-start.12
  69.5 2.4 copy-start.14
  79.7 1.9 copy-start.1
  85.1 13.7 %copy-start.3 = (bf16[2,256,3,16,16]{1,4,3,2,0:T(8,128)(2,1)S(1)}, bf16[2,256,3,16,16]{1,4,3,2,0:T(8,128)(2,1)}, u32[]{:S(2)}) copy-start(bf16[2,256,3,16,16]{1,4,3,2,0:T(8,128)(2,1)} %get-tuple-element.386) | copy-start | bytes 2359300 | tf_op jit(solution)/shard_map/while
  98.9 0.9 copy-start.4
  101.8 1.9 copy-start.1
  107.1 13.7 %copy-start.3 = (bf16[2,256,3,16,16]{1,4,3,2,0:T(8,128)(2,1)S(1)}, bf16[2,256,3,16,16]{1,4,3,2,0:T(8,128)(2,1)}, u32[]{:S(2)}) copy-start(bf16[2,256,3,16,16]{1,4,3,2,0:T(8,128)(2,1)} %get-tuple-element.386) | copy-start | bytes 2359300 | tf_op jit(solution)/shard_map/while
  120.9 0.9 copy-start.4
  121.8 4.5 %copy-start.8 = (bf16[256,768]{1,0:T(8,128)(2,1)S(1)}, bf16[256,768]{1,0:T(8,128)(2,1)}, u32[]{:S(2)}) copy-start(bf16[256,768]{1,0:T(8,128)(2,1)} %param.17) | copy-start | bytes 1179652
  121.8 4.5 %copy-start.13 = (f32[256]{0:T(256)S(1)}, f32[256]{0:T(256)}, u32[]{:S(2)}) copy-start(f32[256]{0:T(256)} %param.16) | copy-start | bytes 3076
  390.7 6.1 %copy-start.2 = (f32[1024,256]{1,0:T(8,128)S(1)}, f32[1024,256]{1,0:T(8,128)}, u32[]{:S(2)}) copy-start(f32[1024,256]{1,0:T(8,128)} %get-tuple-element.409) | copy-start | bytes 3145732
Sparse Core Ops, SparseCore 0:
  126.4 264.2 all-reduce.2
where the time goes:
time: 406 us; the launch traced here: 405 us
  waiting for transfers between devices  266 us (66%)
  matrix products  51.1 us (13%)
  blocking collectives  34.6 us (9%)
  local copies, waits for them, and re-layouts  22.6 us (6%)
  between operations  14.4 us (4%)
  starting transfers between devices  9 us (2%)
  other arithmetic  6.47 us (2%)
    psum x1, waiting for transfers between devices, per_device(): summed = lax.psum(scaled, ('tm', 'tile'))  248 us
    all_to_all x1, blocking collectives, per_device(): lax.all_to_all(sent_keep, 'tm', split_axis=0, concat_axis=2, tiled=True)  20.5 us
    all_to_all x1, blocking collectives, per_device(): lax.all_to_all(block_grad.reshape(own_blocks, pix_count, seq_len, model_w...  14.1 us
    dot_general x2, matrix products, attend_back(): jnp.einsum('hlm,mhe->lhe', score_grad, key_blk, preferred_element_type=jn...  13.8 us
    dot_general x2, matrix products, attend_back(): jnp.einsum('hlm,lhe->mhe', score_grad, query_blk, preferred_element_type=...  13.6 us
    all_to_all x1, waiting for transfers between devices, per_device(): lax.all_to_all(features, 'tm', split_axis=0, concat_axis=2, tiled=True)  9.46 us
    unnamed x29, local copies, waits for them, and re-layouts  8.57 us
    all_to_all x1, waiting for transfers between devices, per_device(): lax.all_to_all(cotangent, 'tm', split_axis=0, concat_axis=2, tiled=True)  8.48 us
  transfers between devices with their start and end apart: 3, of which 3 were waited for; matrix products, arithmetic and copies ran while one was open for 1% of the time, Pallas kernels for 0%

commit v1 on v0

v1 whole, which is shorter than its diff:
```python
import functools

import jax
import jax.numpy as jnp
from jax import lax
from jax.experimental import pallas as pl
from jax.experimental.pallas import tpu as pltpu
from jax.sharding import Mesh
from jax.sharding import PartitionSpec as P

HEADS = 16
CAP = 4
EPS = 1e-05
GELU_C = 0.7978845608028654
GELU_A = 0.044715
ABSENT = 2.0**100

F32 = jnp.float32
BF16 = jnp.bfloat16
VMEM_LIMIT = 48 * 1024 * 1024


def iota(shape, axis):
    return lax.broadcasted_iota(jnp.int32, shape, axis)


def dot(left, right, dims=((1,), (0,))):
    return lax.dot_general(left, right, (dims, ((), ())), preferred_element_type=F32)


TN = ((0,), (0,))
NT = ((1,), (1,))


def slot_matrix(valid, group, rows_per_block):
    date = iota((8, 256), 1) % 8
    day = iota((8, 256), 0)
    held = valid[group * 16 : group * 16 + 16, :].astype(F32)
    keep_all = dot(held, (day == date).astype(F32))
    rank_all = dot(held, (day < date).astype(F32))
    own = iota((16, 256), 0) == iota((16, 256), 1) // 16
    keep = jnp.sum(jnp.where(own, keep_all, 0.0), axis=0, keepdims=True)
    rank = jnp.sum(jnp.where(own, rank_all, 0.0), axis=0, keepdims=True)
    shape = (16 * rows_per_block, 256)
    row, col = iota(shape, 0), iota(shape, 1)
    match = (
        (row // rows_per_block == col // 16)
        & ((row // 4) % 2 == (col // 8) % 2)
        & (rank == (row % 4).astype(F32))
        & (keep > 0.5)
    )
    return match.astype(F32)


def compact_kernel(feat_ref, cot_ref, valid_ref, send_ref):
    valid = valid_ref[...]
    for group in range(2):
        match = slot_matrix(valid, group, 16)
        is_feat = (iota((256, 1), 0) // 8) % 2 == 0
        pick_feat = jnp.where(is_feat, match, 0.0).astype(BF16)
        pick_cot = jnp.where(is_feat, 0.0, match).astype(BF16)
        rows = pl.ds(group * 256, 256)
        got = dot(pick_feat, feat_ref[rows, :]) + dot(pick_cot, cot_ref[rows, :])
        filled = jnp.sum(match, axis=1, keepdims=True) > 0.5
        got = jnp.where(is_feat & jnp.logical_not(filled), ABSENT, got)
        send_ref[rows, :] = got.astype(BF16)


def expand_kernel(back_ref, valid_ref, out_ref):
    valid = valid_ref[...]
    for group in range(2):
        match = slot_matrix(valid, group, 8).astype(BF16)
        back = back_ref[pl.ds(group * 128, 128), :]
        out_ref[pl.ds(group * 256, 256), :] = dot(match, back, TN).astype(BF16)


def row_mean(values):
    return jnp.sum(values, axis=-1, keepdims=True) * (1.0 / values.shape[-1])


def norm_rows(hidden):
    centre = hidden - row_mean(hidden)
    inverse = lax.rsqrt(row_mean(centre * centre) + EPS)
    return centre * inverse, inverse


def norm_back(normed, inverse, gain, upstream):
    scaled = upstream * gain
    return inverse * (scaled - row_mean(scaled) - normed * row_mean(scaled * normed))


def layer_kernel(
    scale,
    recv_ref,
    gain_first_ref,
    qkv_ref,
    out_w_ref,
    gain_second_ref,
    up_ref,
    down_ref,
    grad_ref,
    terms_ref,
    probs,
    proj_t,
    att_t,
    att_grad_t,
    proj_grad_t,
):
    core = lax.axis_index("c")

    def put(group, columns, value):
        terms_ref[(group % 2) ^ core, group // 2, :, columns] = (value * scale).astype(BF16)

    token = iota((256, 512), 0)
    target = (token % 128) // 4 * 16 + token // 128 * 4 + token % 4
    source = iota((256, 512), 1)
    recv = recv_ref[...]
    inputs = dot((source == target).astype(BF16), recv)
    upstream = dot((source == target + 8).astype(BF16), recv).astype(BF16)
    keep = inputs[:, 0:1] < 0.5 * ABSENT
    inputs = jnp.where(keep, inputs, 0.0)
    gain_first = gain_first_ref[...]
    gain_second = gain_second_ref[...]

    normed_one, inverse_one = norm_rows(inputs)
    first_in = (normed_one * gain_first).astype(BF16)
    proj_t[...] = dot(qkv_ref[...], first_in, ((0,), (1,))).astype(BF16)

    def attend(head, carry):
        at = pl.multiple_of(head * 16, 16)
        for pix in range(2):
            cols = pl.ds(pix * 128, 128)
            query = proj_t[pl.ds(at, 16), cols]
            key = proj_t[pl.ds(256 + at, 16), cols]
            value = proj_t[pl.ds(512 + at, 16), cols]
            scores = dot(key, query, TN) * 0.25
            scores = jnp.where(keep[pix * 128 : pix * 128 + 128], scores, -1e30)
            powered = jnp.exp(scores - jnp.max(scores, axis=0, keepdims=True))
            full = powered * (1.0 / jnp.sum(powered, axis=0, keepdims=True))
            probs[pix, head] = full
            att_t[pl.ds(at, 16), cols] = dot(value, full.astype(BF16)).astype(BF16)
        return carry

    lax.fori_loop(0, HEADS, attend, 0, unroll=4)

    attended_t = att_t[...]
    out_w = out_w_ref[...]
    residual = inputs + dot(attended_t, out_w, TN)
    normed_two, inverse_two = norm_rows(residual)
    second_in = (normed_two * gain_second).astype(BF16)
    back = jnp.zeros((256, 256), F32)
    for part in range(4):
        cols = pl.ds(part * 256, 256)
        up_part = up_ref[:, cols]
        pre = dot(second_in, up_part)
        tangent = jnp.tanh(GELU_C * (pre + GELU_A * pre * pre * pre))
        activated = (0.5 * pre * (1.0 + tangent)).astype(BF16)
        slope = 0.5 * (1.0 + tangent) + 0.5 * pre * (1.0 - tangent * tangent) * GELU_C * (
            1.0 + 3.0 * GELU_A * pre * pre
        )
        put(4 + part, slice(0, 256), dot(activated, upstream, TN))
        hidden_grad = (dot(upstream, down_ref[cols, :], NT) * slope).astype(BF16)
        put(part, slice(0, 256), dot(second_in, hidden_grad, TN))
        back = back + dot(hidden_grad, up_part, NT)
    resid_grad = upstream.astype(F32) + norm_back(normed_two, inverse_two, gain_second, back)
    resid_half = resid_grad.astype(BF16)
    out_grad = dot(attended_t, resid_half)
    put(6, slice(256, 384), out_grad[:, :128])
    put(7, slice(256, 384), out_grad[:, 128:])
    att_grad_t[...] = dot(out_w, resid_half, NT).astype(BF16)

    def attend_back(head, carry):
        at = pl.multiple_of(head * 16, 16)
        for pix in range(2):
            cols = pl.ds(pix * 128, 128)
            query = proj_t[pl.ds(at, 16), cols]
            key = proj_t[pl.ds(256 + at, 16), cols]
            value = proj_t[pl.ds(512 + at, 16), cols]
            grad = att_grad_t[pl.ds(at, 16), cols]
            full = probs[pix, head]
            prob_grad = dot(value, grad, TN)
            total = jnp.sum(full * prob_grad, axis=0, keepdims=True)
            score_grad = (full * (prob_grad - total) * 0.25).astype(BF16)
            proj_grad_t[pl.ds(at, 16), cols] = dot(key, score_grad).astype(BF16)
            proj_grad_t[pl.ds(256 + at, 16), cols] = dot(query, score_grad, NT).astype(BF16)
            proj_grad_t[pl.ds(512 + at, 16), cols] = dot(grad, full.astype(BF16), NT).astype(BF16)
        return carry

    lax.fori_loop(0, HEADS, attend_back, 0, unroll=4)

    grad_t = proj_grad_t[...]
    first_t = first_in.T
    for part in range(3):
        qkv_grad = dot(first_t, grad_t[part * 256 : part * 256 + 256], NT)
        put(2 * part, slice(256, 384), qkv_grad[:, :128])
        put(2 * part + 1, slice(256, 384), qkv_grad[:, 128:])
    first_back = dot(grad_t, qkv_ref[...], ((0,), (1,)))
    grad = resid_grad + norm_back(normed_one, inverse_one, gain_first, first_back)
    grad = jnp.where(keep, grad, 0.0).astype(BF16)
    slot = iota((256, 256), 0)
    want = slot // 4 % 2 * 128 + slot // 8 * 4 + slot % 4
    grad_ref[...] = dot((iota((256, 256), 1) == want).astype(BF16), grad).astype(BF16)


def spread_kernel(mine_ref, other_ref, qkv_ref, out_ref, up_ref, down_ref):
    core = lax.axis_index("c")
    for group in range(8):
        flip = (group % 2) ^ core
        near, far = mine_ref[group // 2], other_ref[group // 2]
        piece = jnp.where(flip == 0, near.astype(F32), far.astype(F32))
        if group < 4:
            up_ref[:, pl.ds(group * 256, 256)] = piece[:, :256]
        else:
            down_ref[pl.ds((group - 4) * 256, 256), :] = piece[:, :256]
        if group < 6:
            qkv_ref[:, pl.ds(group * 128, 128)] = piece[:, 256:]
        else:
            out_ref[:, pl.ds((group - 6) * 128, 128)] = piece[:, 256:]


def run(kernel, out_shape, *args, scratch=()):
    return pl.pallas_call(
        kernel,
        out_shape=out_shape,
        scratch_shapes=list(scratch),
        compiler_params=pltpu.CompilerParams(vmem_limit_bytes=VMEM_LIMIT),
    )(*args)


def sum_leading(parts):
    return jnp.sum(parts.astype(F32), axis=0).astype(BF16)


def per_device(
    features,
    cotangent,
    valid_dates,
    gain_first,
    qkv_weight,
    out_weight,
    gain_second,
    up_weight,
    down_weight,
):
    shape = jax.ShapeDtypeStruct
    width = features.shape[-1]
    scale = float(256 * 2 * 256) ** (-0.5)
    with jax.named_scope("compact"):
        send = run(
            compact_kernel,
            shape((512, width), BF16),
            features.reshape(512, width),
            cotangent.reshape(512, width),
            valid_dates,
        )
    with jax.named_scope("to_owner"):
        recv = lax.all_to_all(
            send.reshape(32, 16, width), ("y", "z"), split_axis=0, concat_axis=0, tiled=True
        )
    with jax.named_scope("layer"):
        grad, terms = run(
            functools.partial(layer_kernel, scale),
            (shape((256, width), BF16), shape((2, 4, 256, 384), BF16)),
            recv.reshape(512, width),
            gain_first.reshape(1, width),
            qkv_weight,
            out_weight,
            gain_second.reshape(1, width),
            up_weight,
            down_weight,
            scratch=(
                pltpu.VMEM((2, HEADS, 128, 128), F32),
                pltpu.VMEM((768, 256), BF16),
                pltpu.VMEM((256, 256), BF16),
                pltpu.VMEM((256, 256), BF16),
                pltpu.VMEM((768, 256), BF16),
            ),
        )
    with jax.named_scope("core_sum"):
        other = lax.ppermute(terms[1], "c", [(0, 1), (1, 0)])
        halves = (terms[0].astype(F32) + other.astype(F32)).astype(BF16)
    with jax.named_scope("x_sum"):
        halves = lax.all_to_all(halves, "x", split_axis=0, concat_axis=0, tiled=True)
        part = sum_leading(halves)
    with jax.named_scope("yz_sum"):
        joint = jnp.concatenate(
            [part.reshape(32, 8, 384), grad.reshape(32, 8, width)], axis=2
        )
        joint = lax.all_to_all(joint, ("y", "z"), split_axis=0, concat_axis=0, tiled=True)
        total = sum_leading(joint[:, :, :384])
        back = joint[:, :, 384:]
    with jax.named_scope("yz_gather"):
        part = lax.all_to_all(
            jnp.broadcast_to(total[None], (32, 8, 384)),
            ("y", "z"),
            split_axis=0,
            concat_axis=0,
            tiled=True,
        ).reshape(256, 384)
    with jax.named_scope("x_gather"):
        mine = lax.all_gather(part, "x", axis=0)
    with jax.named_scope("core_gather"):
        other = lax.ppermute(mine, "c", [(0, 1), (1, 0)])
    with jax.named_scope("spread"):
        outs = run(
            spread_kernel,
            (
                shape((256, 768), F32),
                shape((256, 256), F32),
                shape((256, 1024), F32),
                shape((1024, 256), F32),
            ),
            mine,
            other,
        )
    with jax.named_scope("expand"):
        feature_grad = run(
            expand_kernel, shape((512, width), BF16), back.reshape(256, width), valid_dates
        )
    return (feature_grad.reshape(features.shape), *outs)


def solution(mesh):
    fine = Mesh(mesh.devices.reshape(4, 8, 4, 2), ("y", "z", "x", "c"))
    dates, tiles = ("y", "z"), ("x", "c")
    in_specs = (
        P(tiles, None, dates, None),
        P(tiles, None, dates, None),
        P(tiles, dates),
        P(),
        P(),
        P(),
        P(),
        P(),
        P(),
    )
    out_specs = (P(tiles, None, dates, None), P(), P(), P(), P())
    return jax.shard_map(
        per_device, mesh=fine, in_specs=in_specs, out_specs=out_specs, check_vma=False
    )
```

time: 406 us -> 114 us (0.28)
  waiting for transfers between devices: 266 us -> 2.71 us
  matrix products: 51.1 us -> 0 us
  blocking collectives: 34.6 us -> 77.3 us
  local copies, waits for them, and re-layouts: 22.6 us -> 6.12 us
  Pallas kernels: 0 us -> 15.7 us
  between operations: 14.4 us -> 0.71 us
  other arithmetic: 6.47 us -> 0.42 us
    psum x1 -> x0, waiting for transfers between devices: 248 us -> none  [per_device(): summed = lax.psum(scaled, ('tm', 'tile'))]
    dot_general x25 -> x0, matrix products: 51.1 us -> none  [the longest x2 13.8 us: attend_back(): jnp.einsum('hlm,mhe->lhe', score_grad, key_blk, preferred_element_type=jn...]
    all_to_all x2 -> x4, blocking collectives: 34.6 us -> 65.9 us  [the longest x1 21.5 us: per_device(): lax.all_to_all(send.reshape(32, 16, width), ('y', 'z'), split_axis=0, con...]
    all_to_all x2 -> x0, waiting for transfers between devices: 17.9 us -> none  [the longest x1 9.46 us: per_device(): lax.all_to_all(features, 'tm', split_axis=0, concat_axis=2, tiled=True)]
    pallas_call x0 -> x4, Pallas kernels: none -> 15.7 us  [run(): pl.pallas_call(kernel, out_shape=out_shape, scratch_shapes=list(scratch),...]
    all_gather x0 -> x1, blocking collectives: none -> 11.4 us  [per_device(): mine = lax.all_gather(part, 'x', axis=0)]
    ppermute x0 -> x2, starting transfers between devices: none -> 11.1 us  [the longest x1 7.23 us: per_device(): other = lax.ppermute(mine, 'c', [(0, 1), (1, 0)])]
    while x26 -> x0, local copies, waits for them, and re-layouts: 9.05 us -> none
  transfers between devices with their start and end apart: 3 -> 2, of which waited for: 3 -> 2; matrix products, arithmetic and copies ran while one was open for 1% -> 0% of each run, Pallas kernels for 0% -> 1%
where the time goes in v1:
time: 114 us
  blocking collectives  77.3 us (68%)
  Pallas kernels  15.7 us (14%)
  starting transfers between devices  11.1 us (10%)
  local copies, waits for them, and re-layouts  6.12 us (5%)
  waiting for transfers between devices  2.71 us (2%)
    all_to_all x1, blocking collectives, per_device(): lax.all_to_all(send.reshape(32, 16, width), ('y', 'z'), split_axis=0, con...  21.5 us
    pallas_call x4, Pallas kernels, run(): pl.pallas_call(kernel, out_shape=out_shape, scratch_shapes=list(scratch),...  15.7 us
    all_to_all x1, blocking collectives, per_device(): lax.all_to_all(jnp.broadcast_to(total[None], (32, 8, 384)), ('y', 'z'), s...  15.3 us
    all_to_all x1, blocking collectives, per_device(): lax.all_to_all(halves, 'x', split_axis=0, concat_axis=0, tiled=True)  15.2 us
    all_to_all x1, blocking collectives, per_device(): lax.all_to_all(joint, ('y', 'z'), split_axis=0, concat_axis=0, tiled=True)  13.9 us
    all_gather x1, blocking collectives, per_device(): mine = lax.all_gather(part, 'x', axis=0)  11.4 us
    ppermute x1, starting transfers between devices, per_device(): other = lax.ppermute(mine, 'c', [(0, 1), (1, 0)])  7.23 us
    unnamed x17, local copies, waits for them, and re-layouts  6.01 us
  transfers between devices with their start and end apart: 2, of which 2 were waited for; matrix products, arithmetic and copies ran while one was open for 0% of the time, Pallas kernels for 1%

profile of v1, /device:TPU:1, one launch (start us, length us, event | category | flops | bytes accessed | tf_op | source)
XLA Modules:
  0.0 114.0 jit_solution(13580975723267902666)
XLA Ops:
  0.7 0.8 copy.16.valid_ref
  1.5 0.9 copy-done.3
  2.5 0.9 copy-done.4
  3.4 0.4 compact.1
  3.8 21.5 %all_to_all.20 = bf16[32,16,256]{2,1,0:T(8,128)(2,1)S(1)} all-to-all(bf16[32,16,256]{2,1,0:T(8,128)(2,1)S(1)} %bitcast.17), channel_id=1, replica_groups=mesh['y'=4,'z'=8,'x'=4,'c'=2] {'y','z'}, dimensions={0} | all-to-all | bytes 524288 | tf_op jit(solution)/shard_map/to_owner/all_to_all | solution.py:257
  25.4 0.0 copy-done
  25.4 1.0 copy-done.2
  26.4 0.9 copy-done.5
  27.3 0.7 copy-done.6
  28.0 0.7 copy-done.7
  28.6 12.4 %layer.1 = (bf16[256,256]{1,0:T(8,128)(2,1)S(1)}, bf16[2,4,256,384]{3,2,1,0:T(8,128)(2,1)S(1)}) custom-call(bf16[512,256]{1,0:T(8,128)(2,1)S(1)} %bitcast.18, f32[1,256]{1,0:T(1,128)S(1)} %bitcast.22, bf16[256,768]{1,0:T(8,128)(2,1)S(1)} %copy-done.2, bf16[256,256]{1,0:T(8,128)(2,1)S(1)} %copy-done.5, f32[1,256]{1,0:T(1,128)S(1)} %bitcast.23, ...), custom_call_target="tpu_custom_call" | custom-call | tf_op jit(solution)/shard_map/layer/pallas_call | solution.py:222
  41.1 0.1 slice_bitcast_fusion
  41.2 3.8 %collective-permute-start = (bf16[4,256,384]{2,1,0:T(8,128)(2,1)S(1)}, bf16[4,256,384]{2,1,0:T(8,128)(2,1)S(1)}, u32[]{:S(2)}, u32[]{:S(2)}) collective-permute-start(bf16[4,256,384]{2,1,0:T(8,128)(2,1)S(1)} %slice_bitcast_fusion), channel_id=1, source_target_pairs={{0,1},{1,0},{2,3},{3,2},{4,5},{5,4},{6,7},{7,6},{8,9},{9,8},{10,11... | collective-permute-start | bytes 2359304 | tf_op jit(solution)/shard_map/core_sum/ppermute | solution.py:280
  45.0 1.9 %collective-permute-done = bf16[4,256,384]{2,1,0:T(8,128)(2,1)S(1)} collective-permute-done((bf16[4,256,384]{2,1,0:T(8,128)(2,1)S(1)}, bf16[4,256,384]{2,1,0:T(8,128)(2,1)S(1)}, u32[]{:S(2)}, u32[]{:S(2)}) %collective-permute-start) | collective-permute-done | bytes 786464 | tf_op jit(solution)/shard_map/core_sum/ppermute | solution.py:280
  46.9 0.2 fusion
  47.1 15.2 %all_to_all.21 = bf16[4,256,384]{2,1,0:T(8,128)(2,1)S(1)} all-to-all(bf16[4,256,384]{2,1,0:T(8,128)(2,1)S(1)} %fusion), channel_id=1, replica_groups=mesh['y'=4,'z'=8,'x'=4,'c'=2] {'x'}, dimensions={0} | all-to-all | bytes 1572864 | tf_op jit(solution)/shard_map/x_sum/all_to_all | solution.py:283
  62.3 0.2 reduce_sum.24
  62.5 13.9 %all_to_all.22 = bf16[32,8,640]{2,1,0:T(8,128)(2,1)S(1)} all-to-all(bf16[32,8,640]{2,1,0:T(8,128)(2,1)S(1)} %pad_maximum_fusion), channel_id=1, replica_groups=mesh['y'=4,'z'=8,'x'=4,'c'=2] {'y','z'}, dimensions={0} | all-to-all | bytes 655360 | tf_op jit(solution)/shard_map/yz_sum/all_to_all | solution.py:289
  76.5 15.3 %all_to_all.23 = bf16[32,8,384]{2,1,0:T(8,128)(2,1)S(1)} all-to-all(bf16[32,8,384]{2,1,0:T(8,128)(2,1)S(1)} %broadcast_in_dim.2), channel_id=1, replica_groups=mesh['y'=4,'z'=8,'x'=4,'c'=2] {'y','z'}, dimensions={0} | all-to-all | bytes 393216 | tf_op jit(solution)/shard_map/yz_gather/all_to_all | solution.py:293
  91.8 11.4 %all_gather.3.mine_ref = bf16[4,256,384]{2,1,0:T(8,128)(2,1)S(1)} all-gather(bf16[1,256,384]{2,1,0:T(8,128)(2,1)S(1)} %bitcast.25), channel_id=1, replica_groups=mesh['y'=4,'z'=8,'x'=4,'c'=2] {'x'}, dimensions={0}, use_global_device_ids=true | all-gather | bytes 983040 | tf_op jit(solution)/shard_map/x_gather/all_gather | solution.py:301
  103.1 7.2 %collective-permute-start.1 = (bf16[4,256,384]{2,1,0:T(8,128)(2,1)S(1)}, bf16[4,256,384]{2,1,0:T(8,128)(2,1)S(1)}, u32[]{:S(2)}, u32[]{:S(2)}) collective-permute-start(bf16[4,256,384]{2,1,0:T(8,128)(2,1)S(1)} %all_gather.3.mine_ref), channel_id=1, source_target_pairs={{0,1},{1,0},{2,3},{3,2},{4,5},{5,4},{6,7},{7,6},{8,9},{9,8},{10,11... | collective-permute-start | bytes 2359304 | tf_op jit(solution)/shard_map/core_gather/ppermute | solution.py:303
  110.4 1.1 expand.1
  111.5 0.8 collective-permute-done.1.other_ref
  112.3 1.8 %spread.1 = (f32[256,768]{1,0:T(8,128)}, f32[256,256]{1,0:T(8,128)}, f32[256,1024]{1,0:T(8,128)}, f32[1024,256]{1,0:T(8,128)}) custom-call(bf16[4,256,384]{2,1,0:T(8,128)(2,1)S(1)} %all_gather.3.mine_ref, bf16[4,256,384]{2,1,0:T(8,128)(2,1)S(1)} %collective-permute-done.1.other_ref), custom_call_target="tpu_custom_call" | custom-call | tf_op jit(solution)/shard_map/spread/pallas_call | solution.py:222
  (13 shorter events, 0.1 us)
Async XLA Ops:
  0.6 24.7 %copy-start.1 = (bf16[1024,256]{1,0:T(8,128)(2,1)S(1)}, bf16[1024,256]{1,0:T(8,128)(2,1)}, u32[]{:S(2)}) copy-start(bf16[1024,256]{1,0:T(8,128)(2,1)} %down_ref.1) | copy-start | bytes 1572868
  0.6 24.7 %copy-start = (bf16[256,1024]{1,0:T(8,128)(2,1)S(1)}, bf16[256,1024]{1,0:T(8,128)(2,1)}, u32[]{:S(2)}) copy-start(bf16[256,1024]{1,0:T(8,128)(2,1)} %up_ref.1) | copy-start | bytes 1572868
  1.5 0.9 copy-start.3
  2.5 0.9 copy-start.4
  25.4 1.0 copy-start.2
  26.4 0.9 copy-start.5
  27.3 0.7 copy-start.6
  27.9 0.7 copy-start.7
  41.2 5.7 %collective-permute-start = (bf16[4,256,384]{2,1,0:T(8,128)(2,1)S(1)}, bf16[4,256,384]{2,1,0:T(8,128)(2,1)S(1)}, u32[]{:S(2)}, u32[]{:S(2)}) collective-permute-start(bf16[4,256,384]{2,1,0:T(8,128)(2,1)S(1)} %slice_bitcast_fusion), channel_id=1, source_target_pairs={{0,1},{1,0},{2,3},{3,2},{4,5},{5,4},{6,7},{7,6},{8,9},{9,8},{10,11... | collective-permute-start | bytes 2359304 | tf_op jit(solution)/shard_map/core_sum/ppermute | solution.py:280
  103.1 9.1 %collective-permute-start.1 = (bf16[4,256,384]{2,1,0:T(8,128)(2,1)S(1)}, bf16[4,256,384]{2,1,0:T(8,128)(2,1)S(1)}, u32[]{:S(2)}, u32[]{:S(2)}) collective-permute-start(bf16[4,256,384]{2,1,0:T(8,128)(2,1)S(1)} %all_gather.3.mine_ref), channel_id=1, source_target_pairs={{0,1},{1,0},{2,3},{3,2},{4,5},{5,4},{6,7},{7,6},{8,9},{9,8},{10,11... | collective-permute-start | bytes 2359304 | tf_op jit(solution)/shard_map/core_gather/ppermute | solution.py:303

commit v2 on v1

--- a/solution.py
+++ b/solution.py
@@ -52,26 +52,32 @@
     return match.astype(F32)
 
 
-def compact_kernel(feat_ref, cot_ref, valid_ref, send_ref):
+def compact_kernel(feat_hbm, cot_hbm, valid_ref, send_ref, feat, cot, arrived):
+    copies = []
+    for group in range(2):
+        rows = pl.ds(group * 256, 256)
+        copies.append(
+            [
+                pltpu.make_async_copy(feat_hbm.at[rows], feat.at[rows], arrived.at[group, 0]),
+                pltpu.make_async_copy(cot_hbm.at[rows], cot.at[rows], arrived.at[group, 1]),
+            ]
+        )
+    for pair in copies:
+        for copy in pair:
+            copy.start()
     valid = valid_ref[...]
     for group in range(2):
         match = slot_matrix(valid, group, 16)
         is_feat = (iota((256, 1), 0) // 8) % 2 == 0
         pick_feat = jnp.where(is_feat, match, 0.0).astype(BF16)
         pick_cot = jnp.where(is_feat, 0.0, match).astype(BF16)
+        filled = jnp.sum(match, axis=1, keepdims=True) > 0.5
         rows = pl.ds(group * 256, 256)
-        got = dot(pick_feat, feat_ref[rows, :]) + dot(pick_cot, cot_ref[rows, :])
-        filled = jnp.sum(match, axis=1, keepdims=True) > 0.5
+        for copy in copies[group]:
+            copy.wait()
+        got = dot(pick_feat, feat[rows, :]) + dot(pick_cot, cot[rows, :])
         got = jnp.where(is_feat & jnp.logical_not(filled), ABSENT, got)
         send_ref[rows, :] = got.astype(BF16)
-
-
-def expand_kernel(back_ref, valid_ref, out_ref):
-    valid = valid_ref[...]
-    for group in range(2):
-        match = slot_matrix(valid, group, 8).astype(BF16)
-        back = back_ref[pl.ds(group * 128, 128), :]
-        out_ref[pl.ds(group * 256, 256), :] = dot(match, back, TN).astype(BF16)
 
 
 def row_mean(values):
@@ -92,24 +98,57 @@
 def layer_kernel(
     scale,
     recv_ref,
+    gain_first_hbm,
+    qkv_hbm,
+    out_w_hbm,
+    gain_second_hbm,
+    up_hbm,
+    down_hbm,
+    grad_ref,
+    mine_ref,
+    theirs_ref,
     gain_first_ref,
     qkv_ref,
     out_w_ref,
     gain_second_ref,
     up_ref,
     down_ref,
-    grad_ref,
-    terms_ref,
+    arrived,
     probs,
     proj_t,
     att_t,
     att_grad_t,
     proj_grad_t,
 ):
+    copies = [
+        pltpu.make_async_copy(held, ref, arrived.at[at])
+        for at, (held, ref) in enumerate(
+            (
+                (gain_first_hbm, gain_first_ref),
+                (qkv_hbm, qkv_ref),
+                (out_w_hbm, out_w_ref),
+                (gain_second_hbm, gain_second_ref),
+                (up_hbm, up_ref),
+                (down_hbm, down_ref),
+            )
+        )
+    ]
+    for copy in copies:
+        copy.start()
     core = lax.axis_index("c")
+    place = lax.axis_index("x")
 
     def put(group, columns, value):
-        terms_ref[(group % 2) ^ core, group // 2, :, columns] = (value * scale).astype(BF16)
+        slot = lax.rem(group // 2 - place + 4, 4)
+        value = (value * scale).astype(BF16)
+
+        @pl.when(core == group % 2)
+        def _():
+            mine_ref[slot, :, columns] = value
+
+        @pl.when(core != group % 2)
+        def _():
+            theirs_ref[slot, :, columns] = value
 
     token = iota((256, 512), 0)
     target = (token % 128) // 4 * 16 + token // 128 * 4 + token % 4
@@ -119,8 +158,9 @@
     upstream = dot((source == target + 8).astype(BF16), recv).astype(BF16)
     keep = inputs[:, 0:1] < 0.5 * ABSENT
     inputs = jnp.where(keep, inputs, 0.0)
+    copies[0].wait()
+    copies[1].wait()
     gain_first = gain_first_ref[...]
-    gain_second = gain_second_ref[...]
 
     normed_one, inverse_one = norm_rows(inputs)
     first_in = (normed_one * gain_first).astype(BF16)
@@ -143,6 +183,9 @@
 
     lax.fori_loop(0, HEADS, attend, 0, unroll=4)
 
+    for copy in copies[2:]:
+        copy.wait()
+    gain_second = gain_second_ref[...]
     attended_t = att_t[...]
     out_w = out_w_ref[...]
     residual = inputs + dot(attended_t, out_w, TN)
@@ -202,33 +245,63 @@
     grad_ref[...] = dot((iota((256, 256), 1) == want).astype(BF16), grad).astype(BF16)
 
 
+def core_sum_kernel(mine_ref, other_ref, *outs):
+    for slot, out_ref in enumerate(outs):
+        total = mine_ref[slot].astype(F32) + other_ref[slot].astype(F32)
+        out_ref[...] = total.astype(BF16)
+
+
+def x_sum_kernel(own_ref, one_ref, two_ref, three_ref, grad_ref, out_ref):
+    total = own_ref[...].astype(F32) + one_ref[...].astype(F32)
+    total = total + two_ref[...].astype(F32) + three_ref[...].astype(F32)
+    out_ref[:, :, 0:384] = total.astype(BF16).reshape(32, 8, 384)
+    out_ref[:, :, 384:640] = grad_ref[...].reshape(32, 8, 256)
+
+
+def yz_sum_kernel(joint_ref, valid_ref, total_ref, out_ref):
+    total = jnp.sum(joint_ref[:, :, 0:384].astype(F32), axis=0).astype(BF16)
+    total_ref[...] = jnp.broadcast_to(total[None], total_ref.shape)
+    valid = valid_ref[...]
+    for group in range(2):
+        match = slot_matrix(valid, group, 8).astype(BF16)
+        back = joint_ref[group * 16 : group * 16 + 16, :, 384:640].reshape(128, 256)
+        out_ref[pl.ds(group * 256, 256), :] = dot(match, back, TN).astype(BF16)
+
+
 def spread_kernel(mine_ref, other_ref, qkv_ref, out_ref, up_ref, down_ref):
     core = lax.axis_index("c")
     for group in range(8):
-        flip = (group % 2) ^ core
-        near, far = mine_ref[group // 2], other_ref[group // 2]
-        piece = jnp.where(flip == 0, near.astype(F32), far.astype(F32))
-        if group < 4:
-            up_ref[:, pl.ds(group * 256, 256)] = piece[:, :256]
-        else:
-            down_ref[pl.ds((group - 4) * 256, 256), :] = piece[:, :256]
-        if group < 6:
-            qkv_ref[:, pl.ds(group * 128, 128)] = piece[:, 256:]
-        else:
-            out_ref[:, pl.ds((group - 6) * 128, 128)] = piece[:, 256:]
-
-
-def run(kernel, out_shape, *args, scratch=()):
+        for lane in range(4):
+            rows = slice(lane * 64, lane * 64 + 64)
+            near = mine_ref[lane, group // 2].astype(F32)
+            far = other_ref[lane, group // 2].astype(F32)
+            piece = jnp.where(core == group % 2, near, far)
+            if group < 4:
+                up_ref[rows, pl.ds(group * 256, 256)] = piece[:, :256]
+            else:
+                down_ref[pl.ds((group - 4) * 256 + lane * 64, 64), :] = piece[:, :256]
+            if group < 6:
+                qkv_ref[rows, pl.ds(group * 128, 128)] = piece[:, 256:]
+            else:
+                out_ref[rows, pl.ds((group - 6) * 128, 128)] = piece[:, 256:]
+
+
+def run(kernel, out_shape, *args, scratch=(), held=()):
+    specs = [
+        pl.BlockSpec(memory_space=pltpu.HBM if at in held else pltpu.VMEM)
+        for at in range(len(args))
+    ]
     return pl.pallas_call(
         kernel,
         out_shape=out_shape,
+        in_specs=specs,
         scratch_shapes=list(scratch),
         compiler_params=pltpu.CompilerParams(vmem_limit_bytes=VMEM_LIMIT),
     )(*args)
 
 
-def sum_leading(parts):
-    return jnp.sum(parts.astype(F32), axis=0).astype(BF16)
+def shift(array, axis, size, by):
+    return lax.ppermute(array, axis, [(at, (at + by) % size) for at in range(size)])
 
 
 def per_device(
@@ -245,6 +318,7 @@
     shape = jax.ShapeDtypeStruct
     width = features.shape[-1]
     scale = float(256 * 2 * 256) ** (-0.5)
+    dates = ("y", "z")
     with jax.named_scope("compact"):
         send = run(
             compact_kernel,
@@ -252,15 +326,23 @@
             features.reshape(512, width),
             cotangent.reshape(512, width),
             valid_dates,
+            held=(0, 1),
+            scratch=(
+                pltpu.VMEM((512, width), BF16),
+                pltpu.VMEM((512, width), BF16),
+                pltpu.SemaphoreType.DMA((2, 2)),
+            ),
         )
     with jax.named_scope("to_owner"):
         recv = lax.all_to_all(
-            send.reshape(32, 16, width), ("y", "z"), split_axis=0, concat_axis=0, tiled=True
-        )
+            send.reshape(32, 16, width), dates, split_axis=0, concat_axis=0, tiled=True
+        )
+    half = shape((4, 256, 384), BF16)
+    piece = shape((256, 384), BF16)
     with jax.named_scope("layer"):
-        grad, terms = run(
+        grad, mine, theirs = run(
             functools.partial(layer_kernel, scale),
-            (shape((256, width), BF16), shape((2, 4, 256, 384), BF16)),
+            (shape((256, width), BF16), half, half),
             recv.reshape(512, width),
             gain_first.reshape(1, width),
             qkv_weight,
@@ -268,7 +350,15 @@
             gain_second.reshape(1, width),
             up_weight,
             down_weight,
+            held=range(1, 7),
             scratch=(
+                pltpu.VMEM((1, width), F32),
+                pltpu.VMEM((256, 768), BF16),
+                pltpu.VMEM((256, 256), BF16),
+                pltpu.VMEM((1, width), F32),
+                pltpu.VMEM((256, 1024), BF16),
+                pltpu.VMEM((1024, 256), BF16),
+                pltpu.SemaphoreType.DMA((6,)),
                 pltpu.VMEM((2, HEADS, 128, 128), F32),
                 pltpu.VMEM((768, 256), BF16),
                 pltpu.VMEM((256, 256), BF16),
@@ -277,30 +367,26 @@
             ),
         )
     with jax.named_scope("core_sum"):
-        other = lax.ppermute(terms[1], "c", [(0, 1), (1, 0)])
-        halves = (terms[0].astype(F32) + other.astype(F32)).astype(BF16)
+        other = shift(theirs, "c", 2, 1)
+        slots = run(core_sum_kernel, (piece,) * 4, mine, other)
     with jax.named_scope("x_sum"):
-        halves = lax.all_to_all(halves, "x", split_axis=0, concat_axis=0, tiled=True)
-        part = sum_leading(halves)
+        got = [shift(slots[by], "x", 4, by) for by in (1, 3, 2)]
+        joint = run(x_sum_kernel, shape((32, 8, 640), BF16), slots[0], *got, grad)
     with jax.named_scope("yz_sum"):
-        joint = jnp.concatenate(
-            [part.reshape(32, 8, 384), grad.reshape(32, 8, width)], axis=2
-        )
-        joint = lax.all_to_all(joint, ("y", "z"), split_axis=0, concat_axis=0, tiled=True)
-        total = sum_leading(joint[:, :, :384])
-        back = joint[:, :, 384:]
-    with jax.named_scope("yz_gather"):
-        part = lax.all_to_all(
-            jnp.broadcast_to(total[None], (32, 8, 384)),
-            ("y", "z"),
-            split_axis=0,
-            concat_axis=0,
-            tiled=True,
-        ).reshape(256, 384)
-    with jax.named_scope("x_gather"):
-        mine = lax.all_gather(part, "x", axis=0)
+        joint = lax.all_to_all(joint, dates, split_axis=0, concat_axis=0, tiled=True)
+        total, feature_grad = run(
+            yz_sum_kernel,
+            (shape((8, 8, 384), BF16), shape((512, width), BF16)),
+            joint,
+            valid_dates,
+        )
+    with jax.named_scope("z_gather"):
+        part = lax.all_to_all(total, "z", split_axis=0, concat_axis=0, tiled=True)
+    with jax.named_scope("yx_gather"):
+        part = jnp.broadcast_to(part.reshape(1, 64, 384), (16, 64, 384))
+        mine = lax.all_to_all(part, ("y", "x"), split_axis=0, concat_axis=0, tiled=True)
     with jax.named_scope("core_gather"):
-        other = lax.ppermute(mine, "c", [(0, 1), (1, 0)])
+        other = shift(mine, "c", 2, 1)
     with jax.named_scope("spread"):
         outs = run(
             spread_kernel,
@@ -310,12 +396,8 @@
                 shape((256, 1024), F32),
                 shape((1024, 256), F32),
             ),
-            mine,
-            other,
-        )
-    with jax.named_scope("expand"):
-        feature_grad = run(
-            expand_kernel, shape((512, width), BF16), back.reshape(256, width), valid_dates
+            mine.reshape(4, 4, 64, 384),
+            other.reshape(4, 4, 64, 384),
         )
     return (feature_grad.reshape(features.shape), *outs)
 

time: 114 us -> 113 us (level)
  blocking collectives: 77.3 us -> 61 us
  waiting for transfers between devices: 2.71 us -> 12.1 us
  Pallas kernels: 15.7 us -> 21.2 us
  starting transfers between devices: 11.1 us -> 13.6 us
  local copies, waits for them, and re-layouts: 6.12 us -> 4.43 us
    all_gather x1 -> x0, blocking collectives: 11.4 us -> none  [per_device(): mine = lax.all_gather(part, 'x', axis=0)]
    ppermute x2 -> x5, waiting for transfers between devices: 2.71 us -> 12.1 us  [shift(): lax.ppermute(array, axis, [(at, (at + by) % size) for at in range(size)])]
    pallas_call x4 -> x6, Pallas kernels: 15.7 us -> 21.2 us  [run(): pl.pallas_call(kernel, out_shape=out_shape, in_specs=specs, scratch_shape...]
    all_to_all x4, blocking collectives: 65.9 us -> 61 us  [the longest x1 21.7 us: per_device(): lax.all_to_all(send.reshape(32, 16, width), dates, split_axis=0, concat_a...]
    ppermute x2 -> x5, starting transfers between devices: 11.1 us -> 13.6 us  [shift(): lax.ppermute(array, axis, [(at, (at + by) % size) for at in range(size)])]
    unnamed x17, local copies, waits for them, and re-layouts: 6.01 us -> 4.33 us
  transfers between devices with their start and end apart: 2 -> 5, of which waited for: 2 -> 4; matrix products, arithmetic and copies ran while one was open for 0% -> 0% of each run, Pallas kernels for 1% -> 0%
where the time goes in v2:
time: 113 us
  blocking collectives  61 us (54%)
  Pallas kernels  21.2 us (19%)
  starting transfers between devices  13.6 us (12%)
  waiting for transfers between devices  12.1 us (11%)
  local copies, waits for them, and re-layouts  4.43 us (4%)
    all_to_all x1, blocking collectives, per_device(): lax.all_to_all(send.reshape(32, 16, width), dates, split_axis=0, concat_a...  21.7 us
    pallas_call x6, Pallas kernels, run(): pl.pallas_call(kernel, out_shape=out_shape, in_specs=specs, scratch_shape...  21.2 us
    all_to_all x1, blocking collectives, per_device(): lax.all_to_all(joint, dates, split_axis=0, concat_axis=0, tiled=True)  13.9 us
    ppermute x5, starting transfers between devices, shift(): lax.ppermute(array, axis, [(at, (at + by) % size) for at in range(size)])  13.6 us
    all_to_all x1, blocking collectives, per_device(): lax.all_to_all(part, ('y', 'x'), split_axis=0, concat_axis=0, tiled=True)  13.3 us
    ppermute x5, waiting for transfers between devices, shift(): lax.ppermute(array, axis, [(at, (at + by) % size) for at in range(size)])  12.1 us
    all_to_all x1, blocking collectives, per_device(): part = lax.all_to_all(total, 'z', split_axis=0, concat_axis=0, tiled=True)  12.1 us
    unnamed x17, local copies, waits for them, and re-layouts  4.33 us
  transfers between devices with their start and end apart: 5, of which 4 were waited for; matrix products, arithmetic and copies ran while one was open for 0% of the time, Pallas kernels for 0%

profile of v2, /device:TPU:1, one launch (start us, length us, event | category | flops | bytes accessed | tf_op | source)
XLA Modules:
  0.0 113.0 jit_solution(106292403889993377)
XLA Ops:
  0.6 0.8 copy.14.valid_ref
  1.4 0.9 copy-done.3
  2.3 0.9 copy-done.4
  3.3 1.5 %compact.1 = bf16[512,256]{1,0:T(8,128)(2,1)S(1)} custom-call(bf16[512,256]{1,0:T(8,128)(2,1)S(1)} %bitcast.14, bf16[512,256]{1,0:T(8,128)(2,1)S(1)} %bitcast.15, s32[32,8]{1,0:T(8,128)S(1)} %copy.14.valid_ref), custom_call_target="tpu_custom_call" | custom-call | tf_op jit(solution)/shard_map/compact/pallas_call | solution.py:294
  4.9 21.7 %all_to_all.20 = bf16[32,16,256]{2,1,0:T(8,128)(2,1)S(1)} all-to-all(bf16[32,16,256]{2,1,0:T(8,128)(2,1)S(1)} %bitcast.11), channel_id=1, replica_groups=mesh['y'=4,'z'=8,'x'=4,'c'=2] {'y','z'}, dimensions={0} | all-to-all | bytes 524288 | tf_op jit(solution)/shard_map/to_owner/all_to_all | solution.py:337
  26.6 0.7 copy-done.6
  27.2 1.0 copy-done.2
  28.2 16.5 %layer.1 = (bf16[256,256]{1,0:T(8,128)(2,1)S(1)}, bf16[4,256,384]{2,1,0:T(8,128)(2,1)S(1)}, bf16[4,256,384]{2,1,0:T(8,128)(2,1)S(1)}) custom-call(bf16[512,256]{1,0:T(8,128)(2,1)S(1)} %bitcast.12, f32[1,256]{1,0:T(1,128)S(1)} %bitcast.16, bf16[256,768]{1,0:T(8,128)(2,1)S(1)} %copy-done.2, bf16[256,256]{1,0:T(8,128)(2,1)S(1)} %copy-done.5, ...), custom_call_target="tpu_custom_call" | custom-call | tf_op jit(solution)/shard_map/layer/pallas_call | solution.py:294
  44.7 3.8 %collective-permute-start = (bf16[4,256,384]{2,1,0:T(8,128)(2,1)S(1)}, bf16[4,256,384]{2,1,0:T(8,128)(2,1)S(1)}, u32[]{:S(2)}, u32[]{:S(2)}) collective-permute-start(bf16[4,256,384]{2,1,0:T(8,128)(2,1)S(1)} %get-tuple-element.19), channel_id=1, source_target_pairs={{0,1},{1,0},{2,3},{3,2},{4,5},{5,4},{6,7},{7,6},{8,9},{9,8},{10,11... | collective-permute-start | bytes 2359304 | tf_op jit(solution)/shard_map/core_sum/ppermute | solution.py:304
  48.5 1.9 %collective-permute-done.other_ref = bf16[4,256,384]{2,1,0:T(8,128)(2,1)S(1)} collective-permute-done((bf16[4,256,384]{2,1,0:T(8,128)(2,1)S(1)}, bf16[4,256,384]{2,1,0:T(8,128)(2,1)S(1)}, u32[]{:S(2)}, u32[]{:S(2)}) %collective-permute-start) | collective-permute-done | bytes 786464 | tf_op jit(solution)/shard_map/core_sum/ppermute | solution.py:304
  50.4 0.2 core_sum.1
  50.6 1.3 %collective-permute-start.1 = (bf16[256,384]{1,0:T(8,128)(2,1)S(1)}, bf16[256,384]{1,0:T(8,128)(2,1)S(1)}, u32[]{:S(2)}, u32[]{:S(2)}) collective-permute-start(bf16[256,384]{1,0:T(8,128)(2,1)S(1)} %get-tuple-element.21), channel_id=1, source_target_pairs={{0,2},{2,4},{4,6},{6,0},{1,3},{3,5},{5,7},{7,1},{8,10},{10,12},{12... | collective-permute-start | bytes 589832 | tf_op jit(solution)/shard_map/x_sum/ppermute | solution.py:304
  51.9 1.5 %collective-permute-start.2 = (bf16[256,384]{1,0:T(8,128)(2,1)S(1)}, bf16[256,384]{1,0:T(8,128)(2,1)S(1)}, u32[]{:S(2)}, u32[]{:S(2)}) collective-permute-start(bf16[256,384]{1,0:T(8,128)(2,1)S(1)} %get-tuple-element.22), channel_id=1, source_target_pairs={{0,6},{2,0},{4,2},{6,4},{1,7},{3,1},{5,3},{7,5},{8,14},{10,8},{12,... | collective-permute-start | bytes 589832 | tf_op jit(solution)/shard_map/x_sum/ppermute | solution.py:304
  53.4 1.5 %collective-permute-start.3 = (bf16[256,384]{1,0:T(8,128)(2,1)S(1)}, bf16[256,384]{1,0:T(8,128)(2,1)S(1)}, u32[]{:S(2)}, u32[]{:S(2)}) collective-permute-start(bf16[256,384]{1,0:T(8,128)(2,1)S(1)} %get-tuple-element.23), channel_id=1, source_target_pairs={{0,4},{2,6},{4,0},{6,2},{1,5},{3,7},{5,1},{7,3},{8,12},{10,14},{12... | collective-permute-start | bytes 589832 | tf_op jit(solution)/shard_map/x_sum/ppermute | solution.py:304
  54.9 3.1 %collective-permute-done.1.one_ref = bf16[256,384]{1,0:T(8,128)(2,1)S(1)} collective-permute-done((bf16[256,384]{1,0:T(8,128)(2,1)S(1)}, bf16[256,384]{1,0:T(8,128)(2,1)S(1)}, u32[]{:S(2)}, u32[]{:S(2)}) %collective-permute-start.1) | collective-permute-done | bytes 196640 | tf_op jit(solution)/shard_map/x_sum/ppermute | solution.py:304
  58.0 5.2 %collective-permute-done.3.three_ref = bf16[256,384]{1,0:T(8,128)(2,1)S(1)} collective-permute-done((bf16[256,384]{1,0:T(8,128)(2,1)S(1)}, bf16[256,384]{1,0:T(8,128)(2,1)S(1)}, u32[]{:S(2)}, u32[]{:S(2)}) %collective-permute-start.3) | collective-permute-done | bytes 196640 | tf_op jit(solution)/shard_map/x_sum/ppermute | solution.py:304
  63.2 0.1 x_sum.1
  63.3 13.9 %all_to_all.21.joint_ref = bf16[32,8,640]{2,1,0:T(8,128)(2,1)S(1)} all-to-all(bf16[32,8,640]{2,1,0:T(8,128)(2,1)S(1)} %x_sum.1), channel_id=1, replica_groups=mesh['y'=4,'z'=8,'x'=4,'c'=2] {'y','z'}, dimensions={0} | all-to-all | bytes 655360 | tf_op jit(solution)/shard_map/yz_sum/all_to_all | solution.py:376
  77.3 1.1 yz_sum.1
  78.4 12.1 %all_to_all.22 = bf16[8,8,384]{2,1,0:T(8,128)(2,1)S(1)} all-to-all(bf16[8,8,384]{2,1,0:T(8,128)(2,1)S(1)} %get-tuple-element.26), channel_id=1, replica_groups=mesh['y'=4,'z'=8,'x'=4,'c'=2] {'z'}, dimensions={0} | all-to-all | bytes 98304 | tf_op jit(solution)/shard_map/z_gather/all_to_all | solution.py:384
  90.6 13.3 %all_to_all.23 = bf16[16,64,384]{2,1,0:T(8,128)(2,1)S(1)} all-to-all(bf16[16,64,384]{2,1,0:T(8,128)(2,1)S(1)} %broadcast_in_dim.8), channel_id=1, replica_groups=mesh['y'=4,'z'=8,'x'=4,'c'=2] {'y','x'}, dimensions={0} | all-to-all | bytes 1572864 | tf_op jit(solution)/shard_map/yx_gather/all_to_all | solution.py:387
  103.8 5.5 %collective-permute-start.4 = (bf16[16,64,384]{2,1,0:T(8,128)(2,1)S(1)}, bf16[16,64,384]{2,1,0:T(8,128)(2,1)S(1)}, u32[]{:S(2)}, u32[]{:S(2)}) collective-permute-start(bf16[16,64,384]{2,1,0:T(8,128)(2,1)S(1)} %all_to_all.23), channel_id=1, source_target_pairs={{0,1},{1,0},{2,3},{3,2},{4,5},{5,4},{6,7},{7,6},{8,9},{9,8},{10,11... | collective-permute-start | bytes 2359304 | tf_op jit(solution)/shard_map/core_gather/ppermute | solution.py:304
  109.4 1.9 %collective-permute-done.4 = bf16[16,64,384]{2,1,0:T(8,128)(2,1)S(1)} collective-permute-done((bf16[16,64,384]{2,1,0:T(8,128)(2,1)S(1)}, bf16[16,64,384]{2,1,0:T(8,128)(2,1)S(1)}, u32[]{:S(2)}, u32[]{:S(2)}) %collective-permute-start.4) | collective-permute-done | bytes 786464 | tf_op jit(solution)/shard_map/core_gather/ppermute | solution.py:304
  111.3 1.8 %spread.1 = (f32[256,768]{1,0:T(8,128)}, f32[256,256]{1,0:T(8,128)}, f32[256,1024]{1,0:T(8,128)}, f32[1024,256]{1,0:T(8,128)}) custom-call(bf16[4,4,64,384]{3,2,1,0:T(8,128)(2,1)S(1)} %bitcast.10, bf16[4,4,64,384]{3,2,1,0:T(8,128)(2,1)S(1)} %bitcast.13), custom_call_target="tpu_custom_call" | custom-call | tf_op jit(solution)/shard_map/spread/pallas_call | solution.py:294
  (14 shorter events, 0.1 us)
Async XLA Ops:
  1.4 0.9 copy-start.3
  2.3 0.9 copy-start.4
  3.3 23.2 %copy-start = (bf16[256,1024]{1,0:T(8,128)(2,1)S(1)}, bf16[256,1024]{1,0:T(8,128)(2,1)}, u32[]{:S(2)}) copy-start(bf16[256,1024]{1,0:T(8,128)(2,1)} %up_hbm.1) | copy-start | bytes 1572868
  3.3 23.2 %copy-start.1 = (bf16[1024,256]{1,0:T(8,128)(2,1)S(1)}, bf16[1024,256]{1,0:T(8,128)(2,1)}, u32[]{:S(2)}) copy-start(bf16[1024,256]{1,0:T(8,128)(2,1)} %down_hbm.1) | copy-start | bytes 1572868
  4.9 21.7 %copy-start.5 = (bf16[256,256]{1,0:T(8,128)(2,1)S(1)}, bf16[256,256]{1,0:T(8,128)(2,1)}, u32[]{:S(2)}) copy-start(bf16[256,256]{1,0:T(8,128)(2,1)} %out_w_hbm.1) | copy-start | bytes 393220
  4.9 21.7 %copy-start.7 = (f32[256]{0:T(256)S(1)}, f32[256]{0:T(256)}, u32[]{:S(2)}) copy-start(f32[256]{0:T(256)} %param.15) | copy-start | bytes 3076
  26.5 0.7 copy-start.6
  27.2 1.0 copy-start.2
  44.7 5.7 %collective-permute-start = (bf16[4,256,384]{2,1,0:T(8,128)(2,1)S(1)}, bf16[4,256,384]{2,1,0:T(8,128)(2,1)S(1)}, u32[]{:S(2)}, u32[]{:S(2)}) collective-permute-start(bf16[4,256,384]{2,1,0:T(8,128)(2,1)S(1)} %get-tuple-element.19), channel_id=1, source_target_pairs={{0,1},{1,0},{2,3},{3,2},{4,5},{5,4},{6,7},{7,6},{8,9},{9,8},{10,11... | collective-permute-start | bytes 2359304 | tf_op jit(solution)/shard_map/core_sum/ppermute | solution.py:304
  50.6 7.4 %collective-permute-start.1 = (bf16[256,384]{1,0:T(8,128)(2,1)S(1)}, bf16[256,384]{1,0:T(8,128)(2,1)S(1)}, u32[]{:S(2)}, u32[]{:S(2)}) collective-permute-start(bf16[256,384]{1,0:T(8,128)(2,1)S(1)} %get-tuple-element.21), channel_id=1, source_target_pairs={{0,2},{2,4},{4,6},{6,0},{1,3},{3,5},{5,7},{7,1},{8,10},{10,12},{12... | collective-permute-start | bytes 589832 | tf_op jit(solution)/shard_map/x_sum/ppermute | solution.py:304
  51.9 6.1 %collective-permute-start.2 = (bf16[256,384]{1,0:T(8,128)(2,1)S(1)}, bf16[256,384]{1,0:T(8,128)(2,1)S(1)}, u32[]{:S(2)}, u32[]{:S(2)}) collective-permute-start(bf16[256,384]{1,0:T(8,128)(2,1)S(1)} %get-tuple-element.22), channel_id=1, source_target_pairs={{0,6},{2,0},{4,2},{6,4},{1,7},{3,1},{5,3},{7,5},{8,14},{10,8},{12,... | collective-permute-start | bytes 589832 | tf_op jit(solution)/shard_map/x_sum/ppermute | solution.py:304
  53.4 9.8 %collective-permute-start.3 = (bf16[256,384]{1,0:T(8,128)(2,1)S(1)}, bf16[256,384]{1,0:T(8,128)(2,1)S(1)}, u32[]{:S(2)}, u32[]{:S(2)}) collective-permute-start(bf16[256,384]{1,0:T(8,128)(2,1)S(1)} %get-tuple-element.23), channel_id=1, source_target_pairs={{0,4},{2,6},{4,0},{6,2},{1,5},{3,7},{5,1},{7,3},{8,12},{10,14},{12... | collective-permute-start | bytes 589832 | tf_op jit(solution)/shard_map/x_sum/ppermute | solution.py:304
  103.8 7.4 %collective-permute-start.4 = (bf16[16,64,384]{2,1,0:T(8,128)(2,1)S(1)}, bf16[16,64,384]{2,1,0:T(8,128)(2,1)S(1)}, u32[]{:S(2)}, u32[]{:S(2)}) collective-permute-start(bf16[16,64,384]{2,1,0:T(8,128)(2,1)S(1)} %all_to_all.23), channel_id=1, source_target_pairs={{0,1},{1,0},{2,3},{3,2},{4,5},{5,4},{6,7},{7,6},{8,9},{9,8},{10,11... | collective-permute-start | bytes 2359304 | tf_op jit(solution)/shard_map/core_gather/ppermute | solution.py:304

commit v3 on v2

--- a/solution.py
+++ b/solution.py
@@ -52,30 +52,16 @@
     return match.astype(F32)
 
 
-def compact_kernel(feat_hbm, cot_hbm, valid_ref, send_ref, feat, cot, arrived):
-    copies = []
-    for group in range(2):
-        rows = pl.ds(group * 256, 256)
-        copies.append(
-            [
-                pltpu.make_async_copy(feat_hbm.at[rows], feat.at[rows], arrived.at[group, 0]),
-                pltpu.make_async_copy(cot_hbm.at[rows], cot.at[rows], arrived.at[group, 1]),
-            ]
-        )
-    for pair in copies:
-        for copy in pair:
-            copy.start()
+def compact_kernel(feat_ref, cot_ref, valid_ref, send_ref):
     valid = valid_ref[...]
     for group in range(2):
         match = slot_matrix(valid, group, 16)
         is_feat = (iota((256, 1), 0) // 8) % 2 == 0
         pick_feat = jnp.where(is_feat, match, 0.0).astype(BF16)
         pick_cot = jnp.where(is_feat, 0.0, match).astype(BF16)
+        rows = pl.ds(group * 256, 256)
+        got = dot(pick_feat, feat_ref[rows, :]) + dot(pick_cot, cot_ref[rows, :])
         filled = jnp.sum(match, axis=1, keepdims=True) > 0.5
-        rows = pl.ds(group * 256, 256)
-        for copy in copies[group]:
-            copy.wait()
-        got = dot(pick_feat, feat[rows, :]) + dot(pick_cot, cot[rows, :])
         got = jnp.where(is_feat & jnp.logical_not(filled), ABSENT, got)
         send_ref[rows, :] = got.astype(BF16)
 
@@ -98,57 +84,26 @@
 def layer_kernel(
     scale,
     recv_ref,
-    gain_first_hbm,
-    qkv_hbm,
-    out_w_hbm,
-    gain_second_hbm,
-    up_hbm,
-    down_hbm,
-    grad_ref,
-    mine_ref,
-    theirs_ref,
     gain_first_ref,
     qkv_ref,
     out_w_ref,
     gain_second_ref,
     up_ref,
     down_ref,
-    arrived,
+    grad_ref,
+    terms_ref,
     probs,
     proj_t,
     att_t,
     att_grad_t,
     proj_grad_t,
 ):
-    copies = [
-        pltpu.make_async_copy(held, ref, arrived.at[at])
-        for at, (held, ref) in enumerate(
-            (
-                (gain_first_hbm, gain_first_ref),
-                (qkv_hbm, qkv_ref),
-                (out_w_hbm, out_w_ref),
-                (gain_second_hbm, gain_second_ref),
-                (up_hbm, up_ref),
-                (down_hbm, down_ref),
-            )
-        )
-    ]
-    for copy in copies:
-        copy.start()
     core = lax.axis_index("c")
     place = lax.axis_index("x")
 
     def put(group, columns, value):
         slot = lax.rem(group // 2 - place + 4, 4)
-        value = (value * scale).astype(BF16)
-
-        @pl.when(core == group % 2)
-        def _():
-            mine_ref[slot, :, columns] = value
-
-        @pl.when(core != group % 2)
-        def _():
-            theirs_ref[slot, :, columns] = value
+        terms_ref[(group % 2) ^ core, slot, :, columns] = (value * scale).astype(BF16)
 
     token = iota((256, 512), 0)
     target = (token % 128) // 4 * 16 + token // 128 * 4 + token % 4
@@ -158,9 +113,8 @@
     upstream = dot((source == target + 8).astype(BF16), recv).astype(BF16)
     keep = inputs[:, 0:1] < 0.5 * ABSENT
     inputs = jnp.where(keep, inputs, 0.0)
-    copies[0].wait()
-    copies[1].wait()
     gain_first = gain_first_ref[...]
+    gain_second = gain_second_ref[...]
 
     normed_one, inverse_one = norm_rows(inputs)
     first_in = (normed_one * gain_first).astype(BF16)
@@ -183,9 +137,6 @@
 
     lax.fori_loop(0, HEADS, attend, 0, unroll=4)
 
-    for copy in copies[2:]:
-        copy.wait()
-    gain_second = gain_second_ref[...]
     attended_t = att_t[...]
     out_w = out_w_ref[...]
     residual = inputs + dot(attended_t, out_w, TN)
@@ -245,9 +196,9 @@
     grad_ref[...] = dot((iota((256, 256), 1) == want).astype(BF16), grad).astype(BF16)
 
 
-def core_sum_kernel(mine_ref, other_ref, *outs):
+def core_sum_kernel(terms_ref, other_ref, *outs):
     for slot, out_ref in enumerate(outs):
-        total = mine_ref[slot].astype(F32) + other_ref[slot].astype(F32)
+        total = terms_ref[0, slot].astype(F32) + other_ref[slot].astype(F32)
         out_ref[...] = total.astype(BF16)
 
 
@@ -286,15 +237,10 @@
                 out_ref[rows, pl.ds((group - 6) * 128, 128)] = piece[:, 256:]
 
 
-def run(kernel, out_shape, *args, scratch=(), held=()):
-    specs = [
-        pl.BlockSpec(memory_space=pltpu.HBM if at in held else pltpu.VMEM)
-        for at in range(len(args))
-    ]
+def run(kernel, out_shape, *args, scratch=()):
     return pl.pallas_call(
         kernel,
         out_shape=out_shape,
-        in_specs=specs,
         scratch_shapes=list(scratch),
         compiler_params=pltpu.CompilerParams(vmem_limit_bytes=VMEM_LIMIT),
     )(*args)
@@ -326,23 +272,16 @@
             features.reshape(512, width),
             cotangent.reshape(512, width),
             valid_dates,
-            held=(0, 1),
-            scratch=(
-                pltpu.VMEM((512, width), BF16),
-                pltpu.VMEM((512, width), BF16),
-                pltpu.SemaphoreType.DMA((2, 2)),
-            ),
         )
     with jax.named_scope("to_owner"):
         recv = lax.all_to_all(
             send.reshape(32, 16, width), dates, split_axis=0, concat_axis=0, tiled=True
         )
-    half = shape((4, 256, 384), BF16)
     piece = shape((256, 384), BF16)
     with jax.named_scope("layer"):
-        grad, mine, theirs = run(
+        grad, terms = run(
             functools.partial(layer_kernel, scale),
-            (shape((256, width), BF16), half, half),
+            (shape((256, width), BF16), shape((2, 4, 256, 384), BF16)),
             recv.reshape(512, width),
             gain_first.reshape(1, width),
             qkv_weight,
@@ -350,15 +289,7 @@
             gain_second.reshape(1, width),
             up_weight,
             down_weight,
-            held=range(1, 7),
             scratch=(
-                pltpu.VMEM((1, width), F32),
-                pltpu.VMEM((256, 768), BF16),
-                pltpu.VMEM((256, 256), BF16),
-                pltpu.VMEM((1, width), F32),
-                pltpu.VMEM((256, 1024), BF16),
-                pltpu.VMEM((1024, 256), BF16),
-                pltpu.SemaphoreType.DMA((6,)),
                 pltpu.VMEM((2, HEADS, 128, 128), F32),
                 pltpu.VMEM((768, 256), BF16),
                 pltpu.VMEM((256, 256), BF16),
@@ -367,8 +298,8 @@
             ),
         )
     with jax.named_scope("core_sum"):
-        other = shift(theirs, "c", 2, 1)
-        slots = run(core_sum_kernel, (piece,) * 4, mine, other)
+        other = shift(terms[1], "c", 2, 1)
+        slots = run(core_sum_kernel, (piece,) * 4, terms, other)
     with jax.named_scope("x_sum"):
         got = [shift(slots[by], "x", 4, by) for by in (1, 3, 2)]
         joint = run(x_sum_kernel, shape((32, 8, 640), BF16), slots[0], *got, grad)

time: 113 us -> 110 us (0.973)
  Pallas kernels: 21.2 us -> 16 us
  local copies, waits for them, and re-layouts: 4.43 us -> 6.19 us
    pallas_call x6, Pallas kernels: 21.2 us -> 16 us  [run(): pl.pallas_call(kernel, out_shape=out_shape, scratch_shapes=list(scratch),...]
    unnamed x17, local copies, waits for them, and re-layouts: 4.33 us -> 6.01 us
where the time goes in v3:
time: 110 us
  blocking collectives  60.8 us (55%)
  Pallas kernels  16 us (15%)
  starting transfers between devices  13.6 us (12%)
  waiting for transfers between devices  12.1 us (11%)
  local copies, waits for them, and re-layouts  6.19 us (6%)
    all_to_all x1, blocking collectives, per_device(): lax.all_to_all(send.reshape(32, 16, width), dates, split_axis=0, concat_a...  21.5 us
    pallas_call x6, Pallas kernels, run(): pl.pallas_call(kernel, out_shape=out_shape, scratch_shapes=list(scratch),...  16 us
    all_to_all x1, blocking collectives, per_device(): lax.all_to_all(joint, dates, split_axis=0, concat_axis=0, tiled=True)  13.9 us
    ppermute x5, starting transfers between devices, shift(): lax.ppermute(array, axis, [(at, (at + by) % size) for at in range(size)])  13.6 us
    all_to_all x1, blocking collectives, per_device(): lax.all_to_all(part, ('y', 'x'), split_axis=0, concat_axis=0, tiled=True)  13.3 us
    ppermute x5, waiting for transfers between devices, shift(): lax.ppermute(array, axis, [(at, (at + by) % size) for at in range(size)])  12.1 us
    all_to_all x1, blocking collectives, per_device(): part = lax.all_to_all(total, 'z', split_axis=0, concat_axis=0, tiled=True)  12.1 us
    unnamed x17, local copies, waits for them, and re-layouts  6.01 us
  transfers between devices with their start and end apart: 5, of which 4 were waited for; matrix products, arithmetic and copies ran while one was open for 0% of the time, Pallas kernels for 0%

profile of v3, /device:TPU:1, one launch (start us, length us, event | category | flops | bytes accessed | tf_op | source)
XLA Modules:
  0.0 109.5 jit_solution(7006193715889668727)
XLA Ops:
  0.7 0.8 copy.14.valid_ref
  1.5 0.9 copy-done.3
  2.5 0.9 copy-done.4
  3.4 0.4 compact.1
  3.8 21.5 %all_to_all.20 = bf16[32,16,256]{2,1,0:T(8,128)(2,1)S(1)} all-to-all(bf16[32,16,256]{2,1,0:T(8,128)(2,1)S(1)} %bitcast.13), channel_id=1, replica_groups=mesh['y'=4,'z'=8,'x'=4,'c'=2] {'y','z'}, dimensions={0} | all-to-all | bytes 524288 | tf_op jit(solution)/shard_map/to_owner/all_to_all | solution.py:277
  25.4 1.0 copy-done.2
  26.4 0.9 copy-done.5
  27.3 0.7 copy-done.6
  28.0 0.7 copy-done.7
  28.6 12.4 %layer.1 = (bf16[256,256]{1,0:T(8,128)(2,1)S(1)}, bf16[2,4,256,384]{3,2,1,0:T(8,128)(2,1)S(1)}) custom-call(bf16[512,256]{1,0:T(8,128)(2,1)S(1)} %bitcast.14, f32[1,256]{1,0:T(1,128)S(1)} %bitcast.18, bf16[256,768]{1,0:T(8,128)(2,1)S(1)} %copy-done.2, bf16[256,256]{1,0:T(8,128)(2,1)S(1)} %copy-done.5, f32[1,256]{1,0:T(1,128)S(1)} %bitcast.19, ...), custom_call_target="tpu_custom_call" | custom-call | tf_op jit(solution)/shard_map/layer/pallas_call | solution.py:241
  41.2 3.8 %collective-permute-start = (bf16[4,256,384]{2,1,0:T(8,128)(2,1)S(1)}, bf16[4,256,384]{2,1,0:T(8,128)(2,1)S(1)}, u32[]{:S(2)}, u32[]{:S(2)}) collective-permute-start(bf16[4,256,384]{2,1,0:T(8,128)(2,1)S(1)} %slice_bitcast_fusion), channel_id=1, source_target_pairs={{0,1},{1,0},{2,3},{3,2},{4,5},{5,4},{6,7},{7,6},{8,9},{9,8},{10,11... | collective-permute-start | bytes 2359304 | tf_op jit(solution)/shard_map/core_sum/ppermute | solution.py:250
  45.0 1.9 %collective-permute-done.other_ref = bf16[4,256,384]{2,1,0:T(8,128)(2,1)S(1)} collective-permute-done((bf16[4,256,384]{2,1,0:T(8,128)(2,1)S(1)}, bf16[4,256,384]{2,1,0:T(8,128)(2,1)S(1)}, u32[]{:S(2)}, u32[]{:S(2)}) %collective-permute-start) | collective-permute-done | bytes 786464 | tf_op jit(solution)/shard_map/core_sum/ppermute | solution.py:250
  47.1 1.3 %collective-permute-start.1 = (bf16[256,384]{1,0:T(8,128)(2,1)S(1)}, bf16[256,384]{1,0:T(8,128)(2,1)S(1)}, u32[]{:S(2)}, u32[]{:S(2)}) collective-permute-start(bf16[256,384]{1,0:T(8,128)(2,1)S(1)} %get-tuple-element.19), channel_id=1, source_target_pairs={{0,2},{2,4},{4,6},{6,0},{1,3},{3,5},{5,7},{7,1},{8,10},{10,12},{12... | collective-permute-start | bytes 589832 | tf_op jit(solution)/shard_map/x_sum/ppermute | solution.py:250
  48.4 1.5 %collective-permute-start.2 = (bf16[256,384]{1,0:T(8,128)(2,1)S(1)}, bf16[256,384]{1,0:T(8,128)(2,1)S(1)}, u32[]{:S(2)}, u32[]{:S(2)}) collective-permute-start(bf16[256,384]{1,0:T(8,128)(2,1)S(1)} %get-tuple-element.20), channel_id=1, source_target_pairs={{0,6},{2,0},{4,2},{6,4},{1,7},{3,1},{5,3},{7,5},{8,14},{10,8},{12,... | collective-permute-start | bytes 589832 | tf_op jit(solution)/shard_map/x_sum/ppermute | solution.py:250
  49.8 1.5 %collective-permute-start.3 = (bf16[256,384]{1,0:T(8,128)(2,1)S(1)}, bf16[256,384]{1,0:T(8,128)(2,1)S(1)}, u32[]{:S(2)}, u32[]{:S(2)}) collective-permute-start(bf16[256,384]{1,0:T(8,128)(2,1)S(1)} %get-tuple-element.21), channel_id=1, source_target_pairs={{0,4},{2,6},{4,0},{6,2},{1,5},{3,7},{5,1},{7,3},{8,12},{10,14},{12... | collective-permute-start | bytes 589832 | tf_op jit(solution)/shard_map/x_sum/ppermute | solution.py:250
  51.4 3.1 %collective-permute-done.1.one_ref = bf16[256,384]{1,0:T(8,128)(2,1)S(1)} collective-permute-done((bf16[256,384]{1,0:T(8,128)(2,1)S(1)}, bf16[256,384]{1,0:T(8,128)(2,1)S(1)}, u32[]{:S(2)}, u32[]{:S(2)}) %collective-permute-start.1) | collective-permute-done | bytes 196640 | tf_op jit(solution)/shard_map/x_sum/ppermute | solution.py:250
  54.5 5.2 %collective-permute-done.3.three_ref = bf16[256,384]{1,0:T(8,128)(2,1)S(1)} collective-permute-done((bf16[256,384]{1,0:T(8,128)(2,1)S(1)}, bf16[256,384]{1,0:T(8,128)(2,1)S(1)}, u32[]{:S(2)}, u32[]{:S(2)}) %collective-permute-start.3) | collective-permute-done | bytes 196640 | tf_op jit(solution)/shard_map/x_sum/ppermute | solution.py:250
  59.8 13.9 %all_to_all.21.joint_ref = bf16[32,8,640]{2,1,0:T(8,128)(2,1)S(1)} all-to-all(bf16[32,8,640]{2,1,0:T(8,128)(2,1)S(1)} %x_sum.1), channel_id=1, replica_groups=mesh['y'=4,'z'=8,'x'=4,'c'=2] {'y','z'}, dimensions={0} | all-to-all | bytes 655360 | tf_op jit(solution)/shard_map/yz_sum/all_to_all | solution.py:307
  73.7 1.1 %yz_sum.1 = (bf16[8,8,384]{2,1,0:T(8,128)(2,1)S(1)}, bf16[512,256]{1,0:T(8,128)(2,1)}) custom-call(bf16[32,8,640]{2,1,0:T(8,128)(2,1)S(1)} %all_to_all.21.joint_ref, s32[32,8]{1,0:T(8,128)S(1)} %copy.14.valid_ref), custom_call_target="tpu_custom_call" | custom-call | tf_op jit(solution)/shard_map/yz_sum/pallas_call | solution.py:241
  74.8 12.1 %all_to_all.22 = bf16[8,8,384]{2,1,0:T(8,128)(2,1)S(1)} all-to-all(bf16[8,8,384]{2,1,0:T(8,128)(2,1)S(1)} %get-tuple-element.24), channel_id=1, replica_groups=mesh['y'=4,'z'=8,'x'=4,'c'=2] {'z'}, dimensions={0} | all-to-all | bytes 98304 | tf_op jit(solution)/shard_map/z_gather/all_to_all | solution.py:315
  87.0 13.3 %all_to_all.23 = bf16[16,64,384]{2,1,0:T(8,128)(2,1)S(1)} all-to-all(bf16[16,64,384]{2,1,0:T(8,128)(2,1)S(1)} %broadcast_in_dim.8), channel_id=1, replica_groups=mesh['y'=4,'z'=8,'x'=4,'c'=2] {'y','x'}, dimensions={0} | all-to-all | bytes 1572864 | tf_op jit(solution)/shard_map/yx_gather/all_to_all | solution.py:318
  100.3 5.5 %collective-permute-start.4 = (bf16[16,64,384]{2,1,0:T(8,128)(2,1)S(1)}, bf16[16,64,384]{2,1,0:T(8,128)(2,1)S(1)}, u32[]{:S(2)}, u32[]{:S(2)}) collective-permute-start(bf16[16,64,384]{2,1,0:T(8,128)(2,1)S(1)} %all_to_all.23), channel_id=1, source_target_pairs={{0,1},{1,0},{2,3},{3,2},{4,5},{5,4},{6,7},{7,6},{8,9},{9,8},{10,11... | collective-permute-start | bytes 2359304 | tf_op jit(solution)/shard_map/core_gather/ppermute | solution.py:250
  105.8 1.9 %collective-permute-done.4 = bf16[16,64,384]{2,1,0:T(8,128)(2,1)S(1)} collective-permute-done((bf16[16,64,384]{2,1,0:T(8,128)(2,1)S(1)}, bf16[16,64,384]{2,1,0:T(8,128)(2,1)S(1)}, u32[]{:S(2)}, u32[]{:S(2)}) %collective-permute-start.4) | collective-permute-done | bytes 786464 | tf_op jit(solution)/shard_map/core_gather/ppermute | solution.py:250
  107.7 1.8 %spread.1 = (f32[256,768]{1,0:T(8,128)}, f32[256,256]{1,0:T(8,128)}, f32[256,1024]{1,0:T(8,128)}, f32[1024,256]{1,0:T(8,128)}) custom-call(bf16[4,4,64,384]{3,2,1,0:T(8,128)(2,1)S(1)} %bitcast.12, bf16[4,4,64,384]{3,2,1,0:T(8,128)(2,1)S(1)} %bitcast.15), custom_call_target="tpu_custom_call" | custom-call | tf_op jit(solution)/shard_map/spread/pallas_call | solution.py:241
  (15 shorter events, 0.5 us)
Async XLA Ops:
  0.6 24.7 %copy-start.1 = (bf16[1024,256]{1,0:T(8,128)(2,1)S(1)}, bf16[1024,256]{1,0:T(8,128)(2,1)}, u32[]{:S(2)}) copy-start(bf16[1024,256]{1,0:T(8,128)(2,1)} %down_ref.1) | copy-start | bytes 1572868
  0.6 24.7 %copy-start = (bf16[256,1024]{1,0:T(8,128)(2,1)S(1)}, bf16[256,1024]{1,0:T(8,128)(2,1)}, u32[]{:S(2)}) copy-start(bf16[256,1024]{1,0:T(8,128)(2,1)} %up_ref.1) | copy-start | bytes 1572868
  1.5 0.9 copy-start.3
  2.5 0.9 copy-start.4
  25.4 1.0 copy-start.2
  26.4 0.9 copy-start.5
  27.3 0.7 copy-start.6
  27.9 0.7 copy-start.7
  41.2 5.7 %collective-permute-start = (bf16[4,256,384]{2,1,0:T(8,128)(2,1)S(1)}, bf16[4,256,384]{2,1,0:T(8,128)(2,1)S(1)}, u32[]{:S(2)}, u32[]{:S(2)}) collective-permute-start(bf16[4,256,384]{2,1,0:T(8,128)(2,1)S(1)} %slice_bitcast_fusion), channel_id=1, source_target_pairs={{0,1},{1,0},{2,3},{3,2},{4,5},{5,4},{6,7},{7,6},{8,9},{9,8},{10,11... | collective-permute-start | bytes 2359304 | tf_op jit(solution)/shard_map/core_sum/ppermute | solution.py:250
  47.1 7.4 %collective-permute-start.1 = (bf16[256,384]{1,0:T(8,128)(2,1)S(1)}, bf16[256,384]{1,0:T(8,128)(2,1)S(1)}, u32[]{:S(2)}, u32[]{:S(2)}) collective-permute-start(bf16[256,384]{1,0:T(8,128)(2,1)S(1)} %get-tuple-element.19), channel_id=1, source_target_pairs={{0,2},{2,4},{4,6},{6,0},{1,3},{3,5},{5,7},{7,1},{8,10},{10,12},{12... | collective-permute-start | bytes 589832 | tf_op jit(solution)/shard_map/x_sum/ppermute | solution.py:250
  48.4 6.1 %collective-permute-start.2 = (bf16[256,384]{1,0:T(8,128)(2,1)S(1)}, bf16[256,384]{1,0:T(8,128)(2,1)S(1)}, u32[]{:S(2)}, u32[]{:S(2)}) collective-permute-start(bf16[256,384]{1,0:T(8,128)(2,1)S(1)} %get-tuple-element.20), channel_id=1, source_target_pairs={{0,6},{2,0},{4,2},{6,4},{1,7},{3,1},{5,3},{7,5},{8,14},{10,8},{12,... | collective-permute-start | bytes 589832 | tf_op jit(solution)/shard_map/x_sum/ppermute | solution.py:250
  49.8 9.8 %collective-permute-start.3 = (bf16[256,384]{1,0:T(8,128)(2,1)S(1)}, bf16[256,384]{1,0:T(8,128)(2,1)S(1)}, u32[]{:S(2)}, u32[]{:S(2)}) collective-permute-start(bf16[256,384]{1,0:T(8,128)(2,1)S(1)} %get-tuple-element.21), channel_id=1, source_target_pairs={{0,4},{2,6},{4,0},{6,2},{1,5},{3,7},{5,1},{7,3},{8,12},{10,14},{12... | collective-permute-start | bytes 589832 | tf_op jit(solution)/shard_map/x_sum/ppermute | solution.py:250
  100.3 7.4 %collective-permute-start.4 = (bf16[16,64,384]{2,1,0:T(8,128)(2,1)S(1)}, bf16[16,64,384]{2,1,0:T(8,128)(2,1)S(1)}, u32[]{:S(2)}, u32[]{:S(2)}) collective-permute-start(bf16[16,64,384]{2,1,0:T(8,128)(2,1)S(1)} %all_to_all.23), channel_id=1, source_target_pairs={{0,1},{1,0},{2,3},{3,2},{4,5},{5,4},{6,7},{7,6},{8,9},{9,8},{10,11... | collective-permute-start | bytes 2359304 | tf_op jit(solution)/shard_map/core_gather/ppermute | solution.py:250

commit v4 on v3

--- a/solution.py
+++ b/solution.py
@@ -9,6 +9,7 @@
 from jax.sharding import PartitionSpec as P
 
 HEADS = 16
+BATCH = 16
 CAP = 4
 EPS = 1e-05
 GELU_C = 0.7978845608028654
@@ -120,22 +121,28 @@
     first_in = (normed_one * gain_first).astype(BF16)
     proj_t[...] = dot(qkv_ref[...], first_in, ((0,), (1,))).astype(BF16)
 
-    def attend(head, carry):
-        at = pl.multiple_of(head * 16, 16)
-        for pix in range(2):
+    def attend(batch, carry):
+        units = [(pix, batch * BATCH + step) for step in range(BATCH) for pix in range(2)]
+        scores, full = [], []
+        for pix, head in units:
+            at = pl.multiple_of(head * 16, 16)
             cols = pl.ds(pix * 128, 128)
             query = proj_t[pl.ds(at, 16), cols]
             key = proj_t[pl.ds(256 + at, 16), cols]
+            scores.append(dot(key, query, TN))
+        for (pix, head), score in zip(units, scores):
+            score = jnp.where(keep[pix * 128 : pix * 128 + 128], score * 0.25, -1e30)
+            powered = jnp.exp(score - jnp.max(score, axis=0, keepdims=True))
+            full.append(powered * (1.0 / jnp.sum(powered, axis=0, keepdims=True)))
+        for (pix, head), prob in zip(units, full):
+            probs[pix, head] = prob
+            at = pl.multiple_of(head * 16, 16)
+            cols = pl.ds(pix * 128, 128)
             value = proj_t[pl.ds(512 + at, 16), cols]
-            scores = dot(key, query, TN) * 0.25
-            scores = jnp.where(keep[pix * 128 : pix * 128 + 128], scores, -1e30)
-            powered = jnp.exp(scores - jnp.max(scores, axis=0, keepdims=True))
-            full = powered * (1.0 / jnp.sum(powered, axis=0, keepdims=True))
-            probs[pix, head] = full
-            att_t[pl.ds(at, 16), cols] = dot(value, full.astype(BF16)).astype(BF16)
+            att_t[pl.ds(at, 16), cols] = dot(value, prob.astype(BF16)).astype(BF16)
         return carry
 
-    lax.fori_loop(0, HEADS, attend, 0, unroll=4)
+    lax.fori_loop(0, HEADS // BATCH, attend, 0)
 
     attended_t = att_t[...]
     out_w = out_w_ref[...]
@@ -163,24 +170,40 @@
     put(7, slice(256, 384), out_grad[:, 128:])
     att_grad_t[...] = dot(out_w, resid_half, NT).astype(BF16)
 
-    def attend_back(head, carry):
-        at = pl.multiple_of(head * 16, 16)
-        for pix in range(2):
+    def attend_back(batch, carry):
+        units = [(pix, batch * BATCH + step) for step in range(BATCH) for pix in range(2)]
+        prob_grads, score_grads, outs = [], [], []
+        for pix, head in units:
+            at = pl.multiple_of(head * 16, 16)
+            cols = pl.ds(pix * 128, 128)
+            value = proj_t[pl.ds(512 + at, 16), cols]
+            prob_grads.append(dot(value, att_grad_t[pl.ds(at, 16), cols], TN))
+        for (pix, head), prob_grad in zip(units, prob_grads):
+            full = probs[pix, head]
+            total = jnp.sum(full * prob_grad, axis=0, keepdims=True)
+            score_grads.append((full * (prob_grad - total) * 0.25).astype(BF16))
+        for (pix, head), score_grad in zip(units, score_grads):
+            at = pl.multiple_of(head * 16, 16)
             cols = pl.ds(pix * 128, 128)
             query = proj_t[pl.ds(at, 16), cols]
             key = proj_t[pl.ds(256 + at, 16), cols]
-            value = proj_t[pl.ds(512 + at, 16), cols]
             grad = att_grad_t[pl.ds(at, 16), cols]
-            full = probs[pix, head]
-            prob_grad = dot(value, grad, TN)
-            total = jnp.sum(full * prob_grad, axis=0, keepdims=True)
-            score_grad = (full * (prob_grad - total) * 0.25).astype(BF16)
-            proj_grad_t[pl.ds(at, 16), cols] = dot(key, score_grad).astype(BF16)
-            proj_grad_t[pl.ds(256 + at, 16), cols] = dot(query, score_grad, NT).astype(BF16)
-            proj_grad_t[pl.ds(512 + at, 16), cols] = dot(grad, full.astype(BF16), NT).astype(BF16)
+            outs.append(
+                (
+                    dot(key, score_grad),
+                    dot(score_grad, query, NT),
+                    dot(probs[pix, head].astype(BF16), grad, NT),
+                )
+            )
+        for (pix, head), got in zip(units, outs):
+            at = pl.multiple_of(head * 16, 16)
+            cols = pl.ds(pix * 128, 128)
+            proj_grad_t[pl.ds(at, 16), cols] = got[0].astype(BF16)
+            proj_grad_t[pl.ds(256 + at, 16), cols] = got[1].T.astype(BF16)
+            proj_grad_t[pl.ds(512 + at, 16), cols] = got[2].T.astype(BF16)
         return carry
 
-    lax.fori_loop(0, HEADS, attend_back, 0, unroll=4)
+    lax.fori_loop(0, HEADS // BATCH, attend_back, 0)
 
     grad_t = proj_grad_t[...]
     first_t = first_in.T

time: 110 us -> 104 us (0.945)
  Pallas kernels: 16 us -> 9.88 us
    pallas_call x6, Pallas kernels: 16 us -> 9.88 us  [run(): pl.pallas_call(kernel, out_shape=out_shape, scratch_shapes=list(scratch),...]
where the time goes in v4:
time: 104 us; the launch traced here: 103 us
  blocking collectives  60.8 us (58%)
  starting transfers between devices  13.6 us (13%)
  waiting for transfers between devices  12.1 us (12%)
  Pallas kernels  9.88 us (10%)
  local copies, waits for them, and re-layouts  6.19 us (6%)
    all_to_all x1, blocking collectives, per_device(): lax.all_to_all(send.reshape(32, 16, width), dates, split_axis=0, concat_a...  21.5 us
    all_to_all x1, blocking collectives, per_device(): lax.all_to_all(joint, dates, split_axis=0, concat_axis=0, tiled=True)  13.9 us
    ppermute x5, starting transfers between devices, shift(): lax.ppermute(array, axis, [(at, (at + by) % size) for at in range(size)])  13.6 us
    all_to_all x1, blocking collectives, per_device(): lax.all_to_all(part, ('y', 'x'), split_axis=0, concat_axis=0, tiled=True)  13.3 us
    ppermute x5, waiting for transfers between devices, shift(): lax.ppermute(array, axis, [(at, (at + by) % size) for at in range(size)])  12.1 us
    all_to_all x1, blocking collectives, per_device(): part = lax.all_to_all(total, 'z', split_axis=0, concat_axis=0, tiled=True)  12.1 us
    pallas_call x6, Pallas kernels, run(): pl.pallas_call(kernel, out_shape=out_shape, scratch_shapes=list(scratch),...  9.88 us
    unnamed x17, local copies, waits for them, and re-layouts  6.01 us
  transfers between devices with their start and end apart: 5, of which 4 were waited for; matrix products, arithmetic and copies ran while one was open for 0% of the time, Pallas kernels for 0%

profile of v4, /device:TPU:1, one launch (start us, length us, event | category | flops | bytes accessed | tf_op | source)
XLA Modules:
  0.0 103.3 jit_solution(9476660171638858025)
XLA Ops:
  0.7 0.8 copy.14.valid_ref
  1.5 0.9 copy-done.3
  2.5 0.9 copy-done.4
  3.4 0.4 compact.1
  3.8 21.5 %all_to_all.20 = bf16[32,16,256]{2,1,0:T(8,128)(2,1)S(1)} all-to-all(bf16[32,16,256]{2,1,0:T(8,128)(2,1)S(1)} %bitcast.13), channel_id=1, replica_groups=mesh['y'=4,'z'=8,'x'=4,'c'=2] {'y','z'}, dimensions={0} | all-to-all | bytes 524288 | tf_op jit(solution)/shard_map/to_owner/all_to_all | solution.py:300
  25.4 1.0 copy-done.2
  26.4 0.9 copy-done.5
  27.3 0.7 copy-done.6
  28.0 0.7 copy-done.7
  28.6 6.3 %layer.1 = (bf16[256,256]{1,0:T(8,128)(2,1)S(1)}, bf16[2,4,256,384]{3,2,1,0:T(8,128)(2,1)S(1)}) custom-call(bf16[512,256]{1,0:T(8,128)(2,1)S(1)} %bitcast.14, f32[1,256]{1,0:T(1,128)S(1)} %bitcast.18, bf16[256,768]{1,0:T(8,128)(2,1)S(1)} %copy-done.2, bf16[256,256]{1,0:T(8,128)(2,1)S(1)} %copy-done.5, f32[1,256]{1,0:T(1,128)S(1)} %bitcast.19, ...), custom_call_target="tpu_custom_call" | custom-call | tf_op jit(solution)/shard_map/layer/pallas_call | solution.py:264
  35.0 3.8 %collective-permute-start = (bf16[4,256,384]{2,1,0:T(8,128)(2,1)S(1)}, bf16[4,256,384]{2,1,0:T(8,128)(2,1)S(1)}, u32[]{:S(2)}, u32[]{:S(2)}) collective-permute-start(bf16[4,256,384]{2,1,0:T(8,128)(2,1)S(1)} %slice_bitcast_fusion), channel_id=1, source_target_pairs={{0,1},{1,0},{2,3},{3,2},{4,5},{5,4},{6,7},{7,6},{8,9},{9,8},{10,11... | collective-permute-start | bytes 2359304 | tf_op jit(solution)/shard_map/core_sum/ppermute | solution.py:273
  38.8 1.9 %collective-permute-done.other_ref = bf16[4,256,384]{2,1,0:T(8,128)(2,1)S(1)} collective-permute-done((bf16[4,256,384]{2,1,0:T(8,128)(2,1)S(1)}, bf16[4,256,384]{2,1,0:T(8,128)(2,1)S(1)}, u32[]{:S(2)}, u32[]{:S(2)}) %collective-permute-start) | collective-permute-done | bytes 786464 | tf_op jit(solution)/shard_map/core_sum/ppermute | solution.py:273
  40.9 1.3 %collective-permute-start.1 = (bf16[256,384]{1,0:T(8,128)(2,1)S(1)}, bf16[256,384]{1,0:T(8,128)(2,1)S(1)}, u32[]{:S(2)}, u32[]{:S(2)}) collective-permute-start(bf16[256,384]{1,0:T(8,128)(2,1)S(1)} %get-tuple-element.19), channel_id=1, source_target_pairs={{0,2},{2,4},{4,6},{6,0},{1,3},{3,5},{5,7},{7,1},{8,10},{10,12},{12... | collective-permute-start | bytes 589832 | tf_op jit(solution)/shard_map/x_sum/ppermute | solution.py:273
  42.2 1.5 %collective-permute-start.2 = (bf16[256,384]{1,0:T(8,128)(2,1)S(1)}, bf16[256,384]{1,0:T(8,128)(2,1)S(1)}, u32[]{:S(2)}, u32[]{:S(2)}) collective-permute-start(bf16[256,384]{1,0:T(8,128)(2,1)S(1)} %get-tuple-element.20), channel_id=1, source_target_pairs={{0,6},{2,0},{4,2},{6,4},{1,7},{3,1},{5,3},{7,5},{8,14},{10,8},{12,... | collective-permute-start | bytes 589832 | tf_op jit(solution)/shard_map/x_sum/ppermute | solution.py:273
  43.7 1.5 %collective-permute-start.3 = (bf16[256,384]{1,0:T(8,128)(2,1)S(1)}, bf16[256,384]{1,0:T(8,128)(2,1)S(1)}, u32[]{:S(2)}, u32[]{:S(2)}) collective-permute-start(bf16[256,384]{1,0:T(8,128)(2,1)S(1)} %get-tuple-element.21), channel_id=1, source_target_pairs={{0,4},{2,6},{4,0},{6,2},{1,5},{3,7},{5,1},{7,3},{8,12},{10,14},{12... | collective-permute-start | bytes 589832 | tf_op jit(solution)/shard_map/x_sum/ppermute | solution.py:273
  45.2 3.1 %collective-permute-done.1.one_ref = bf16[256,384]{1,0:T(8,128)(2,1)S(1)} collective-permute-done((bf16[256,384]{1,0:T(8,128)(2,1)S(1)}, bf16[256,384]{1,0:T(8,128)(2,1)S(1)}, u32[]{:S(2)}, u32[]{:S(2)}) %collective-permute-start.1) | collective-permute-done | bytes 196640 | tf_op jit(solution)/shard_map/x_sum/ppermute | solution.py:273
  48.3 5.2 %collective-permute-done.3.three_ref = bf16[256,384]{1,0:T(8,128)(2,1)S(1)} collective-permute-done((bf16[256,384]{1,0:T(8,128)(2,1)S(1)}, bf16[256,384]{1,0:T(8,128)(2,1)S(1)}, u32[]{:S(2)}, u32[]{:S(2)}) %collective-permute-start.3) | collective-permute-done | bytes 196640 | tf_op jit(solution)/shard_map/x_sum/ppermute | solution.py:273
  53.6 13.9 %all_to_all.21.joint_ref = bf16[32,8,640]{2,1,0:T(8,128)(2,1)S(1)} all-to-all(bf16[32,8,640]{2,1,0:T(8,128)(2,1)S(1)} %x_sum.1), channel_id=1, replica_groups=mesh['y'=4,'z'=8,'x'=4,'c'=2] {'y','z'}, dimensions={0} | all-to-all | bytes 655360 | tf_op jit(solution)/shard_map/yz_sum/all_to_all | solution.py:330
  67.6 1.1 %yz_sum.1 = (bf16[8,8,384]{2,1,0:T(8,128)(2,1)S(1)}, bf16[512,256]{1,0:T(8,128)(2,1)}) custom-call(bf16[32,8,640]{2,1,0:T(8,128)(2,1)S(1)} %all_to_all.21.joint_ref, s32[32,8]{1,0:T(8,128)S(1)} %copy.14.valid_ref), custom_call_target="tpu_custom_call" | custom-call | tf_op jit(solution)/shard_map/yz_sum/pallas_call | solution.py:264
  68.7 12.1 %all_to_all.22 = bf16[8,8,384]{2,1,0:T(8,128)(2,1)S(1)} all-to-all(bf16[8,8,384]{2,1,0:T(8,128)(2,1)S(1)} %get-tuple-element.24), channel_id=1, replica_groups=mesh['y'=4,'z'=8,'x'=4,'c'=2] {'z'}, dimensions={0} | all-to-all | bytes 98304 | tf_op jit(solution)/shard_map/z_gather/all_to_all | solution.py:338
  80.9 13.3 %all_to_all.23 = bf16[16,64,384]{2,1,0:T(8,128)(2,1)S(1)} all-to-all(bf16[16,64,384]{2,1,0:T(8,128)(2,1)S(1)} %broadcast_in_dim.8), channel_id=1, replica_groups=mesh['y'=4,'z'=8,'x'=4,'c'=2] {'y','x'}, dimensions={0} | all-to-all | bytes 1572864 | tf_op jit(solution)/shard_map/yx_gather/all_to_all | solution.py:341
  94.1 5.5 %collective-permute-start.4 = (bf16[16,64,384]{2,1,0:T(8,128)(2,1)S(1)}, bf16[16,64,384]{2,1,0:T(8,128)(2,1)S(1)}, u32[]{:S(2)}, u32[]{:S(2)}) collective-permute-start(bf16[16,64,384]{2,1,0:T(8,128)(2,1)S(1)} %all_to_all.23), channel_id=1, source_target_pairs={{0,1},{1,0},{2,3},{3,2},{4,5},{5,4},{6,7},{7,6},{8,9},{9,8},{10,11... | collective-permute-start | bytes 2359304 | tf_op jit(solution)/shard_map/core_gather/ppermute | solution.py:273
  99.6 1.9 %collective-permute-done.4 = bf16[16,64,384]{2,1,0:T(8,128)(2,1)S(1)} collective-permute-done((bf16[16,64,384]{2,1,0:T(8,128)(2,1)S(1)}, bf16[16,64,384]{2,1,0:T(8,128)(2,1)S(1)}, u32[]{:S(2)}, u32[]{:S(2)}) %collective-permute-start.4) | collective-permute-done | bytes 786464 | tf_op jit(solution)/shard_map/core_gather/ppermute | solution.py:273
  101.6 1.8 %spread.1 = (f32[256,768]{1,0:T(8,128)}, f32[256,256]{1,0:T(8,128)}, f32[256,1024]{1,0:T(8,128)}, f32[1024,256]{1,0:T(8,128)}) custom-call(bf16[4,4,64,384]{3,2,1,0:T(8,128)(2,1)S(1)} %bitcast.12, bf16[4,4,64,384]{3,2,1,0:T(8,128)(2,1)S(1)} %bitcast.15), custom_call_target="tpu_custom_call" | custom-call | tf_op jit(solution)/shard_map/spread/pallas_call | solution.py:264
  (15 shorter events, 0.5 us)
Async XLA Ops:
  0.6 24.7 %copy-start.1 = (bf16[1024,256]{1,0:T(8,128)(2,1)S(1)}, bf16[1024,256]{1,0:T(8,128)(2,1)}, u32[]{:S(2)}) copy-start(bf16[1024,256]{1,0:T(8,128)(2,1)} %down_ref.1) | copy-start | bytes 1572868
  0.6 24.7 %copy-start = (bf16[256,1024]{1,0:T(8,128)(2,1)S(1)}, bf16[256,1024]{1,0:T(8,128)(2,1)}, u32[]{:S(2)}) copy-start(bf16[256,1024]{1,0:T(8,128)(2,1)} %up_ref.1) | copy-start | bytes 1572868
  1.5 0.9 copy-start.3
  2.5 0.9 copy-start.4
  25.4 1.0 copy-start.2
  26.4 0.9 copy-start.5
  27.3 0.7 copy-start.6
  27.9 0.7 copy-start.7
  35.0 5.7 %collective-permute-start = (bf16[4,256,384]{2,1,0:T(8,128)(2,1)S(1)}, bf16[4,256,384]{2,1,0:T(8,128)(2,1)S(1)}, u32[]{:S(2)}, u32[]{:S(2)}) collective-permute-start(bf16[4,256,384]{2,1,0:T(8,128)(2,1)S(1)} %slice_bitcast_fusion), channel_id=1, source_target_pairs={{0,1},{1,0},{2,3},{3,2},{4,5},{5,4},{6,7},{7,6},{8,9},{9,8},{10,11... | collective-permute-start | bytes 2359304 | tf_op jit(solution)/shard_map/core_sum/ppermute | solution.py:273
  40.9 7.4 %collective-permute-start.1 = (bf16[256,384]{1,0:T(8,128)(2,1)S(1)}, bf16[256,384]{1,0:T(8,128)(2,1)S(1)}, u32[]{:S(2)}, u32[]{:S(2)}) collective-permute-start(bf16[256,384]{1,0:T(8,128)(2,1)S(1)} %get-tuple-element.19), channel_id=1, source_target_pairs={{0,2},{2,4},{4,6},{6,0},{1,3},{3,5},{5,7},{7,1},{8,10},{10,12},{12... | collective-permute-start | bytes 589832 | tf_op jit(solution)/shard_map/x_sum/ppermute | solution.py:273
  42.2 6.1 %collective-permute-start.2 = (bf16[256,384]{1,0:T(8,128)(2,1)S(1)}, bf16[256,384]{1,0:T(8,128)(2,1)S(1)}, u32[]{:S(2)}, u32[]{:S(2)}) collective-permute-start(bf16[256,384]{1,0:T(8,128)(2,1)S(1)} %get-tuple-element.20), channel_id=1, source_target_pairs={{0,6},{2,0},{4,2},{6,4},{1,7},{3,1},{5,3},{7,5},{8,14},{10,8},{12,... | collective-permute-start | bytes 589832 | tf_op jit(solution)/shard_map/x_sum/ppermute | solution.py:273
  43.7 9.8 %collective-permute-start.3 = (bf16[256,384]{1,0:T(8,128)(2,1)S(1)}, bf16[256,384]{1,0:T(8,128)(2,1)S(1)}, u32[]{:S(2)}, u32[]{:S(2)}) collective-permute-start(bf16[256,384]{1,0:T(8,128)(2,1)S(1)} %get-tuple-element.21), channel_id=1, source_target_pairs={{0,4},{2,6},{4,0},{6,2},{1,5},{3,7},{5,1},{7,3},{8,12},{10,14},{12... | collective-permute-start | bytes 589832 | tf_op jit(solution)/shard_map/x_sum/ppermute | solution.py:273
  94.1 7.4 %collective-permute-start.4 = (bf16[16,64,384]{2,1,0:T(8,128)(2,1)S(1)}, bf16[16,64,384]{2,1,0:T(8,128)(2,1)S(1)}, u32[]{:S(2)}, u32[]{:S(2)}) collective-permute-start(bf16[16,64,384]{2,1,0:T(8,128)(2,1)S(1)} %all_to_all.23), channel_id=1, source_target_pairs={{0,1},{1,0},{2,3},{3,2},{4,5},{5,4},{6,7},{7,6},{8,9},{9,8},{10,11... | collective-permute-start | bytes 2359304 | tf_op jit(solution)/shard_map/core_gather/ppermute | solution.py:273

commit v5 on v4

--- a/solution.py
+++ b/solution.py
@@ -36,10 +36,10 @@
 def slot_matrix(valid, group, rows_per_block):
     date = iota((8, 256), 1) % 8
     day = iota((8, 256), 0)
-    held = valid[group * 16 : group * 16 + 16, :].astype(F32)
-    keep_all = dot(held, (day == date).astype(F32))
-    rank_all = dot(held, (day < date).astype(F32))
-    own = iota((16, 256), 0) == iota((16, 256), 1) // 16
+    held = valid.astype(F32)
+    keep_all = dot(held, (day == date).astype(F32), TN)
+    rank_all = dot(held, (day < date).astype(F32), TN)
+    own = iota((32, 256), 0) == iota((32, 256), 1) // 16 + group * 16
     keep = jnp.sum(jnp.where(own, keep_all, 0.0), axis=0, keepdims=True)
     rank = jnp.sum(jnp.where(own, rank_all, 0.0), axis=0, keepdims=True)
     shape = (16 * rows_per_block, 256)
@@ -53,18 +53,30 @@
     return match.astype(F32)
 
 
-def compact_kernel(feat_ref, cot_ref, valid_ref, send_ref):
+def compact_kernel(feat_hbm, cot_hbm, valid_hbm, send_ref, feat, cot, valid_ref, arrived):
+    copies = [
+        pltpu.make_async_copy(valid_hbm, valid_ref, arrived.at[0]),
+        pltpu.make_async_copy(feat_hbm, feat, arrived.at[1]),
+        pltpu.make_async_copy(cot_hbm, cot, arrived.at[2]),
+    ]
+    for copy in copies:
+        copy.start()
+    copies[0].wait()
     valid = valid_ref[...]
+    is_feat = (iota((256, 1), 0) // 8) % 2 == 0
+    picks = []
     for group in range(2):
         match = slot_matrix(valid, group, 16)
-        is_feat = (iota((256, 1), 0) // 8) % 2 == 0
         pick_feat = jnp.where(is_feat, match, 0.0).astype(BF16)
         pick_cot = jnp.where(is_feat, 0.0, match).astype(BF16)
+        filled = jnp.sum(match, axis=1, keepdims=True) > 0.5
+        picks.append((pick_feat, pick_cot, is_feat & jnp.logical_not(filled)))
+    copies[1].wait()
+    copies[2].wait()
+    for group, (pick_feat, pick_cot, absent) in enumerate(picks):
         rows = pl.ds(group * 256, 256)
-        got = dot(pick_feat, feat_ref[rows, :]) + dot(pick_cot, cot_ref[rows, :])
-        filled = jnp.sum(match, axis=1, keepdims=True) > 0.5
-        got = jnp.where(is_feat & jnp.logical_not(filled), ABSENT, got)
-        send_ref[rows, :] = got.astype(BF16)
+        got = dot(pick_feat, feat[rows, :]) + dot(pick_cot, cot[rows, :])
+        send_ref[rows, :] = jnp.where(absent, ABSENT, got).astype(BF16)
 
 
 def row_mean(values):
@@ -85,20 +97,40 @@
 def layer_kernel(
     scale,
     recv_ref,
+    gain_first_hbm,
+    qkv_hbm,
+    out_w_hbm,
+    gain_second_hbm,
+    up_hbm,
+    down_hbm,
+    grad_ref,
+    terms_ref,
     gain_first_ref,
     qkv_ref,
     out_w_ref,
     gain_second_ref,
     up_ref,
     down_ref,
-    grad_ref,
-    terms_ref,
+    arrived,
     probs,
     proj_t,
     att_t,
     att_grad_t,
     proj_grad_t,
 ):
+    pairs = (
+        (qkv_hbm, qkv_ref),
+        (gain_first_hbm, gain_first_ref),
+        (out_w_hbm, out_w_ref),
+        (gain_second_hbm, gain_second_ref),
+        (up_hbm, up_ref),
+        (down_hbm, down_ref),
+    )
+    copies = [
+        pltpu.make_async_copy(held, ref, arrived.at[at]) for at, (held, ref) in enumerate(pairs)
+    ]
+    for copy in copies:
+        copy.start()
     core = lax.axis_index("c")
     place = lax.axis_index("x")
 
@@ -114,10 +146,10 @@
     upstream = dot((source == target + 8).astype(BF16), recv).astype(BF16)
     keep = inputs[:, 0:1] < 0.5 * ABSENT
     inputs = jnp.where(keep, inputs, 0.0)
+    normed_one, inverse_one = norm_rows(inputs)
+    copies[0].wait()
+    copies[1].wait()
     gain_first = gain_first_ref[...]
-    gain_second = gain_second_ref[...]
-
-    normed_one, inverse_one = norm_rows(inputs)
     first_in = (normed_one * gain_first).astype(BF16)
     proj_t[...] = dot(qkv_ref[...], first_in, ((0,), (1,))).astype(BF16)
 
@@ -144,6 +176,9 @@
 
     lax.fori_loop(0, HEADS // BATCH, attend, 0)
 
+    for copy in copies[2:]:
+        copy.wait()
+    gain_second = gain_second_ref[...]
     attended_t = att_t[...]
     out_w = out_w_ref[...]
     residual = inputs + dot(attended_t, out_w, TN)
@@ -232,9 +267,12 @@
     out_ref[:, :, 384:640] = grad_ref[...].reshape(32, 8, 256)
 
 
-def yz_sum_kernel(joint_ref, valid_ref, total_ref, out_ref):
+def yz_sum_kernel(joint_ref, valid_hbm, total_ref, out_ref, valid_ref, arrived):
+    copy = pltpu.make_async_copy(valid_hbm, valid_ref, arrived)
+    copy.start()
     total = jnp.sum(joint_ref[:, :, 0:384].astype(F32), axis=0).astype(BF16)
     total_ref[...] = jnp.broadcast_to(total[None], total_ref.shape)
+    copy.wait()
     valid = valid_ref[...]
     for group in range(2):
         match = slot_matrix(valid, group, 8).astype(BF16)
@@ -242,28 +280,71 @@
         out_ref[pl.ds(group * 256, 256), :] = dot(match, back, TN).astype(BF16)
 
 
-def spread_kernel(mine_ref, other_ref, qkv_ref, out_ref, up_ref, down_ref):
-    core = lax.axis_index("c")
-    for group in range(8):
+def spread_kernel(flip, held_ref, *refs):
+    qkv_hbm, out_hbm, up_hbm, down_hbm, wide, narrow, sent = refs[-7:]
+    core = lax.axis_index("c") ^ flip
+    copies = []
+    for pair in range(4):
+        group = 2 * pair + core
         for lane in range(4):
             rows = slice(lane * 64, lane * 64 + 64)
-            near = mine_ref[lane, group // 2].astype(F32)
-            far = other_ref[lane, group // 2].astype(F32)
-            piece = jnp.where(core == group % 2, near, far)
-            if group < 4:
-                up_ref[rows, pl.ds(group * 256, 256)] = piece[:, :256]
-            else:
-                down_ref[pl.ds((group - 4) * 256 + lane * 64, 64), :] = piece[:, :256]
-            if group < 6:
-                qkv_ref[rows, pl.ds(group * 128, 128)] = piece[:, 256:]
-            else:
-                out_ref[rows, pl.ds((group - 6) * 128, 128)] = piece[:, 256:]
-
-
-def run(kernel, out_shape, *args, scratch=()):
+            piece = held_ref[lane, pair].astype(F32)
+            wide[pair, rows, :] = piece[:, :256]
+            narrow[pair, rows, :] = piece[:, 256:]
+        if pair < 2:
+            far = up_hbm.at[:, pl.ds(pl.multiple_of(group * 256, 256), 256)]
+        else:
+            far = down_hbm.at[pl.ds(pl.multiple_of((group - 4) * 256, 256), 256), :]
+        if pair < 3:
+            near = qkv_hbm.at[:, pl.ds(pl.multiple_of(group * 128, 128), 128)]
+        else:
+            near = out_hbm.at[:, pl.ds(pl.multiple_of((group - 6) * 128, 128), 128)]
+        for source, target, at in ((wide, far, 0), (narrow, near, 1)):
+            copy = pltpu.make_async_copy(source.at[pair], target, sent.at[pair, at])
+            copy.start()
+            copies.append(copy)
+    for copy in copies:
+        copy.wait()
+
+
+def spread(flip, held, *outs):
+    shape = jax.ShapeDtypeStruct
+    kept = pl.BlockSpec(memory_space=pl.ANY)
+    return pl.pallas_call(
+        functools.partial(spread_kernel, flip),
+        out_shape=(
+            shape((256, 768), F32),
+            shape((256, 256), F32),
+            shape((256, 1024), F32),
+            shape((1024, 256), F32),
+        ),
+        in_specs=[pl.BlockSpec(memory_space=pltpu.VMEM)] + [kept] * len(outs),
+        out_specs=[kept] * 4,
+        scratch_shapes=[
+            pltpu.VMEM((4, 256, 256), F32),
+            pltpu.VMEM((4, 256, 128), F32),
+            pltpu.SemaphoreType.DMA((4, 2)),
+        ],
+        input_output_aliases={at + 1: at for at in range(len(outs))},
+        compiler_params=pltpu.CompilerParams(vmem_limit_bytes=VMEM_LIMIT),
+        cost_estimate=pl.CostEstimate(flops=0, bytes_accessed=3000000, transcendentals=0),
+    )(held, *outs)
+
+
+def stay(array):
+    return pltpu.with_memory_space_constraint(array, pltpu.HBM)
+
+
+def run(kernel, out_shape, *args, scratch=(), held=()):
+    specs = [
+        pl.BlockSpec(memory_space=pltpu.HBM if at in held else pltpu.VMEM)
+        for at in range(len(args))
+    ]
+    args = [stay(array) if at in held else array for at, array in enumerate(args)]
     return pl.pallas_call(
         kernel,
         out_shape=out_shape,
+        in_specs=specs,
         scratch_shapes=list(scratch),
         compiler_params=pltpu.CompilerParams(vmem_limit_bytes=VMEM_LIMIT),
     )(*args)
@@ -294,7 +375,14 @@
             shape((512, width), BF16),
             features.reshape(512, width),
             cotangent.reshape(512, width),
-            valid_dates,
+            valid_dates.T,
+            held=(0, 1, 2),
+            scratch=(
+                pltpu.VMEM((512, width), BF16),
+                pltpu.VMEM((512, width), BF16),
+                pltpu.VMEM((8, 32), jnp.int32),
+                pltpu.SemaphoreType.DMA((3,)),
+            ),
         )
     with jax.named_scope("to_owner"):
         recv = lax.all_to_all(
@@ -312,7 +400,15 @@
             gain_second.reshape(1, width),
             up_weight,
             down_weight,
+            held=range(1, 7),
             scratch=(
+                pltpu.VMEM((1, width), F32),
+                pltpu.VMEM((256, 768), BF16),
+                pltpu.VMEM((256, 256), BF16),
+                pltpu.VMEM((1, width), F32),
+                pltpu.VMEM((256, 1024), BF16),
+                pltpu.VMEM((1024, 256), BF16),
+                pltpu.SemaphoreType.DMA((6,)),
                 pltpu.VMEM((2, HEADS, 128, 128), F32),
                 pltpu.VMEM((768, 256), BF16),
                 pltpu.VMEM((256, 256), BF16),
@@ -332,7 +428,9 @@
             yz_sum_kernel,
             (shape((8, 8, 384), BF16), shape((512, width), BF16)),
             joint,
-            valid_dates,
+            valid_dates.T,
+            held=(1,),
+            scratch=(pltpu.VMEM((8, 32), jnp.int32), pltpu.SemaphoreType.DMA),
         )
     with jax.named_scope("z_gather"):
         part = lax.all_to_all(total, "z", split_axis=0, concat_axis=0, tiled=True)
@@ -342,17 +440,8 @@
     with jax.named_scope("core_gather"):
         other = shift(mine, "c", 2, 1)
     with jax.named_scope("spread"):
-        outs = run(
-            spread_kernel,
-            (
-                shape((256, 768), F32),
-                shape((256, 256), F32),
-                shape((256, 1024), F32),
-                shape((1024, 256), F32),
-            ),
-            mine.reshape(4, 4, 64, 384),
-            other.reshape(4, 4, 64, 384),
-        )
+        outs = spread(0, mine.reshape(4, 4, 64, 384))
+        outs = spread(1, other.reshape(4, 4, 64, 384), *outs)
     return (feature_grad.reshape(features.shape), *outs)
 
 

time: 104 us -> 99.4 us (0.956)
  local copies, waits for them, and re-layouts: 6.19 us -> 0.17 us
  Pallas kernels: 9.88 us -> 12.9 us
  waiting for transfers between devices: 12.1 us -> 10.9 us
    unnamed x17 -> x0, local copies, waits for them, and re-layouts: 6.01 us -> none
    pallas_call x6 -> x7, Pallas kernels: 9.88 us -> 12.9 us  [the longest x5 10.5 us: run(): pl.pallas_call(kernel, out_shape=out_shape, in_specs=specs, scratch_shape...]
    ppermute x5, waiting for transfers between devices: 12.1 us -> 10.9 us  [shift(): lax.ppermute(array, axis, [(at, (at + by) % size) for at in range(size)])]
  transfers between devices with their start and end apart: 5 -> 5, of which waited for: 4 -> 4; matrix products, arithmetic and copies ran while one was open for 0% -> 0% of each run, Pallas kernels for 0% -> 1%
where the time goes in v5:
time: 99.4 us; the launch traced here: 99.1 us
  blocking collectives  60.8 us (61%)
  starting transfers between devices  13.6 us (14%)
  Pallas kernels  12.9 us (13%)
  waiting for transfers between devices  10.9 us (11%)
    all_to_all x1, blocking collectives, per_device(): lax.all_to_all(send.reshape(32, 16, width), dates, split_axis=0, concat_a...  21.5 us
    all_to_all x1, blocking collectives, per_device(): lax.all_to_all(joint, dates, split_axis=0, concat_axis=0, tiled=True)  13.9 us
    ppermute x5, starting transfers between devices, shift(): lax.ppermute(array, axis, [(at, (at + by) % size) for at in range(size)])  13.6 us
    all_to_all x1, blocking collectives, per_device(): lax.all_to_all(part, ('y', 'x'), split_axis=0, concat_axis=0, tiled=True)  13.3 us
    all_to_all x1, blocking collectives, per_device(): part = lax.all_to_all(total, 'z', split_axis=0, concat_axis=0, tiled=True)  12.1 us
    ppermute x5, waiting for transfers between devices, shift(): lax.ppermute(array, axis, [(at, (at + by) % size) for at in range(size)])  10.9 us
    pallas_call x5, Pallas kernels, run(): pl.pallas_call(kernel, out_shape=out_shape, in_specs=specs, scratch_shape...  10.5 us
    pallas_call x2, Pallas kernels, spread(): pl.pallas_call(functools.partial(spread_kernel, flip), out_shape=(shape((...  2.43 us
  transfers between devices with their start and end apart: 5, of which 4 were waited for; matrix products, arithmetic and copies ran while one was open for 0% of the time, Pallas kernels for 1%

profile of v5, /device:TPU:1, one launch (start us, length us, event | category | flops | bytes accessed | tf_op | source)
XLA Modules:
  0.0 99.1 jit_solution(4287617471923388165)
XLA Ops:
  0.6 1.4 %compact.1 = bf16[512,256]{1,0:T(8,128)(2,1)S(1)} custom-call(bf16[512,256]{1,0:T(8,128)(2,1)} %bitcast.17, bf16[512,256]{1,0:T(8,128)(2,1)} %bitcast.18, s32[8,32]{1,0:T(8,128)} %bitcast.20), custom_call_target="tpu_custom_call" | custom-call | tf_op jit(solution)/shard_map/compact/pallas_call | solution.py:344
  2.0 21.5 %all_to_all.20 = bf16[32,16,256]{2,1,0:T(8,128)(2,1)S(1)} all-to-all(bf16[32,16,256]{2,1,0:T(8,128)(2,1)S(1)} %bitcast.14), channel_id=1, replica_groups=mesh['y'=4,'z'=8,'x'=4,'c'=2] {'y','z'}, dimensions={0} | all-to-all | bytes 524288 | tf_op jit(solution)/shard_map/to_owner/all_to_all | solution.py:388
  23.5 6.9 %layer.1 = (bf16[256,256]{1,0:T(8,128)(2,1)S(1)}, bf16[2,4,256,384]{3,2,1,0:T(8,128)(2,1)S(1)}) custom-call(bf16[512,256]{1,0:T(8,128)(2,1)S(1)} %bitcast.15, f32[1,256]{1,0:T(1,128)} %bitcast.22, bf16[256,768]{1,0:T(8,128)(2,1)} %qkv_hbm.1, bf16[256,256]{1,0:T(8,128)(2,1)} %out_w_hbm.1, f32[1,256]{1,0:T(1,128)} %bitcast.23, bf16[256,1024]{1,0:T(8,128)(2,1)} %up_hbm.1, ...), custom_call_target="tpu_custom_call" | custom-call | tf_op jit(solution)/shard_map/layer/pallas_call | solution.py:344
  30.5 0.1 slice_bitcast_fusion
  30.6 3.8 %collective-permute-start = (bf16[4,256,384]{2,1,0:T(8,128)(2,1)S(1)}, bf16[4,256,384]{2,1,0:T(8,128)(2,1)S(1)}, u32[]{:S(2)}, u32[]{:S(2)}) collective-permute-start(bf16[4,256,384]{2,1,0:T(8,128)(2,1)S(1)} %slice_bitcast_fusion), channel_id=1, source_target_pairs={{0,1},{1,0},{2,3},{3,2},{4,5},{5,4},{6,7},{7,6},{8,9},{9,8},{10,11... | collective-permute-start | bytes 2359304 | tf_op jit(solution)/shard_map/core_sum/ppermute | solution.py:354
  34.4 1.9 %collective-permute-done.other_ref = bf16[4,256,384]{2,1,0:T(8,128)(2,1)S(1)} collective-permute-done((bf16[4,256,384]{2,1,0:T(8,128)(2,1)S(1)}, bf16[4,256,384]{2,1,0:T(8,128)(2,1)S(1)}, u32[]{:S(2)}, u32[]{:S(2)}) %collective-permute-start) | collective-permute-done | bytes 786464 | tf_op jit(solution)/shard_map/core_sum/ppermute | solution.py:354
  36.3 0.2 core_sum.1
  36.5 1.3 %collective-permute-start.1 = (bf16[256,384]{1,0:T(8,128)(2,1)S(1)}, bf16[256,384]{1,0:T(8,128)(2,1)S(1)}, u32[]{:S(2)}, u32[]{:S(2)}) collective-permute-start(bf16[256,384]{1,0:T(8,128)(2,1)S(1)} %get-tuple-element.23), channel_id=1, source_target_pairs={{0,2},{2,4},{4,6},{6,0},{1,3},{3,5},{5,7},{7,1},{8,10},{10,12},{12... | collective-permute-start | bytes 589832 | tf_op jit(solution)/shard_map/x_sum/ppermute | solution.py:354
  37.8 1.5 %collective-permute-start.2 = (bf16[256,384]{1,0:T(8,128)(2,1)S(1)}, bf16[256,384]{1,0:T(8,128)(2,1)S(1)}, u32[]{:S(2)}, u32[]{:S(2)}) collective-permute-start(bf16[256,384]{1,0:T(8,128)(2,1)S(1)} %get-tuple-element.24), channel_id=1, source_target_pairs={{0,6},{2,0},{4,2},{6,4},{1,7},{3,1},{5,3},{7,5},{8,14},{10,8},{12,... | collective-permute-start | bytes 589832 | tf_op jit(solution)/shard_map/x_sum/ppermute | solution.py:354
  39.3 1.5 %collective-permute-start.3 = (bf16[256,384]{1,0:T(8,128)(2,1)S(1)}, bf16[256,384]{1,0:T(8,128)(2,1)S(1)}, u32[]{:S(2)}, u32[]{:S(2)}) collective-permute-start(bf16[256,384]{1,0:T(8,128)(2,1)S(1)} %get-tuple-element.25), channel_id=1, source_target_pairs={{0,4},{2,6},{4,0},{6,2},{1,5},{3,7},{5,1},{7,3},{8,12},{10,14},{12... | collective-permute-start | bytes 589832 | tf_op jit(solution)/shard_map/x_sum/ppermute | solution.py:354
  40.8 3.1 %collective-permute-done.1.one_ref = bf16[256,384]{1,0:T(8,128)(2,1)S(1)} collective-permute-done((bf16[256,384]{1,0:T(8,128)(2,1)S(1)}, bf16[256,384]{1,0:T(8,128)(2,1)S(1)}, u32[]{:S(2)}, u32[]{:S(2)}) %collective-permute-start.1) | collective-permute-done | bytes 196640 | tf_op jit(solution)/shard_map/x_sum/ppermute | solution.py:354
  43.9 0.0 collective-permute-done.2.two_ref
  43.9 5.2 %collective-permute-done.3.three_ref = bf16[256,384]{1,0:T(8,128)(2,1)S(1)} collective-permute-done((bf16[256,384]{1,0:T(8,128)(2,1)S(1)}, bf16[256,384]{1,0:T(8,128)(2,1)S(1)}, u32[]{:S(2)}, u32[]{:S(2)}) %collective-permute-start.3) | collective-permute-done | bytes 196640 | tf_op jit(solution)/shard_map/x_sum/ppermute | solution.py:354
  49.1 0.1 x_sum.1
  49.2 13.9 %all_to_all.21.joint_ref = bf16[32,8,640]{2,1,0:T(8,128)(2,1)S(1)} all-to-all(bf16[32,8,640]{2,1,0:T(8,128)(2,1)S(1)} %x_sum.1), channel_id=1, replica_groups=mesh['y'=4,'z'=8,'x'=4,'c'=2] {'y','z'}, dimensions={0} | all-to-all | bytes 655360 | tf_op jit(solution)/shard_map/yz_sum/all_to_all | solution.py:426
  63.1 1.9 %yz_sum.1 = (bf16[8,8,384]{2,1,0:T(8,128)(2,1)S(1)}, bf16[512,256]{1,0:T(8,128)(2,1)}) custom-call(bf16[32,8,640]{2,1,0:T(8,128)(2,1)S(1)} %all_to_all.21.joint_ref, s32[8,32]{1,0:T(8,128)} %bitcast.21), custom_call_target="tpu_custom_call" | custom-call | tf_op jit(solution)/shard_map/yz_sum/pallas_call | solution.py:344
  65.0 12.1 %all_to_all.22 = bf16[8,8,384]{2,1,0:T(8,128)(2,1)S(1)} all-to-all(bf16[8,8,384]{2,1,0:T(8,128)(2,1)S(1)} %get-tuple-element.28), channel_id=1, replica_groups=mesh['y'=4,'z'=8,'x'=4,'c'=2] {'z'}, dimensions={0} | all-to-all | bytes 98304 | tf_op jit(solution)/shard_map/z_gather/all_to_all | solution.py:436
  77.1 0.1 broadcast_in_dim.8
  77.2 13.3 %all_to_all.23 = bf16[16,64,384]{2,1,0:T(8,128)(2,1)S(1)} all-to-all(bf16[16,64,384]{2,1,0:T(8,128)(2,1)S(1)} %broadcast_in_dim.8), channel_id=1, replica_groups=mesh['y'=4,'z'=8,'x'=4,'c'=2] {'y','x'}, dimensions={0} | all-to-all | bytes 1572864 | tf_op jit(solution)/shard_map/yx_gather/all_to_all | solution.py:439
  90.5 5.5 %collective-permute-start.4 = (bf16[16,64,384]{2,1,0:T(8,128)(2,1)S(1)}, bf16[16,64,384]{2,1,0:T(8,128)(2,1)S(1)}, u32[]{:S(2)}, u32[]{:S(2)}) collective-permute-start(bf16[16,64,384]{2,1,0:T(8,128)(2,1)S(1)} %all_to_all.23), channel_id=1, source_target_pairs={{0,1},{1,0},{2,3},{3,2},{4,5},{5,4},{6,7},{7,6},{8,9},{9,8},{10,11... | collective-permute-start | bytes 2359304 | tf_op jit(solution)/shard_map/core_gather/ppermute | solution.py:354
  96.0 1.2 %spread.2 = (f32[256,768]{1,0:T(8,128)}, f32[256,256]{1,0:T(8,128)}, f32[256,1024]{1,0:T(8,128)}, f32[1024,256]{1,0:T(8,128)}) custom-call(bf16[4,4,64,384]{3,2,1,0:T(8,128)(2,1)S(1)} %bitcast.13), custom_call_target="tpu_custom_call" | custom-call | bytes 3000000 | tf_op jit(solution)/shard_map/spread/pallas_call | solution.py:313
  97.2 0.7 collective-permute-done.4
  97.9 1.2 %spread.3 = (f32[256,768]{1,0:T(8,128)}, f32[256,256]{1,0:T(8,128)}, f32[256,1024]{1,0:T(8,128)}, f32[1024,256]{1,0:T(8,128)}) custom-call(bf16[4,4,64,384]{3,2,1,0:T(8,128)(2,1)S(1)} %bitcast.16, f32[256,768]{1,0:T(8,128)} %get-tuple-element.29.refs_0_, ...), custom_call_target="tpu_custom_call", output_to_operand_aliasing={{0}: (1, {}), {1}: (2, {}), {2}: (3, {}), {3}: (4, {})} | custom-call | bytes 3000000 | tf_op jit(solution)/shard_map/spread/pallas_call | solution.py:313
Async XLA Ops:
  30.6 5.7 %collective-permute-start = (bf16[4,256,384]{2,1,0:T(8,128)(2,1)S(1)}, bf16[4,256,384]{2,1,0:T(8,128)(2,1)S(1)}, u32[]{:S(2)}, u32[]{:S(2)}) collective-permute-start(bf16[4,256,384]{2,1,0:T(8,128)(2,1)S(1)} %slice_bitcast_fusion), channel_id=1, source_target_pairs={{0,1},{1,0},{2,3},{3,2},{4,5},{5,4},{6,7},{7,6},{8,9},{9,8},{10,11... | collective-permute-start | bytes 2359304 | tf_op jit(solution)/shard_map/core_sum/ppermute | solution.py:354
  36.5 7.4 %collective-permute-start.1 = (bf16[256,384]{1,0:T(8,128)(2,1)S(1)}, bf16[256,384]{1,0:T(8,128)(2,1)S(1)}, u32[]{:S(2)}, u32[]{:S(2)}) collective-permute-start(bf16[256,384]{1,0:T(8,128)(2,1)S(1)} %get-tuple-element.23), channel_id=1, source_target_pairs={{0,2},{2,4},{4,6},{6,0},{1,3},{3,5},{5,7},{7,1},{8,10},{10,12},{12... | collective-permute-start | bytes 589832 | tf_op jit(solution)/shard_map/x_sum/ppermute | solution.py:354
  37.8 6.1 %collective-permute-start.2 = (bf16[256,384]{1,0:T(8,128)(2,1)S(1)}, bf16[256,384]{1,0:T(8,128)(2,1)S(1)}, u32[]{:S(2)}, u32[]{:S(2)}) collective-permute-start(bf16[256,384]{1,0:T(8,128)(2,1)S(1)} %get-tuple-element.24), channel_id=1, source_target_pairs={{0,6},{2,0},{4,2},{6,4},{1,7},{3,1},{5,3},{7,5},{8,14},{10,8},{12,... | collective-permute-start | bytes 589832 | tf_op jit(solution)/shard_map/x_sum/ppermute | solution.py:354
  39.3 9.8 %collective-permute-start.3 = (bf16[256,384]{1,0:T(8,128)(2,1)S(1)}, bf16[256,384]{1,0:T(8,128)(2,1)S(1)}, u32[]{:S(2)}, u32[]{:S(2)}) collective-permute-start(bf16[256,384]{1,0:T(8,128)(2,1)S(1)} %get-tuple-element.25), channel_id=1, source_target_pairs={{0,4},{2,6},{4,0},{6,2},{1,5},{3,7},{5,1},{7,3},{8,12},{10,14},{12... | collective-permute-start | bytes 589832 | tf_op jit(solution)/shard_map/x_sum/ppermute | solution.py:354
  90.5 7.4 %collective-permute-start.4 = (bf16[16,64,384]{2,1,0:T(8,128)(2,1)S(1)}, bf16[16,64,384]{2,1,0:T(8,128)(2,1)S(1)}, u32[]{:S(2)}, u32[]{:S(2)}) collective-permute-start(bf16[16,64,384]{2,1,0:T(8,128)(2,1)S(1)} %all_to_all.23), channel_id=1, source_target_pairs={{0,1},{1,0},{2,3},{3,2},{4,5},{5,4},{6,7},{7,6},{8,9},{9,8},{10,11... | collective-permute-start | bytes 2359304 | tf_op jit(solution)/shard_map/core_gather/ppermute | solution.py:354

commit v6 on v5

--- a/solution.py
+++ b/solution.py
@@ -267,11 +267,14 @@
     out_ref[:, :, 384:640] = grad_ref[...].reshape(32, 8, 256)
 
 
-def yz_sum_kernel(joint_ref, valid_hbm, total_ref, out_ref, valid_ref, arrived):
+def yz_sum_kernel(joint_ref, total_ref):
+    total = jnp.sum(joint_ref[:, :, 0:384].astype(F32), axis=0).astype(BF16)
+    total_ref[...] = jnp.broadcast_to(total[None], total_ref.shape)
+
+
+def expand_kernel(joint_ref, valid_hbm, out_ref, valid_ref, arrived):
     copy = pltpu.make_async_copy(valid_hbm, valid_ref, arrived)
     copy.start()
-    total = jnp.sum(joint_ref[:, :, 0:384].astype(F32), axis=0).astype(BF16)
-    total_ref[...] = jnp.broadcast_to(total[None], total_ref.shape)
     copy.wait()
     valid = valid_ref[...]
     for group in range(2):
@@ -335,7 +338,7 @@
     return pltpu.with_memory_space_constraint(array, pltpu.HBM)
 
 
-def run(kernel, out_shape, *args, scratch=(), held=()):
+def run(kernel, out_shape, *args, scratch=(), held=(), cost=None):
     specs = [
         pl.BlockSpec(memory_space=pltpu.HBM if at in held else pltpu.VMEM)
         for at in range(len(args))
@@ -347,6 +350,8 @@
         in_specs=specs,
         scratch_shapes=list(scratch),
         compiler_params=pltpu.CompilerParams(vmem_limit_bytes=VMEM_LIMIT),
+        cost_estimate=cost
+        and pl.CostEstimate(flops=0, bytes_accessed=cost, transcendentals=0),
     )(*args)
 
 
@@ -420,18 +425,11 @@
         other = shift(terms[1], "c", 2, 1)
         slots = run(core_sum_kernel, (piece,) * 4, terms, other)
     with jax.named_scope("x_sum"):
-        got = [shift(slots[by], "x", 4, by) for by in (1, 3, 2)]
+        got = [shift(slots[by], "x", 4, by) for by in (2, 1, 3)]
         joint = run(x_sum_kernel, shape((32, 8, 640), BF16), slots[0], *got, grad)
     with jax.named_scope("yz_sum"):
         joint = lax.all_to_all(joint, dates, split_axis=0, concat_axis=0, tiled=True)
-        total, feature_grad = run(
-            yz_sum_kernel,
-            (shape((8, 8, 384), BF16), shape((512, width), BF16)),
-            joint,
-            valid_dates.T,
-            held=(1,),
-            scratch=(pltpu.VMEM((8, 32), jnp.int32), pltpu.SemaphoreType.DMA),
-        )
+        total = run(yz_sum_kernel, shape((8, 8, 384), BF16), joint)
     with jax.named_scope("z_gather"):
         part = lax.all_to_all(total, "z", split_axis=0, concat_axis=0, tiled=True)
     with jax.named_scope("yx_gather"):
@@ -439,6 +437,17 @@
         mine = lax.all_to_all(part, ("y", "x"), split_axis=0, concat_axis=0, tiled=True)
     with jax.named_scope("core_gather"):
         other = shift(mine, "c", 2, 1)
+        joint, _ = lax.optimization_barrier((joint, mine))
+    with jax.named_scope("expand"):
+        feature_grad = run(
+            expand_kernel,
+            shape((512, width), BF16),
+            joint,
+            valid_dates.T,
+            held=(1,),
+            scratch=(pltpu.VMEM((8, 32), jnp.int32), pltpu.SemaphoreType.DMA),
+            cost=1000000,
+        )
     with jax.named_scope("spread"):
         outs = spread(0, mine.reshape(4, 4, 64, 384))
         outs = spread(1, other.reshape(4, 4, 64, 384), *outs)

time: 99.4 us -> 101 us (1.016)
  blocking collectives: 60.8 us -> 64 us
  waiting for transfers between devices: 10.9 us -> 9.03 us
    all_to_all x1, blocking collectives: 13.3 us -> 16 us  [per_device(): lax.all_to_all(part, ('y', 'x'), split_axis=0, concat_axis=0, tiled=True)]
    ppermute x5, waiting for transfers between devices: 10.9 us -> 9.03 us  [shift(): lax.ppermute(array, axis, [(at, (at + by) % size) for at in range(size)])]
    pallas_call x5 -> x6, Pallas kernels: 10.5 us -> 10.5 us  [run(): pl.pallas_call(kernel, out_shape=out_shape, in_specs=specs, scratch_shape...]
  transfers between devices with their start and end apart: 5 -> 5, of which waited for: 4 -> 3; matrix products, arithmetic and copies ran while one was open for 0% -> 0% of each run, Pallas kernels for 1% -> 3%
where the time goes in v6:
time: 101 us; the launch traced here: 100 us
  blocking collectives  64 us (63%)
  starting transfers between devices  13.4 us (13%)
  Pallas kernels  13 us (13%)
  waiting for transfers between devices  9.03 us (9%)
    all_to_all x1, blocking collectives, per_device(): lax.all_to_all(send.reshape(32, 16, width), dates, split_axis=0, concat_a...  21.5 us
    all_to_all x1, blocking collectives, per_device(): lax.all_to_all(part, ('y', 'x'), split_axis=0, concat_axis=0, tiled=True)  16 us
    all_to_all x1, blocking collectives, per_device(): lax.all_to_all(joint, dates, split_axis=0, concat_axis=0, tiled=True)  14.2 us
    ppermute x5, starting transfers between devices, shift(): lax.ppermute(array, axis, [(at, (at + by) % size) for at in range(size)])  13.4 us
    all_to_all x1, blocking collectives, per_device(): part = lax.all_to_all(total, 'z', split_axis=0, concat_axis=0, tiled=True)  12.3 us
    pallas_call x6, Pallas kernels, run(): pl.pallas_call(kernel, out_shape=out_shape, in_specs=specs, scratch_shape...  10.5 us
    ppermute x5, waiting for transfers between devices, shift(): lax.ppermute(array, axis, [(at, (at + by) % size) for at in range(size)])  9.03 us
    pallas_call x2, Pallas kernels, spread(): pl.pallas_call(functools.partial(spread_kernel, flip), out_shape=(shape((...  2.44 us
  transfers between devices with their start and end apart: 5, of which 3 were waited for; matrix products, arithmetic and copies ran while one was open for 0% of the time, Pallas kernels for 3%

profile of v6, /device:TPU:1, one launch (start us, length us, event | category | flops | bytes accessed | tf_op | source)
XLA Modules:
  0.0 100.2 jit_solution(8565736474978544123)
XLA Ops:
  0.6 1.4 %compact.1 = bf16[512,256]{1,0:T(8,128)(2,1)S(1)} custom-call(bf16[512,256]{1,0:T(8,128)(2,1)} %bitcast.17, bf16[512,256]{1,0:T(8,128)(2,1)} %bitcast.18, s32[8,32]{1,0:T(8,128)} %bitcast.21), custom_call_target="tpu_custom_call" | custom-call | tf_op jit(solution)/shard_map/compact/pallas_call | solution.py:347
  2.0 21.5 %all_to_all.20 = bf16[32,16,256]{2,1,0:T(8,128)(2,1)S(1)} all-to-all(bf16[32,16,256]{2,1,0:T(8,128)(2,1)S(1)} %bitcast.14), channel_id=1, replica_groups=mesh['y'=4,'z'=8,'x'=4,'c'=2] {'y','z'}, dimensions={0} | all-to-all | bytes 524288 | tf_op jit(solution)/shard_map/to_owner/all_to_all | solution.py:393
  23.5 6.9 %layer.1 = (bf16[256,256]{1,0:T(8,128)(2,1)S(1)}, bf16[2,4,256,384]{3,2,1,0:T(8,128)(2,1)S(1)}) custom-call(bf16[512,256]{1,0:T(8,128)(2,1)S(1)} %bitcast.15, f32[1,256]{1,0:T(1,128)} %bitcast.23, bf16[256,768]{1,0:T(8,128)(2,1)} %qkv_hbm.1, bf16[256,256]{1,0:T(8,128)(2,1)} %out_w_hbm.1, f32[1,256]{1,0:T(1,128)} %bitcast.24, bf16[256,1024]{1,0:T(8,128)(2,1)} %up_hbm.1, ...), custom_call_target="tpu_custom_call" | custom-call | tf_op jit(solution)/shard_map/layer/pallas_call | solution.py:347
  30.5 0.1 slice_bitcast_fusion
  30.6 3.8 %collective-permute-start = (bf16[4,256,384]{2,1,0:T(8,128)(2,1)S(1)}, bf16[4,256,384]{2,1,0:T(8,128)(2,1)S(1)}, u32[]{:S(2)}, u32[]{:S(2)}) collective-permute-start(bf16[4,256,384]{2,1,0:T(8,128)(2,1)S(1)} %slice_bitcast_fusion), channel_id=1, source_target_pairs={{0,1},{1,0},{2,3},{3,2},{4,5},{5,4},{6,7},{7,6},{8,9},{9,8},{10,11... | collective-permute-start | bytes 2359304 | tf_op jit(solution)/shard_map/core_sum/ppermute | solution.py:359
  34.4 1.9 %collective-permute-done.other_ref = bf16[4,256,384]{2,1,0:T(8,128)(2,1)S(1)} collective-permute-done((bf16[4,256,384]{2,1,0:T(8,128)(2,1)S(1)}, bf16[4,256,384]{2,1,0:T(8,128)(2,1)S(1)}, u32[]{:S(2)}, u32[]{:S(2)}) %collective-permute-start) | collective-permute-done | bytes 786464 | tf_op jit(solution)/shard_map/core_sum/ppermute | solution.py:359
  36.3 0.2 core_sum.1
  36.5 2.8 %collective-permute-start.1 = (bf16[256,384]{1,0:T(8,128)(2,1)S(1)}, bf16[256,384]{1,0:T(8,128)(2,1)S(1)}, u32[]{:S(2)}, u32[]{:S(2)}) collective-permute-start(bf16[256,384]{1,0:T(8,128)(2,1)S(1)} %get-tuple-element.22), channel_id=1, source_target_pairs={{0,4},{2,6},{4,0},{6,2},{1,5},{3,7},{5,1},{7,3},{8,12},{10,14},{12... | collective-permute-start | bytes 589832 | tf_op jit(solution)/shard_map/x_sum/ppermute | solution.py:359
  39.3 0.3 collective-permute-start.2
  39.6 2.4 %collective-permute-start.3 = (bf16[256,384]{1,0:T(8,128)(2,1)S(1)}, bf16[256,384]{1,0:T(8,128)(2,1)S(1)}, u32[]{:S(2)}, u32[]{:S(2)}) collective-permute-start(bf16[256,384]{1,0:T(8,128)(2,1)S(1)} %get-tuple-element.24), channel_id=1, source_target_pairs={{0,6},{2,0},{4,2},{6,4},{1,7},{3,1},{5,3},{7,5},{8,14},{10,8},{12,... | collective-permute-start | bytes 589832 | tf_op jit(solution)/shard_map/x_sum/ppermute | solution.py:359
  42.0 2.2 %collective-permute-done.1.one_ref = bf16[256,384]{1,0:T(8,128)(2,1)S(1)} collective-permute-done((bf16[256,384]{1,0:T(8,128)(2,1)S(1)}, bf16[256,384]{1,0:T(8,128)(2,1)S(1)}, u32[]{:S(2)}, u32[]{:S(2)}) %collective-permute-start.1) | collective-permute-done | bytes 196640 | tf_op jit(solution)/shard_map/x_sum/ppermute | solution.py:359
  44.2 4.9 %collective-permute-done.2.two_ref = bf16[256,384]{1,0:T(8,128)(2,1)S(1)} collective-permute-done((bf16[256,384]{1,0:T(8,128)(2,1)S(1)}, bf16[256,384]{1,0:T(8,128)(2,1)S(1)}, u32[]{:S(2)}, u32[]{:S(2)}) %collective-permute-start.2) | collective-permute-done | bytes 196640 | tf_op jit(solution)/shard_map/x_sum/ppermute | solution.py:359
  49.1 0.0 collective-permute-done.3.three_ref
  49.1 0.1 x_sum.1
  49.2 14.2 %all_to_all.21.joint_ref = bf16[32,8,640]{2,1,0:T(8,128)(2,1)S(1)} all-to-all(bf16[32,8,640]{2,1,0:T(8,128)(2,1)S(1)} %x_sum.1), channel_id=1, replica_groups=mesh['y'=4,'z'=8,'x'=4,'c'=2] {'y','z'}, dimensions={0} | all-to-all | bytes 655360 | tf_op jit(solution)/shard_map/yz_sum/all_to_all | solution.py:431
  63.5 12.3 %all_to_all.22 = bf16[8,8,384]{2,1,0:T(8,128)(2,1)S(1)} all-to-all(bf16[8,8,384]{2,1,0:T(8,128)(2,1)S(1)} %yz_sum.1), channel_id=1, replica_groups=mesh['y'=4,'z'=8,'x'=4,'c'=2] {'z'}, dimensions={0} | all-to-all | bytes 98304 | tf_op jit(solution)/shard_map/z_gather/all_to_all | solution.py:434
  75.8 0.1 broadcast_in_dim.8
  75.9 16.0 %all_to_all.23 = bf16[16,64,384]{2,1,0:T(8,128)(2,1)S(1)} all-to-all(bf16[16,64,384]{2,1,0:T(8,128)(2,1)S(1)} %broadcast_in_dim.8), channel_id=1, replica_groups=mesh['y'=4,'z'=8,'x'=4,'c'=2] {'y','x'}, dimensions={0} | all-to-all | bytes 1572864 | tf_op jit(solution)/shard_map/yx_gather/all_to_all | solution.py:437
  91.8 4.1 %collective-permute-start.4 = (bf16[16,64,384]{2,1,0:T(8,128)(2,1)S(1)}, bf16[16,64,384]{2,1,0:T(8,128)(2,1)S(1)}, u32[]{:S(2)}, u32[]{:S(2)}) collective-permute-start(bf16[16,64,384]{2,1,0:T(8,128)(2,1)S(1)} %all_to_all.23), channel_id=1, source_target_pairs={{0,1},{1,0},{2,3},{3,2},{4,5},{5,4},{6,7},{7,6},{8,9},{9,8},{10,11... | collective-permute-start | bytes 2359304 | tf_op jit(solution)/shard_map/core_gather/ppermute | solution.py:359
  95.9 1.9 %expand.1 = bf16[512,256]{1,0:T(8,128)(2,1)} custom-call(bf16[32,8,640]{2,1,0:T(8,128)(2,1)S(1)} %all_to_all.21.joint_ref, s32[8,32]{1,0:T(8,128)} %bitcast.22), custom_call_target="tpu_custom_call" | custom-call | bytes 1000000 | tf_op jit(solution)/shard_map/expand/pallas_call | solution.py:347
  97.8 1.2 %spread.2 = (f32[256,768]{1,0:T(8,128)}, f32[256,256]{1,0:T(8,128)}, f32[256,1024]{1,0:T(8,128)}, f32[1024,256]{1,0:T(8,128)}) custom-call(bf16[4,4,64,384]{3,2,1,0:T(8,128)(2,1)S(1)} %bitcast.13), custom_call_target="tpu_custom_call" | custom-call | bytes 3000000 | tf_op jit(solution)/shard_map/spread/pallas_call | solution.py:316
  99.0 0.0 collective-permute-done.4
  99.0 1.2 %spread.3 = (f32[256,768]{1,0:T(8,128)}, f32[256,256]{1,0:T(8,128)}, f32[256,1024]{1,0:T(8,128)}, f32[1024,256]{1,0:T(8,128)}) custom-call(bf16[4,4,64,384]{3,2,1,0:T(8,128)(2,1)S(1)} %bitcast.16, f32[256,768]{1,0:T(8,128)} %get-tuple-element.27.refs_0_, ...), custom_call_target="tpu_custom_call", output_to_operand_aliasing={{0}: (1, {}), {1}: (2, {}), {2}: (3, {}), {3}: (4, {})} | custom-call | bytes 3000000 | tf_op jit(solution)/shard_map/spread/pallas_call | solution.py:316
  (1 shorter events, 0.0 us)
Async XLA Ops:
  30.6 5.7 %collective-permute-start = (bf16[4,256,384]{2,1,0:T(8,128)(2,1)S(1)}, bf16[4,256,384]{2,1,0:T(8,128)(2,1)S(1)}, u32[]{:S(2)}, u32[]{:S(2)}) collective-permute-start(bf16[4,256,384]{2,1,0:T(8,128)(2,1)S(1)} %slice_bitcast_fusion), channel_id=1, source_target_pairs={{0,1},{1,0},{2,3},{3,2},{4,5},{5,4},{6,7},{7,6},{8,9},{9,8},{10,11... | collective-permute-start | bytes 2359304 | tf_op jit(solution)/shard_map/core_sum/ppermute | solution.py:359
  36.5 7.7 %collective-permute-start.1 = (bf16[256,384]{1,0:T(8,128)(2,1)S(1)}, bf16[256,384]{1,0:T(8,128)(2,1)S(1)}, u32[]{:S(2)}, u32[]{:S(2)}) collective-permute-start(bf16[256,384]{1,0:T(8,128)(2,1)S(1)} %get-tuple-element.22), channel_id=1, source_target_pairs={{0,4},{2,6},{4,0},{6,2},{1,5},{3,7},{5,1},{7,3},{8,12},{10,14},{12... | collective-permute-start | bytes 589832 | tf_op jit(solution)/shard_map/x_sum/ppermute | solution.py:359
  39.3 9.8 %collective-permute-start.2 = (bf16[256,384]{1,0:T(8,128)(2,1)S(1)}, bf16[256,384]{1,0:T(8,128)(2,1)S(1)}, u32[]{:S(2)}, u32[]{:S(2)}) collective-permute-start(bf16[256,384]{1,0:T(8,128)(2,1)S(1)} %get-tuple-element.23), channel_id=1, source_target_pairs={{0,2},{2,4},{4,6},{6,0},{1,3},{3,5},{5,7},{7,1},{8,10},{10,12},{12... | collective-permute-start | bytes 589832 | tf_op jit(solution)/shard_map/x_sum/ppermute | solution.py:359
  39.6 9.5 %collective-permute-start.3 = (bf16[256,384]{1,0:T(8,128)(2,1)S(1)}, bf16[256,384]{1,0:T(8,128)(2,1)S(1)}, u32[]{:S(2)}, u32[]{:S(2)}) collective-permute-start(bf16[256,384]{1,0:T(8,128)(2,1)S(1)} %get-tuple-element.24), channel_id=1, source_target_pairs={{0,6},{2,0},{4,2},{6,4},{1,7},{3,1},{5,3},{7,5},{8,14},{10,8},{12,... | collective-permute-start | bytes 589832 | tf_op jit(solution)/shard_map/x_sum/ppermute | solution.py:359
  91.8 7.2 %collective-permute-start.4 = (bf16[16,64,384]{2,1,0:T(8,128)(2,1)S(1)}, bf16[16,64,384]{2,1,0:T(8,128)(2,1)S(1)}, u32[]{:S(2)}, u32[]{:S(2)}) collective-permute-start(bf16[16,64,384]{2,1,0:T(8,128)(2,1)S(1)} %all_to_all.23), channel_id=1, source_target_pairs={{0,1},{1,0},{2,3},{3,2},{4,5},{5,4},{6,7},{7,6},{8,9},{9,8},{10,11... | collective-permute-start | bytes 2359304 | tf_op jit(solution)/shard_map/core_gather/ppermute | solution.py:359

commit v7 on v6

--- a/solution.py
+++ b/solution.py
@@ -33,7 +33,7 @@
 NT = ((1,), (1,))
 
 
-def slot_matrix(valid, group, rows_per_block):
+def slot_matrix(valid, group):
     date = iota((8, 256), 1) % 8
     day = iota((8, 256), 0)
     held = valid.astype(F32)
@@ -42,10 +42,10 @@
     own = iota((32, 256), 0) == iota((32, 256), 1) // 16 + group * 16
     keep = jnp.sum(jnp.where(own, keep_all, 0.0), axis=0, keepdims=True)
     rank = jnp.sum(jnp.where(own, rank_all, 0.0), axis=0, keepdims=True)
-    shape = (16 * rows_per_block, 256)
+    shape = (256, 256)
     row, col = iota(shape, 0), iota(shape, 1)
     match = (
-        (row // rows_per_block == col // 16)
+        (row // 16 == col // 16)
         & ((row // 4) % 2 == (col // 8) % 2)
         & (rank == (row % 4).astype(F32))
         & (keep > 0.5)
@@ -53,7 +53,7 @@
     return match.astype(F32)
 
 
-def compact_kernel(feat_hbm, cot_hbm, valid_hbm, send_ref, feat, cot, valid_ref, arrived):
+def compact_kernel(feat_hbm, cot_hbm, valid_hbm, send_ref, match_ref, feat, cot, valid_ref, arrived):
     copies = [
         pltpu.make_async_copy(valid_hbm, valid_ref, arrived.at[0]),
         pltpu.make_async_copy(feat_hbm, feat, arrived.at[1]),
@@ -66,10 +66,11 @@
     is_feat = (iota((256, 1), 0) // 8) % 2 == 0
     picks = []
     for group in range(2):
-        match = slot_matrix(valid, group, 16)
+        match = slot_matrix(valid, group)
         pick_feat = jnp.where(is_feat, match, 0.0).astype(BF16)
         pick_cot = jnp.where(is_feat, 0.0, match).astype(BF16)
         filled = jnp.sum(match, axis=1, keepdims=True) > 0.5
+        match_ref[group] = match.reshape(16, 16, 256)[:, :8].reshape(128, 256).astype(BF16)
         picks.append((pick_feat, pick_cot, is_feat & jnp.logical_not(filled)))
     copies[1].wait()
     copies[2].wait()
@@ -104,20 +105,10 @@
     up_hbm,
     down_hbm,
     grad_ref,
-    terms_ref,
-    gain_first_ref,
-    qkv_ref,
-    out_w_ref,
-    gain_second_ref,
-    up_ref,
-    down_ref,
-    arrived,
-    probs,
-    proj_t,
-    att_t,
-    att_grad_t,
-    proj_grad_t,
+    *rest,
 ):
+    (*sent_refs, gain_first_ref, qkv_ref, out_w_ref, gain_second_ref, up_ref, down_ref) = rest[:14]
+    arrived, probs, proj_t, att_t, att_grad_t, proj_grad_t, terms_ref = rest[14:]
     pairs = (
         (qkv_hbm, qkv_ref),
         (gain_first_hbm, gain_first_ref),
@@ -252,16 +243,17 @@
     slot = iota((256, 256), 0)
     want = slot // 4 % 2 * 128 + slot // 8 * 4 + slot % 4
     grad_ref[...] = dot((iota((256, 256), 1) == want).astype(BF16), grad).astype(BF16)
-
-
-def core_sum_kernel(terms_ref, other_ref, *outs):
-    for slot, out_ref in enumerate(outs):
-        total = terms_ref[0, slot].astype(F32) + other_ref[slot].astype(F32)
-        out_ref[...] = total.astype(BF16)
-
-
-def x_sum_kernel(own_ref, one_ref, two_ref, three_ref, grad_ref, out_ref):
-    total = own_ref[...].astype(F32) + one_ref[...].astype(F32)
+    for at, sent_ref in enumerate(sent_refs):
+        sent_ref[...] = terms_ref[at // 4, at % 4]
+
+
+def core_sum_kernel(mine_ref, other_ref, out_ref):
+    out_ref[...] = (mine_ref[...].astype(F32) + other_ref[...].astype(F32)).astype(BF16)
+
+
+def x_sum_kernel(mine_ref, other_ref, one_ref, two_ref, three_ref, grad_ref, out_ref):
+    total = mine_ref[...].astype(F32) + other_ref[...].astype(F32)
+    total = total + one_ref[...].astype(F32)
     total = total + two_ref[...].astype(F32) + three_ref[...].astype(F32)
     out_ref[:, :, 0:384] = total.astype(BF16).reshape(32, 8, 384)
     out_ref[:, :, 384:640] = grad_ref[...].reshape(32, 8, 256)
@@ -272,66 +264,76 @@
     total_ref[...] = jnp.broadcast_to(total[None], total_ref.shape)
 
 
-def expand_kernel(joint_ref, valid_hbm, out_ref, valid_ref, arrived):
-    copy = pltpu.make_async_copy(valid_hbm, valid_ref, arrived)
-    copy.start()
-    copy.wait()
-    valid = valid_ref[...]
+def expand_kernel(joint_ref, match_ref, out_ref):
     for group in range(2):
-        match = slot_matrix(valid, group, 8).astype(BF16)
         back = joint_ref[group * 16 : group * 16 + 16, :, 384:640].reshape(128, 256)
-        out_ref[pl.ds(group * 256, 256), :] = dot(match, back, TN).astype(BF16)
-
-
-def spread_kernel(flip, held_ref, *refs):
+        out_ref[pl.ds(group * 256, 256), :] = dot(match_ref[group], back, TN).astype(BF16)
+
+
+def spread_kernel(pieces, *refs):
+    count = len(pieces)
+    held = refs[:count]
     qkv_hbm, out_hbm, up_hbm, down_hbm, wide, narrow, sent = refs[-7:]
-    core = lax.axis_index("c") ^ flip
-    copies = []
-    for pair in range(4):
-        group = 2 * pair + core
-        for lane in range(4):
-            rows = slice(lane * 64, lane * 64 + 64)
-            piece = held_ref[lane, pair].astype(F32)
-            wide[pair, rows, :] = piece[:, :256]
-            narrow[pair, rows, :] = piece[:, 256:]
-        if pair < 2:
-            far = up_hbm.at[:, pl.ds(pl.multiple_of(group * 256, 256), 256)]
-        else:
-            far = down_hbm.at[pl.ds(pl.multiple_of((group - 4) * 256, 256), 256), :]
-        if pair < 3:
-            near = qkv_hbm.at[:, pl.ds(pl.multiple_of(group * 128, 128), 128)]
-        else:
-            near = out_hbm.at[:, pl.ds(pl.multiple_of((group - 6) * 128, 128), 128)]
-        for source, target, at in ((wide, far, 0), (narrow, near, 1)):
-            copy = pltpu.make_async_copy(source.at[pair], target, sent.at[pair, at])
-            copy.start()
-            copies.append(copy)
-    for copy in copies:
+    core, place = lax.axis_index("c"), lax.axis_index("x")
+
+    def each(act):
+        for at, (hops, flip) in enumerate(pieces):
+            pair = lax.rem(place - hops + 4, 4)
+            group = 2 * pair + (core ^ flip)
+
+            def move(test, source, target, sem):
+                @pl.when(test)
+                def _():
+                    act(pltpu.make_async_copy(source.at[at], target(), sent.at[at, sem]))
+
+            def across(ref, first, size):
+                return lambda: ref.at[:, pl.ds(pl.multiple_of((group - first) * size, size), size)]
+
+            def along():
+                return down_hbm.at[pl.ds(pl.multiple_of((group - 4) * 256, 256), 256), :]
+
+            if act is start:
+                piece = held[at][...].astype(F32)
+                wide[at] = piece[:, :256]
+                narrow[at] = piece[:, 256:]
+            move(pair < 2, wide, across(up_hbm, 0, 256), 0)
+            move(pair >= 2, wide, along, 0)
+            move(pair < 3, narrow, across(qkv_hbm, 0, 128), 1)
+            move(pair >= 3, narrow, across(out_hbm, 6, 128), 1)
+
+    def start(copy):
+        copy.start()
+
+    def wait(copy):
         copy.wait()
 
-
-def spread(flip, held, *outs):
+    each(start)
+    each(wait)
+
+
+def spread(pieces, held, outs=()):
     shape = jax.ShapeDtypeStruct
     kept = pl.BlockSpec(memory_space=pl.ANY)
+    count = len(pieces)
     return pl.pallas_call(
-        functools.partial(spread_kernel, flip),
+        functools.partial(spread_kernel, pieces),
         out_shape=(
             shape((256, 768), F32),
             shape((256, 256), F32),
             shape((256, 1024), F32),
             shape((1024, 256), F32),
         ),
-        in_specs=[pl.BlockSpec(memory_space=pltpu.VMEM)] + [kept] * len(outs),
+        in_specs=[pl.BlockSpec(memory_space=pltpu.VMEM)] * count + [kept] * len(outs),
         out_specs=[kept] * 4,
         scratch_shapes=[
-            pltpu.VMEM((4, 256, 256), F32),
-            pltpu.VMEM((4, 256, 128), F32),
-            pltpu.SemaphoreType.DMA((4, 2)),
+            pltpu.VMEM((count, 256, 256), F32),
+            pltpu.VMEM((count, 256, 128), F32),
+            pltpu.SemaphoreType.DMA((count, 2)),
         ],
-        input_output_aliases={at + 1: at for at in range(len(outs))},
+        input_output_aliases={at + count: at for at in range(len(outs))},
         compiler_params=pltpu.CompilerParams(vmem_limit_bytes=VMEM_LIMIT),
-        cost_estimate=pl.CostEstimate(flops=0, bytes_accessed=3000000, transcendentals=0),
-    )(held, *outs)
+        cost_estimate=pl.CostEstimate(flops=0, bytes_accessed=2000000, transcendentals=0),
+    )(*held, *outs)
 
 
 def stay(array):
@@ -375,9 +377,9 @@
     scale = float(256 * 2 * 256) ** (-0.5)
     dates = ("y", "z")
     with jax.named_scope("compact"):
-        send = run(
+        send, match = run(
             compact_kernel,
-            shape((512, width), BF16),
+            (shape((512, width), BF16), shape((2, 128, 256), BF16)),
             features.reshape(512, width),
             cotangent.reshape(512, width),
             valid_dates.T,
@@ -395,9 +397,9 @@
         )
     piece = shape((256, 384), BF16)
     with jax.named_scope("layer"):
-        grad, terms = run(
+        grad, *terms = run(
             functools.partial(layer_kernel, scale),
-            (shape((256, width), BF16), shape((2, 4, 256, 384), BF16)),
+            (shape((256, width), BF16),) + (piece,) * 8,
             recv.reshape(512, width),
             gain_first.reshape(1, width),
             qkv_weight,
@@ -419,38 +421,37 @@
                 pltpu.VMEM((256, 256), BF16),
                 pltpu.VMEM((256, 256), BF16),
                 pltpu.VMEM((768, 256), BF16),
+                pltpu.VMEM((2, 4, 256, 384), BF16),
             ),
         )
     with jax.named_scope("core_sum"):
-        other = shift(terms[1], "c", 2, 1)
-        slots = run(core_sum_kernel, (piece,) * 4, terms, other)
+        other = {by: shift(terms[4 + by], "c", 2, 1) for by in (3, 1, 2, 0)}
+        slots = {by: run(core_sum_kernel, piece, terms[by], other[by]) for by in (3, 1, 2)}
     with jax.named_scope("x_sum"):
-        got = [shift(slots[by], "x", 4, by) for by in (2, 1, 3)]
-        joint = run(x_sum_kernel, shape((32, 8, 640), BF16), slots[0], *got, grad)
+        got = [shift(slots[by], "x", 4, by) for by in (3, 1, 2)]
+        joint = run(x_sum_kernel, shape((32, 8, 640), BF16), terms[0], other[0], *got, grad)
     with jax.named_scope("yz_sum"):
         joint = lax.all_to_all(joint, dates, split_axis=0, concat_axis=0, tiled=True)
-        total = run(yz_sum_kernel, shape((8, 8, 384), BF16), joint)
-    with jax.named_scope("z_gather"):
-        part = lax.all_to_all(total, "z", split_axis=0, concat_axis=0, tiled=True)
-    with jax.named_scope("yx_gather"):
-        part = jnp.broadcast_to(part.reshape(1, 64, 384), (16, 64, 384))
-        mine = lax.all_to_all(part, ("y", "x"), split_axis=0, concat_axis=0, tiled=True)
-    with jax.named_scope("core_gather"):
-        other = shift(mine, "c", 2, 1)
-        joint, _ = lax.optimization_barrier((joint, mine))
+        total = run(yz_sum_kernel, shape((32, 8, 384), BF16), joint)
+    with jax.named_scope("yz_gather"):
+        part = lax.all_to_all(total, dates, split_axis=0, concat_axis=0, tiled=True)
+        part = part.reshape(256, 384)
+        joint, _ = lax.optimization_barrier((joint, part))
+    with jax.named_scope("x_gather"):
+        near = {by: shift(part, "x", 4, by) for by in (2, 1, 3)}
+        part_far = shift(part, "c", 2, 1)
     with jax.named_scope("expand"):
         feature_grad = run(
-            expand_kernel,
-            shape((512, width), BF16),
-            joint,
-            valid_dates.T,
-            held=(1,),
-            scratch=(pltpu.VMEM((8, 32), jnp.int32), pltpu.SemaphoreType.DMA),
-            cost=1000000,
+            expand_kernel, shape((512, width), BF16), joint, match, cost=1000000
         )
     with jax.named_scope("spread"):
-        outs = spread(0, mine.reshape(4, 4, 64, 384))
-        outs = spread(1, other.reshape(4, 4, 64, 384), *outs)
+        outs = spread(((0, 0), (0, 1)), (part, part_far))
+    with jax.named_scope("core_gather"):
+        near, feature_grad, outs = lax.optimization_barrier((near, feature_grad, outs))
+        far = {by: shift(near[by], "c", 2, 1) for by in (2, 1, 3)}
+    with jax.named_scope("spread"):
+        outs = spread(((2, 0), (1, 0), (3, 0)), [near[by] for by in (2, 1, 3)], outs)
+        outs = spread(((2, 1), (1, 1), (3, 1)), [far[by] for by in (2, 1, 3)], outs)
     return (feature_grad.reshape(features.shape), *outs)
 
 

time: 101 us -> 98.6 us (0.976)
  blocking collectives: 64 us -> 52.4 us
  waiting for transfers between devices: 9.03 us -> 14.4 us
  starting transfers between devices: 13.4 us -> 18 us
    all_to_all x2 -> x1, blocking collectives: 28.3 us -> 16.7 us  [per_device(): part = lax.all_to_all(total, dates, split_axis=0, concat_axis=0, tiled=True)]
    ppermute x5 -> x14, waiting for transfers between devices: 9.03 us -> 14.4 us  [shift(): lax.ppermute(array, axis, [(at, (at + by) % size) for at in range(size)])]
    ppermute x5 -> x14, starting transfers between devices: 13.4 us -> 18 us  [shift(): lax.ppermute(array, axis, [(at, (at + by) % size) for at in range(size)])]
    pallas_call x6 -> x8, Pallas kernels: 10.5 us -> 9.71 us  [run(): pl.pallas_call(kernel, out_shape=out_shape, in_specs=specs, scratch_shape...]
    pallas_call x2 -> x3, Pallas kernels: 2.44 us -> 3.06 us  [spread(): pl.pallas_call(functools.partial(spread_kernel, pieces), out_shape=(shape...]
  transfers between devices with their start and end apart: 5 -> 14, of which waited for: 3 -> 6; matrix products, arithmetic and copies ran while one was open for 0% -> 0% of each run, Pallas kernels for 3% -> 3%
where the time goes in v7:
time: 98.6 us; the launch traced here: 98.4 us
  blocking collectives  52.4 us (53%)
  starting transfers between devices  18 us (18%)
  waiting for transfers between devices  14.4 us (15%)
  Pallas kernels  12.8 us (13%)
    all_to_all x1, blocking collectives, per_device(): lax.all_to_all(send.reshape(32, 16, width), dates, split_axis=0, concat_a...  21.5 us
    ppermute x14, starting transfers between devices, shift(): lax.ppermute(array, axis, [(at, (at + by) % size) for at in range(size)])  18 us
    all_to_all x1, blocking collectives, per_device(): part = lax.all_to_all(total, dates, split_axis=0, concat_axis=0, tiled=True)  16.7 us
    ppermute x14, waiting for transfers between devices, shift(): lax.ppermute(array, axis, [(at, (at + by) % size) for at in range(size)])  14.4 us
    all_to_all x1, blocking collectives, per_device(): lax.all_to_all(joint, dates, split_axis=0, concat_axis=0, tiled=True)  14.2 us
    pallas_call x8, Pallas kernels, run(): pl.pallas_call(kernel, out_shape=out_shape, in_specs=specs, scratch_shape...  9.71 us
    pallas_call x3, Pallas kernels, spread(): pl.pallas_call(functools.partial(spread_kernel, pieces), out_shape=(shape...  3.06 us
  transfers between devices with their start and end apart: 14, of which 6 were waited for; matrix products, arithmetic and copies ran while one was open for 0% of the time, Pallas kernels for 3%

profile of v7, /device:TPU:1, one launch (start us, length us, event | category | flops | bytes accessed | tf_op | source)
XLA Modules:
  0.0 98.4 jit_solution(10692497369847101719)
XLA Ops:
  0.6 1.4 %compact.1 = (bf16[512,256]{1,0:T(8,128)(2,1)S(1)}, bf16[2,128,256]{2,1,0:T(8,128)(2,1)S(1)}) custom-call(bf16[512,256]{1,0:T(8,128)(2,1)} %bitcast.16, bf16[512,256]{1,0:T(8,128)(2,1)} %bitcast.17, s32[8,32]{1,0:T(8,128)} %bitcast.19), custom_call_target="tpu_custom_call" | custom-call | tf_op jit(solution)/shard_map/compact/pallas_call | solution.py:349
  2.0 21.5 %all_to_all.15 = bf16[32,16,256]{2,1,0:T(8,128)(2,1)S(1)} all-to-all(bf16[32,16,256]{2,1,0:T(8,128)(2,1)S(1)} %bitcast.15), channel_id=1, replica_groups=mesh['y'=4,'z'=8,'x'=4,'c'=2] {'y','z'}, dimensions={0} | all-to-all | bytes 524288 | tf_op jit(solution)/shard_map/to_owner/all_to_all | solution.py:395
  23.5 7.0 %layer.1 = (bf16[256,256]{1,0:T(8,128)(2,1)S(1)}, bf16[256,384]{1,0:T(8,128)(2,1)S(1)}, bf16[256,384]{1,0:T(8,128)(2,1)S(1)}, bf16[256,384]{1,0:T(8,128)(2,1)S(1...) custom-call(bf16[512,256]{1,0:T(8,128)(2,1)S(1)} %bitcast.9, ...), custom_call_target="tpu_custom_call" | custom-call | tf_op jit(solution)/shard_map/layer/pallas_call | solution.py:349
  30.6 3.8 %collective-permute-start.5 = (bf16[256,384]{1,0:T(8,128)(2,1)S(1)}, bf16[256,384]{1,0:T(8,128)(2,1)S(1)}, u32[]{:S(2)}, u32[]{:S(2)}) collective-permute-start(bf16[256,384]{1,0:T(8,128)(2,1)S(1)} %get-tuple-element.45), channel_id=1, source_target_pairs={{0,1},{1,0},{2,3},{3,2},{4,5},{5,4},{6,7},{7,6},{8,9},{9,8},{10,11... | collective-permute-start | bytes 589832 | tf_op jit(solution)/shard_map/core_sum/ppermute | solution.py:361
  34.5 0.4 collective-permute-start.1
  35.0 0.5 collective-permute-done.5.other_ref
  35.5 2.8 %collective-permute-start.6 = (bf16[256,384]{1,0:T(8,128)(2,1)S(1)}, bf16[256,384]{1,0:T(8,128)(2,1)S(1)}, u32[]{:S(2)}, u32[]{:S(2)}) collective-permute-start(bf16[256,384]{1,0:T(8,128)(2,1)S(1)} %core_sum.5), channel_id=1, source_target_pairs={{0,4},{2,6},{4,0},{6,2},{1,5},{3,7},{5,1},{7,3},{8,12},{10,14},{12... | collective-permute-start | bytes 589832 | tf_op jit(solution)/shard_map/x_sum/ppermute | solution.py:361
  38.9 2.4 %collective-permute-start.2 = (bf16[256,384]{1,0:T(8,128)(2,1)S(1)}, bf16[256,384]{1,0:T(8,128)(2,1)S(1)}, u32[]{:S(2)}, u32[]{:S(2)}) collective-permute-start(bf16[256,384]{1,0:T(8,128)(2,1)S(1)} %core_sum.3), channel_id=1, source_target_pairs={{0,6},{2,0},{4,2},{6,4},{1,7},{3,1},{5,3},{7,5},{8,14},{10,8},{12,... | collective-permute-start | bytes 589832 | tf_op jit(solution)/shard_map/x_sum/ppermute | solution.py:361
  41.3 1.9 %collective-permute-done.6.three_ref = bf16[256,384]{1,0:T(8,128)(2,1)S(1)} collective-permute-done((bf16[256,384]{1,0:T(8,128)(2,1)S(1)}, bf16[256,384]{1,0:T(8,128)(2,1)S(1)}, u32[]{:S(2)}, u32[]{:S(2)}) %collective-permute-start.6) | collective-permute-done | bytes 196640 | tf_op jit(solution)/shard_map/x_sum/ppermute | solution.py:361
  43.2 4.9 %collective-permute-done.4.two_ref = bf16[256,384]{1,0:T(8,128)(2,1)S(1)} collective-permute-done((bf16[256,384]{1,0:T(8,128)(2,1)S(1)}, bf16[256,384]{1,0:T(8,128)(2,1)S(1)}, u32[]{:S(2)}, u32[]{:S(2)}) %collective-permute-start.4) | collective-permute-done | bytes 196640 | tf_op jit(solution)/shard_map/x_sum/ppermute | solution.py:361
  48.2 14.2 %all_to_all.16.joint_ref = bf16[32,8,640]{2,1,0:T(8,128)(2,1)S(1)} all-to-all(bf16[32,8,640]{2,1,0:T(8,128)(2,1)S(1)} %x_sum.1), channel_id=1, replica_groups=mesh['y'=4,'z'=8,'x'=4,'c'=2] {'y','z'}, dimensions={0} | all-to-all | bytes 655360 | tf_op jit(solution)/shard_map/yz_sum/all_to_all | solution.py:434
  62.4 16.7 %all_to_all.17 = bf16[32,8,384]{2,1,0:T(8,128)(2,1)S(1)} all-to-all(bf16[32,8,384]{2,1,0:T(8,128)(2,1)S(1)} %yz_sum.1), channel_id=1, replica_groups=mesh['y'=4,'z'=8,'x'=4,'c'=2] {'y','z'}, dimensions={0} | all-to-all | bytes 393216 | tf_op jit(solution)/shard_map/yz_gather/all_to_all | solution.py:437
  79.1 3.0 %collective-permute-start.10 = (bf16[256,384]{1,0:T(8,128)(2,1)S(1)}, bf16[256,384]{1,0:T(8,128)(2,1)S(1)}, u32[]{:S(2)}, u32[]{:S(2)}) collective-permute-start(bf16[256,384]{1,0:T(8,128)(2,1)S(1)} %bitcast.10), channel_id=1, source_target_pairs={{0,1},{1,0},{2,3},{3,2},{4,5},{5,4},{6,7},{7,6},{8,9},{9,8},{10,11... | collective-permute-start | bytes 589832 | tf_op jit(solution)/shard_map/x_gather/ppermute | solution.py:361
  82.1 1.3 %collective-permute-start.7 = (bf16[256,384]{1,0:T(8,128)(2,1)S(1)}, bf16[256,384]{1,0:T(8,128)(2,1)S(1)}, u32[]{:S(2)}, u32[]{:S(2)}) collective-permute-start(bf16[256,384]{1,0:T(8,128)(2,1)S(1)} %bitcast.11), channel_id=1, source_target_pairs={{0,2},{2,4},{4,6},{6,0},{1,3},{3,5},{5,7},{7,1},{8,10},{10,12},{12... | collective-permute-start | bytes 589832 | tf_op jit(solution)/shard_map/x_gather/ppermute | solution.py:361
  83.4 2.0 %collective-permute-start.8 = (bf16[256,384]{1,0:T(8,128)(2,1)S(1)}, bf16[256,384]{1,0:T(8,128)(2,1)S(1)}, u32[]{:S(2)}, u32[]{:S(2)}) collective-permute-start(bf16[256,384]{1,0:T(8,128)(2,1)S(1)} %bitcast.12), channel_id=1, source_target_pairs={{0,4},{2,6},{4,0},{6,2},{1,5},{3,7},{5,1},{7,3},{8,12},{10,14},{12... | collective-permute-start | bytes 589832 | tf_op jit(solution)/shard_map/x_gather/ppermute | solution.py:361
  85.4 0.4 collective-permute-start.9
  85.8 1.0 expand.1
  86.7 0.9 spread.3
  87.7 2.2 %collective-permute-done.7.refs_1_ = bf16[256,384]{1,0:T(8,128)(2,1)S(1)} collective-permute-done((bf16[256,384]{1,0:T(8,128)(2,1)S(1)}, bf16[256,384]{1,0:T(8,128)(2,1)S(1)}, u32[]{:S(2)}, u32[]{:S(2)}) %collective-permute-start.7) | collective-permute-done | bytes 196640 | tf_op jit(solution)/shard_map/x_gather/ppermute | solution.py:361
  89.8 4.8 %collective-permute-done.8.refs_0_ = bf16[256,384]{1,0:T(8,128)(2,1)S(1)} collective-permute-done((bf16[256,384]{1,0:T(8,128)(2,1)S(1)}, bf16[256,384]{1,0:T(8,128)(2,1)S(1)}, u32[]{:S(2)}, u32[]{:S(2)}) %collective-permute-start.8) | collective-permute-done | bytes 196640 | tf_op jit(solution)/shard_map/x_gather/ppermute | solution.py:361
  94.7 0.8 collective-permute-start.11
  95.5 0.5 collective-permute-start.13
  96.0 1.1 %spread.4 = (f32[256,768]{1,0:T(8,128)}, f32[256,256]{1,0:T(8,128)}, f32[256,1024]{1,0:T(8,128)}, f32[1024,256]{1,0:T(8,128)}) custom-call(bf16[256,384]{1,0:T(8,128)(2,1)S(1)} %collective-permute-done.8.refs_0_, bf16[256,384]{1,0:T(8,128)(2,1)S(1)} %collective-permute-done.7.refs_1_, ...), custom_call_target="tpu_custom_call", output_to_operand_aliasing={{0}: (3, {}), {1}: (4, {}), {2}: (5, {}), {3}: (6, {})} | custom-call | bytes 2000000 | tf_op jit(solution)/shard_map/spread/pallas_call | solution.py:318
  97.2 1.1 %spread.5 = (f32[256,768]{1,0:T(8,128)}, f32[256,256]{1,0:T(8,128)}, f32[256,1024]{1,0:T(8,128)}, f32[1024,256]{1,0:T(8,128)}) custom-call(bf16[256,384]{1,0:T(8,128)(2,1)S(1)} %collective-permute-done.11.refs_0_, bf16[256,384]{1,0:T(8,128)(2,1)S(1)} %collective-permute-done.12.refs_1_, ...), custom_call_target="tpu_custom_call", output_to_operand_aliasing={{0}: (3, {}), {1}: (4, {}), {2}: (5, {}), {3}: (6, {})} | custom-call | bytes 2000000 | tf_op jit(solution)/shard_map/spread/pallas_call | solution.py:318
  (18 shorter events, 1.1 us)
Async XLA Ops:
  30.6 4.9 %collective-permute-start.5 = (bf16[256,384]{1,0:T(8,128)(2,1)S(1)}, bf16[256,384]{1,0:T(8,128)(2,1)S(1)}, u32[]{:S(2)}, u32[]{:S(2)}) collective-permute-start(bf16[256,384]{1,0:T(8,128)(2,1)S(1)} %get-tuple-element.45), channel_id=1, source_target_pairs={{0,1},{1,0},{2,3},{3,2},{4,5},{5,4},{6,7},{7,6},{8,9},{9,8},{10,11... | collective-permute-start | bytes 589832 | tf_op jit(solution)/shard_map/core_sum/ppermute | solution.py:361
  34.4 4.0 %collective-permute-start.3 = (bf16[256,384]{1,0:T(8,128)(2,1)S(1)}, bf16[256,384]{1,0:T(8,128)(2,1)S(1)}, u32[]{:S(2)}, u32[]{:S(2)}) collective-permute-start(bf16[256,384]{1,0:T(8,128)(2,1)S(1)} %get-tuple-element.43), channel_id=1, source_target_pairs={{0,1},{1,0},{2,3},{3,2},{4,5},{5,4},{6,7},{7,6},{8,9},{9,8},{10,11... | collective-permute-start | bytes 589832 | tf_op jit(solution)/shard_map/core_sum/ppermute | solution.py:361
  34.5 4.3 %collective-permute-start.1 = (bf16[256,384]{1,0:T(8,128)(2,1)S(1)}, bf16[256,384]{1,0:T(8,128)(2,1)S(1)}, u32[]{:S(2)}, u32[]{:S(2)}) collective-permute-start(bf16[256,384]{1,0:T(8,128)(2,1)S(1)} %get-tuple-element.41), channel_id=1, source_target_pairs={{0,1},{1,0},{2,3},{3,2},{4,5},{5,4},{6,7},{7,6},{8,9},{9,8},{10,11... | collective-permute-start | bytes 589832 | tf_op jit(solution)/shard_map/core_sum/ppermute | solution.py:361
  34.9 6.4 %collective-permute-start = (bf16[256,384]{1,0:T(8,128)(2,1)S(1)}, bf16[256,384]{1,0:T(8,128)(2,1)S(1)}, u32[]{:S(2)}, u32[]{:S(2)}) collective-permute-start(bf16[256,384]{1,0:T(8,128)(2,1)S(1)} %get-tuple-element.39), channel_id=1, source_target_pairs={{0,1},{1,0},{2,3},{3,2},{4,5},{5,4},{6,7},{7,6},{8,9},{9,8},{10,11... | collective-permute-start | bytes 589832 | tf_op jit(solution)/shard_map/core_sum/ppermute | solution.py:361
  35.5 7.7 %collective-permute-start.6 = (bf16[256,384]{1,0:T(8,128)(2,1)S(1)}, bf16[256,384]{1,0:T(8,128)(2,1)S(1)}, u32[]{:S(2)}, u32[]{:S(2)}) collective-permute-start(bf16[256,384]{1,0:T(8,128)(2,1)S(1)} %core_sum.5), channel_id=1, source_target_pairs={{0,4},{2,6},{4,0},{6,2},{1,5},{3,7},{5,1},{7,3},{8,12},{10,14},{12... | collective-permute-start | bytes 589832 | tf_op jit(solution)/shard_map/x_sum/ppermute | solution.py:361
  38.4 9.7 %collective-permute-start.4 = (bf16[256,384]{1,0:T(8,128)(2,1)S(1)}, bf16[256,384]{1,0:T(8,128)(2,1)S(1)}, u32[]{:S(2)}, u32[]{:S(2)}) collective-permute-start(bf16[256,384]{1,0:T(8,128)(2,1)S(1)} %core_sum.4), channel_id=1, source_target_pairs={{0,2},{2,4},{4,6},{6,0},{1,3},{3,5},{5,7},{7,1},{8,10},{10,12},{12... | collective-permute-start | bytes 589832 | tf_op jit(solution)/shard_map/x_sum/ppermute | solution.py:361
  38.9 9.2 %collective-permute-start.2 = (bf16[256,384]{1,0:T(8,128)(2,1)S(1)}, bf16[256,384]{1,0:T(8,128)(2,1)S(1)}, u32[]{:S(2)}, u32[]{:S(2)}) collective-permute-start(bf16[256,384]{1,0:T(8,128)(2,1)S(1)} %core_sum.3), channel_id=1, source_target_pairs={{0,6},{2,0},{4,2},{6,4},{1,7},{3,1},{5,3},{7,5},{8,14},{10,8},{12,... | collective-permute-start | bytes 589832 | tf_op jit(solution)/shard_map/x_sum/ppermute | solution.py:361
  79.1 7.6 %collective-permute-start.10 = (bf16[256,384]{1,0:T(8,128)(2,1)S(1)}, bf16[256,384]{1,0:T(8,128)(2,1)S(1)}, u32[]{:S(2)}, u32[]{:S(2)}) collective-permute-start(bf16[256,384]{1,0:T(8,128)(2,1)S(1)} %bitcast.10), channel_id=1, source_target_pairs={{0,1},{1,0},{2,3},{3,2},{4,5},{5,4},{6,7},{7,6},{8,9},{9,8},{10,11... | collective-permute-start | bytes 589832 | tf_op jit(solution)/shard_map/x_gather/ppermute | solution.py:361
  82.1 7.7 %collective-permute-start.7 = (bf16[256,384]{1,0:T(8,128)(2,1)S(1)}, bf16[256,384]{1,0:T(8,128)(2,1)S(1)}, u32[]{:S(2)}, u32[]{:S(2)}) collective-permute-start(bf16[256,384]{1,0:T(8,128)(2,1)S(1)} %bitcast.11), channel_id=1, source_target_pairs={{0,2},{2,4},{4,6},{6,0},{1,3},{3,5},{5,7},{7,1},{8,10},{10,12},{12... | collective-permute-start | bytes 589832 | tf_op jit(solution)/shard_map/x_gather/ppermute | solution.py:361
  83.4 11.3 %collective-permute-start.8 = (bf16[256,384]{1,0:T(8,128)(2,1)S(1)}, bf16[256,384]{1,0:T(8,128)(2,1)S(1)}, u32[]{:S(2)}, u32[]{:S(2)}) collective-permute-start(bf16[256,384]{1,0:T(8,128)(2,1)S(1)} %bitcast.12), channel_id=1, source_target_pairs={{0,4},{2,6},{4,0},{6,2},{1,5},{3,7},{5,1},{7,3},{8,12},{10,14},{12... | collective-permute-start | bytes 589832 | tf_op jit(solution)/shard_map/x_gather/ppermute | solution.py:361
  85.4 9.3 %collective-permute-start.9 = (bf16[256,384]{1,0:T(8,128)(2,1)S(1)}, bf16[256,384]{1,0:T(8,128)(2,1)S(1)}, u32[]{:S(2)}, u32[]{:S(2)}) collective-permute-start(bf16[256,384]{1,0:T(8,128)(2,1)S(1)} %bitcast.13), channel_id=1, source_target_pairs={{0,6},{2,0},{4,2},{6,4},{1,7},{3,1},{5,3},{7,5},{8,14},{10,8},{12,... | collective-permute-start | bytes 589832 | tf_op jit(solution)/shard_map/x_gather/ppermute | solution.py:361
  94.7 2.4 %collective-permute-start.11 = (bf16[256,384]{1,0:T(8,128)(2,1)S(1)}, bf16[256,384]{1,0:T(8,128)(2,1)S(1)}, u32[]{:S(2)}, u32[]{:S(2)}) collective-permute-start(bf16[256,384]{1,0:T(8,128)(2,1)S(1)} %collective-permute-done.8.refs_0_), channel_id=1, source_target_pairs={{0,1},{1,0},{2,3},{3,2},{4,5},{5,4},{6,7},{7,6},{8,9},{9,8},{10,11... | collective-permute-start | bytes 589832 | tf_op jit(solution)/shard_map/core_gather/ppermute | solution.py:361
  95.4 1.6 %collective-permute-start.12 = (bf16[256,384]{1,0:T(8,128)(2,1)S(1)}, bf16[256,384]{1,0:T(8,128)(2,1)S(1)}, u32[]{:S(2)}, u32[]{:S(2)}) collective-permute-start(bf16[256,384]{1,0:T(8,128)(2,1)S(1)} %collective-permute-done.7.refs_1_), channel_id=1, source_target_pairs={{0,1},{1,0},{2,3},{3,2},{4,5},{5,4},{6,7},{7,6},{8,9},{9,8},{10,11... | collective-permute-start | bytes 589832 | tf_op jit(solution)/shard_map/core_gather/ppermute | solution.py:361
  95.5 1.7 %collective-permute-start.13 = (bf16[256,384]{1,0:T(8,128)(2,1)S(1)}, bf16[256,384]{1,0:T(8,128)(2,1)S(1)}, u32[]{:S(2)}, u32[]{:S(2)}) collective-permute-start(bf16[256,384]{1,0:T(8,128)(2,1)S(1)} %collective-permute-done.9.refs_2_), channel_id=1, source_target_pairs={{0,1},{1,0},{2,3},{3,2},{4,5},{5,4},{6,7},{7,6},{8,9},{9,8},{10,11... | collective-permute-start | bytes 589832 | tf_op jit(solution)/shard_map/core_gather/ppermute | solution.py:361

commit v8 on v7

--- a/solution.py
+++ b/solution.py
@@ -10,7 +10,7 @@
 
 HEADS = 16
 BATCH = 16
-CAP = 4
+ORDER = (2, 1, 3)
 EPS = 1e-05
 GELU_C = 0.7978845608028654
 GELU_A = 0.044715
@@ -438,7 +438,7 @@
         part = part.reshape(256, 384)
         joint, _ = lax.optimization_barrier((joint, part))
     with jax.named_scope("x_gather"):
-        near = {by: shift(part, "x", 4, by) for by in (2, 1, 3)}
+        near = [shift(part, "x", 4, by) for by in ORDER]
         part_far = shift(part, "c", 2, 1)
     with jax.named_scope("expand"):
         feature_grad = run(
@@ -448,10 +448,10 @@
         outs = spread(((0, 0), (0, 1)), (part, part_far))
     with jax.named_scope("core_gather"):
         near, feature_grad, outs = lax.optimization_barrier((near, feature_grad, outs))
-        far = {by: shift(near[by], "c", 2, 1) for by in (2, 1, 3)}
+        far = [shift(got, "c", 2, 1) for got in near]
     with jax.named_scope("spread"):
-        outs = spread(((2, 0), (1, 0), (3, 0)), [near[by] for by in (2, 1, 3)], outs)
-        outs = spread(((2, 1), (1, 1), (3, 1)), [far[by] for by in (2, 1, 3)], outs)
+        outs = spread([(by, 0) for by in ORDER], near, outs)
+        outs = spread([(by, 1) for by in ORDER], far, outs)
     return (feature_grad.reshape(features.shape), *outs)
 
 

time: 98.6 us -> 98.3 us (level)
  no operation moved by 1% of the time
where the time goes in v8:
time: 98.3 us; the launch traced here: 98.1 us
  blocking collectives  52.4 us (53%)
  starting transfers between devices  18 us (18%)
  waiting for transfers between devices  14.1 us (14%)
  Pallas kernels  12.8 us (13%)
    all_to_all x1, blocking collectives, per_device(): lax.all_to_all(send.reshape(32, 16, width), dates, split_axis=0, concat_a...  21.5 us
    ppermute x14, starting transfers between devices, shift(): lax.ppermute(array, axis, [(at, (at + by) % size) for at in range(size)])  18 us
    all_to_all x1, blocking collectives, per_device(): part = lax.all_to_all(total, dates, split_axis=0, concat_axis=0, tiled=True)  16.7 us
    all_to_all x1, blocking collectives, per_device(): lax.all_to_all(joint, dates, split_axis=0, concat_axis=0, tiled=True)  14.2 us
    ppermute x14, waiting for transfers between devices, shift(): lax.ppermute(array, axis, [(at, (at + by) % size) for at in range(size)])  14.1 us
    pallas_call x8, Pallas kernels, run(): pl.pallas_call(kernel, out_shape=out_shape, in_specs=specs, scratch_shape...  9.7 us
    pallas_call x3, Pallas kernels, spread(): pl.pallas_call(functools.partial(spread_kernel, pieces), out_shape=(shape...  3.06 us
  transfers between devices with their start and end apart: 14, of which 6 were waited for; matrix products, arithmetic and copies ran while one was open for 0% of the time, Pallas kernels for 3%

profile of v8, /device:TPU:1, one launch (start us, length us, event | category | flops | bytes accessed | tf_op | source)
XLA Modules:
  0.0 98.1 jit_solution(12193187816618474378)
XLA Ops:
  0.6 1.4 %compact.1 = (bf16[512,256]{1,0:T(8,128)(2,1)S(1)}, bf16[2,128,256]{2,1,0:T(8,128)(2,1)S(1)}) custom-call(bf16[512,256]{1,0:T(8,128)(2,1)} %bitcast.16, bf16[512,256]{1,0:T(8,128)(2,1)} %bitcast.17, s32[8,32]{1,0:T(8,128)} %bitcast.19), custom_call_target="tpu_custom_call" | custom-call | tf_op jit(solution)/shard_map/compact/pallas_call | solution.py:349
  2.0 21.5 %all_to_all.15 = bf16[32,16,256]{2,1,0:T(8,128)(2,1)S(1)} all-to-all(bf16[32,16,256]{2,1,0:T(8,128)(2,1)S(1)} %bitcast.15), channel_id=1, replica_groups=mesh['y'=4,'z'=8,'x'=4,'c'=2] {'y','z'}, dimensions={0} | all-to-all | bytes 524288 | tf_op jit(solution)/shard_map/to_owner/all_to_all | solution.py:395
  23.5 7.0 %layer.1 = (bf16[256,256]{1,0:T(8,128)(2,1)S(1)}, bf16[256,384]{1,0:T(8,128)(2,1)S(1)}, bf16[256,384]{1,0:T(8,128)(2,1)S(1)}, bf16[256,384]{1,0:T(8,128)(2,1)S(1...) custom-call(bf16[512,256]{1,0:T(8,128)(2,1)S(1)} %bitcast.9, ...), custom_call_target="tpu_custom_call" | custom-call | tf_op jit(solution)/shard_map/layer/pallas_call | solution.py:349
  30.6 3.8 %collective-permute-start.5 = (bf16[256,384]{1,0:T(8,128)(2,1)S(1)}, bf16[256,384]{1,0:T(8,128)(2,1)S(1)}, u32[]{:S(2)}, u32[]{:S(2)}) collective-permute-start(bf16[256,384]{1,0:T(8,128)(2,1)S(1)} %get-tuple-element.45), channel_id=1, source_target_pairs={{0,1},{1,0},{2,3},{3,2},{4,5},{5,4},{6,7},{7,6},{8,9},{9,8},{10,11... | collective-permute-start | bytes 589832 | tf_op jit(solution)/shard_map/core_sum/ppermute | solution.py:361
  34.5 0.4 collective-permute-start.1
  35.0 0.5 collective-permute-done.5.other_ref
  35.5 2.8 %collective-permute-start.6 = (bf16[256,384]{1,0:T(8,128)(2,1)S(1)}, bf16[256,384]{1,0:T(8,128)(2,1)S(1)}, u32[]{:S(2)}, u32[]{:S(2)}) collective-permute-start(bf16[256,384]{1,0:T(8,128)(2,1)S(1)} %core_sum.5), channel_id=1, source_target_pairs={{0,4},{2,6},{4,0},{6,2},{1,5},{3,7},{5,1},{7,3},{8,12},{10,14},{12... | collective-permute-start | bytes 589832 | tf_op jit(solution)/shard_map/x_sum/ppermute | solution.py:361
  38.9 2.4 %collective-permute-start.2 = (bf16[256,384]{1,0:T(8,128)(2,1)S(1)}, bf16[256,384]{1,0:T(8,128)(2,1)S(1)}, u32[]{:S(2)}, u32[]{:S(2)}) collective-permute-start(bf16[256,384]{1,0:T(8,128)(2,1)S(1)} %core_sum.3), channel_id=1, source_target_pairs={{0,6},{2,0},{4,2},{6,4},{1,7},{3,1},{5,3},{7,5},{8,14},{10,8},{12,... | collective-permute-start | bytes 589832 | tf_op jit(solution)/shard_map/x_sum/ppermute | solution.py:361
  41.3 1.9 %collective-permute-done.6.three_ref = bf16[256,384]{1,0:T(8,128)(2,1)S(1)} collective-permute-done((bf16[256,384]{1,0:T(8,128)(2,1)S(1)}, bf16[256,384]{1,0:T(8,128)(2,1)S(1)}, u32[]{:S(2)}, u32[]{:S(2)}) %collective-permute-start.6) | collective-permute-done | bytes 196640 | tf_op jit(solution)/shard_map/x_sum/ppermute | solution.py:361
  43.2 4.9 %collective-permute-done.4.two_ref = bf16[256,384]{1,0:T(8,128)(2,1)S(1)} collective-permute-done((bf16[256,384]{1,0:T(8,128)(2,1)S(1)}, bf16[256,384]{1,0:T(8,128)(2,1)S(1)}, u32[]{:S(2)}, u32[]{:S(2)}) %collective-permute-start.4) | collective-permute-done | bytes 196640 | tf_op jit(solution)/shard_map/x_sum/ppermute | solution.py:361
  48.2 14.2 %all_to_all.16.joint_ref = bf16[32,8,640]{2,1,0:T(8,128)(2,1)S(1)} all-to-all(bf16[32,8,640]{2,1,0:T(8,128)(2,1)S(1)} %x_sum.1), channel_id=1, replica_groups=mesh['y'=4,'z'=8,'x'=4,'c'=2] {'y','z'}, dimensions={0} | all-to-all | bytes 655360 | tf_op jit(solution)/shard_map/yz_sum/all_to_all | solution.py:434
  62.4 16.7 %all_to_all.17 = bf16[32,8,384]{2,1,0:T(8,128)(2,1)S(1)} all-to-all(bf16[32,8,384]{2,1,0:T(8,128)(2,1)S(1)} %yz_sum.1), channel_id=1, replica_groups=mesh['y'=4,'z'=8,'x'=4,'c'=2] {'y','z'}, dimensions={0} | all-to-all | bytes 393216 | tf_op jit(solution)/shard_map/yz_gather/all_to_all | solution.py:437
  79.1 3.0 %collective-permute-start.10 = (bf16[256,384]{1,0:T(8,128)(2,1)S(1)}, bf16[256,384]{1,0:T(8,128)(2,1)S(1)}, u32[]{:S(2)}, u32[]{:S(2)}) collective-permute-start(bf16[256,384]{1,0:T(8,128)(2,1)S(1)} %bitcast.10), channel_id=1, source_target_pairs={{0,1},{1,0},{2,3},{3,2},{4,5},{5,4},{6,7},{7,6},{8,9},{9,8},{10,11... | collective-permute-start | bytes 589832 | tf_op jit(solution)/shard_map/x_gather/ppermute | solution.py:361
  82.1 1.3 %collective-permute-start.7 = (bf16[256,384]{1,0:T(8,128)(2,1)S(1)}, bf16[256,384]{1,0:T(8,128)(2,1)S(1)}, u32[]{:S(2)}, u32[]{:S(2)}) collective-permute-start(bf16[256,384]{1,0:T(8,128)(2,1)S(1)} %bitcast.11), channel_id=1, source_target_pairs={{0,4},{2,6},{4,0},{6,2},{1,5},{3,7},{5,1},{7,3},{8,12},{10,14},{12... | collective-permute-start | bytes 589832 | tf_op jit(solution)/shard_map/x_gather/ppermute | solution.py:361
  83.4 1.4 %collective-permute-start.8 = (bf16[256,384]{1,0:T(8,128)(2,1)S(1)}, bf16[256,384]{1,0:T(8,128)(2,1)S(1)}, u32[]{:S(2)}, u32[]{:S(2)}) collective-permute-start(bf16[256,384]{1,0:T(8,128)(2,1)S(1)} %bitcast.12), channel_id=1, source_target_pairs={{0,2},{2,4},{4,6},{6,0},{1,3},{3,5},{5,7},{7,1},{8,10},{10,12},{12... | collective-permute-start | bytes 589832 | tf_op jit(solution)/shard_map/x_gather/ppermute | solution.py:361
  84.8 1.3 %collective-permute-start.9 = (bf16[256,384]{1,0:T(8,128)(2,1)S(1)}, bf16[256,384]{1,0:T(8,128)(2,1)S(1)}, u32[]{:S(2)}, u32[]{:S(2)}) collective-permute-start(bf16[256,384]{1,0:T(8,128)(2,1)S(1)} %bitcast.13), channel_id=1, source_target_pairs={{0,6},{2,0},{4,2},{6,4},{1,7},{3,1},{5,3},{7,5},{8,14},{10,8},{12,... | collective-permute-start | bytes 589832 | tf_op jit(solution)/shard_map/x_gather/ppermute | solution.py:361
  86.0 1.0 expand.1
  87.0 0.9 spread.3
  87.9 2.2 %collective-permute-done.7.refs_0_ = bf16[256,384]{1,0:T(8,128)(2,1)S(1)} collective-permute-done((bf16[256,384]{1,0:T(8,128)(2,1)S(1)}, bf16[256,384]{1,0:T(8,128)(2,1)S(1)}, u32[]{:S(2)}, u32[]{:S(2)}) %collective-permute-start.7) | collective-permute-done | bytes 196640 | tf_op jit(solution)/shard_map/x_gather/ppermute | solution.py:361
  90.2 4.5 %collective-permute-done.8.refs_1_ = bf16[256,384]{1,0:T(8,128)(2,1)S(1)} collective-permute-done((bf16[256,384]{1,0:T(8,128)(2,1)S(1)}, bf16[256,384]{1,0:T(8,128)(2,1)S(1)}, u32[]{:S(2)}, u32[]{:S(2)}) %collective-permute-start.8) | collective-permute-done | bytes 196640 | tf_op jit(solution)/shard_map/x_gather/ppermute | solution.py:361
  94.7 0.5 collective-permute-start.11
  95.2 0.5 collective-permute-start.13
  95.6 1.1 %spread.4 = (f32[256,768]{1,0:T(8,128)}, f32[256,256]{1,0:T(8,128)}, f32[256,1024]{1,0:T(8,128)}, f32[1024,256]{1,0:T(8,128)}) custom-call(bf16[256,384]{1,0:T(8,128)(2,1)S(1)} %collective-permute-done.7.refs_0_, bf16[256,384]{1,0:T(8,128)(2,1)S(1)} %collective-permute-done.8.refs_1_, ...), custom_call_target="tpu_custom_call", output_to_operand_aliasing={{0}: (3, {}), {1}: (4, {}), {2}: (5, {}), {3}: (6, {})} | custom-call | bytes 2000000 | tf_op jit(solution)/shard_map/spread/pallas_call | solution.py:318
  96.8 1.1 %spread.5 = (f32[256,768]{1,0:T(8,128)}, f32[256,256]{1,0:T(8,128)}, f32[256,1024]{1,0:T(8,128)}, f32[1024,256]{1,0:T(8,128)}) custom-call(bf16[256,384]{1,0:T(8,128)(2,1)S(1)} %collective-permute-done.11.refs_0_, bf16[256,384]{1,0:T(8,128)(2,1)S(1)} %collective-permute-done.12.refs_1_, ...), custom_call_target="tpu_custom_call", output_to_operand_aliasing={{0}: (3, {}), {1}: (4, {}), {2}: (5, {}), {3}: (6, {})} | custom-call | bytes 2000000 | tf_op jit(solution)/shard_map/spread/pallas_call | solution.py:318
  (18 shorter events, 1.1 us)
Async XLA Ops:
  30.6 4.9 %collective-permute-start.5 = (bf16[256,384]{1,0:T(8,128)(2,1)S(1)}, bf16[256,384]{1,0:T(8,128)(2,1)S(1)}, u32[]{:S(2)}, u32[]{:S(2)}) collective-permute-start(bf16[256,384]{1,0:T(8,128)(2,1)S(1)} %get-tuple-element.45), channel_id=1, source_target_pairs={{0,1},{1,0},{2,3},{3,2},{4,5},{5,4},{6,7},{7,6},{8,9},{9,8},{10,11... | collective-permute-start | bytes 589832 | tf_op jit(solution)/shard_map/core_sum/ppermute | solution.py:361
  34.4 4.0 %collective-permute-start.3 = (bf16[256,384]{1,0:T(8,128)(2,1)S(1)}, bf16[256,384]{1,0:T(8,128)(2,1)S(1)}, u32[]{:S(2)}, u32[]{:S(2)}) collective-permute-start(bf16[256,384]{1,0:T(8,128)(2,1)S(1)} %get-tuple-element.43), channel_id=1, source_target_pairs={{0,1},{1,0},{2,3},{3,2},{4,5},{5,4},{6,7},{7,6},{8,9},{9,8},{10,11... | collective-permute-start | bytes 589832 | tf_op jit(solution)/shard_map/core_sum/ppermute | solution.py:361
  34.5 4.3 %collective-permute-start.1 = (bf16[256,384]{1,0:T(8,128)(2,1)S(1)}, bf16[256,384]{1,0:T(8,128)(2,1)S(1)}, u32[]{:S(2)}, u32[]{:S(2)}) collective-permute-start(bf16[256,384]{1,0:T(8,128)(2,1)S(1)} %get-tuple-element.41), channel_id=1, source_target_pairs={{0,1},{1,0},{2,3},{3,2},{4,5},{5,4},{6,7},{7,6},{8,9},{9,8},{10,11... | collective-permute-start | bytes 589832 | tf_op jit(solution)/shard_map/core_sum/ppermute | solution.py:361
  34.9 6.4 %collective-permute-start = (bf16[256,384]{1,0:T(8,128)(2,1)S(1)}, bf16[256,384]{1,0:T(8,128)(2,1)S(1)}, u32[]{:S(2)}, u32[]{:S(2)}) collective-permute-start(bf16[256,384]{1,0:T(8,128)(2,1)S(1)} %get-tuple-element.39), channel_id=1, source_target_pairs={{0,1},{1,0},{2,3},{3,2},{4,5},{5,4},{6,7},{7,6},{8,9},{9,8},{10,11... | collective-permute-start | bytes 589832 | tf_op jit(solution)/shard_map/core_sum/ppermute | solution.py:361
  35.5 7.7 %collective-permute-start.6 = (bf16[256,384]{1,0:T(8,128)(2,1)S(1)}, bf16[256,384]{1,0:T(8,128)(2,1)S(1)}, u32[]{:S(2)}, u32[]{:S(2)}) collective-permute-start(bf16[256,384]{1,0:T(8,128)(2,1)S(1)} %core_sum.5), channel_id=1, source_target_pairs={{0,4},{2,6},{4,0},{6,2},{1,5},{3,7},{5,1},{7,3},{8,12},{10,14},{12... | collective-permute-start | bytes 589832 | tf_op jit(solution)/shard_map/x_sum/ppermute | solution.py:361
  38.4 9.7 %collective-permute-start.4 = (bf16[256,384]{1,0:T(8,128)(2,1)S(1)}, bf16[256,384]{1,0:T(8,128)(2,1)S(1)}, u32[]{:S(2)}, u32[]{:S(2)}) collective-permute-start(bf16[256,384]{1,0:T(8,128)(2,1)S(1)} %core_sum.4), channel_id=1, source_target_pairs={{0,2},{2,4},{4,6},{6,0},{1,3},{3,5},{5,7},{7,1},{8,10},{10,12},{12... | collective-permute-start | bytes 589832 | tf_op jit(solution)/shard_map/x_sum/ppermute | solution.py:361
  38.9 9.2 %collective-permute-start.2 = (bf16[256,384]{1,0:T(8,128)(2,1)S(1)}, bf16[256,384]{1,0:T(8,128)(2,1)S(1)}, u32[]{:S(2)}, u32[]{:S(2)}) collective-permute-start(bf16[256,384]{1,0:T(8,128)(2,1)S(1)} %core_sum.3), channel_id=1, source_target_pairs={{0,6},{2,0},{4,2},{6,4},{1,7},{3,1},{5,3},{7,5},{8,14},{10,8},{12,... | collective-permute-start | bytes 589832 | tf_op jit(solution)/shard_map/x_sum/ppermute | solution.py:361
  79.1 7.9 %collective-permute-start.10 = (bf16[256,384]{1,0:T(8,128)(2,1)S(1)}, bf16[256,384]{1,0:T(8,128)(2,1)S(1)}, u32[]{:S(2)}, u32[]{:S(2)}) collective-permute-start(bf16[256,384]{1,0:T(8,128)(2,1)S(1)} %bitcast.10), channel_id=1, source_target_pairs={{0,1},{1,0},{2,3},{3,2},{4,5},{5,4},{6,7},{7,6},{8,9},{9,8},{10,11... | collective-permute-start | bytes 589832 | tf_op jit(solution)/shard_map/x_gather/ppermute | solution.py:361
  82.1 8.1 %collective-permute-start.7 = (bf16[256,384]{1,0:T(8,128)(2,1)S(1)}, bf16[256,384]{1,0:T(8,128)(2,1)S(1)}, u32[]{:S(2)}, u32[]{:S(2)}) collective-permute-start(bf16[256,384]{1,0:T(8,128)(2,1)S(1)} %bitcast.11), channel_id=1, source_target_pairs={{0,4},{2,6},{4,0},{6,2},{1,5},{3,7},{5,1},{7,3},{8,12},{10,14},{12... | collective-permute-start | bytes 589832 | tf_op jit(solution)/shard_map/x_gather/ppermute | solution.py:361
  83.4 11.3 %collective-permute-start.8 = (bf16[256,384]{1,0:T(8,128)(2,1)S(1)}, bf16[256,384]{1,0:T(8,128)(2,1)S(1)}, u32[]{:S(2)}, u32[]{:S(2)}) collective-permute-start(bf16[256,384]{1,0:T(8,128)(2,1)S(1)} %bitcast.12), channel_id=1, source_target_pairs={{0,2},{2,4},{4,6},{6,0},{1,3},{3,5},{5,7},{7,1},{8,10},{10,12},{12... | collective-permute-start | bytes 589832 | tf_op jit(solution)/shard_map/x_gather/ppermute | solution.py:361
  84.8 9.9 %collective-permute-start.9 = (bf16[256,384]{1,0:T(8,128)(2,1)S(1)}, bf16[256,384]{1,0:T(8,128)(2,1)S(1)}, u32[]{:S(2)}, u32[]{:S(2)}) collective-permute-start(bf16[256,384]{1,0:T(8,128)(2,1)S(1)} %bitcast.13), channel_id=1, source_target_pairs={{0,6},{2,0},{4,2},{6,4},{1,7},{3,1},{5,3},{7,5},{8,14},{10,8},{12,... | collective-permute-start | bytes 589832 | tf_op jit(solution)/shard_map/x_gather/ppermute | solution.py:361
  94.7 2.1 %collective-permute-start.11 = (bf16[256,384]{1,0:T(8,128)(2,1)S(1)}, bf16[256,384]{1,0:T(8,128)(2,1)S(1)}, u32[]{:S(2)}, u32[]{:S(2)}) collective-permute-start(bf16[256,384]{1,0:T(8,128)(2,1)S(1)} %collective-permute-done.7.refs_0_), channel_id=1, source_target_pairs={{0,1},{1,0},{2,3},{3,2},{4,5},{5,4},{6,7},{7,6},{8,9},{9,8},{10,11... | collective-permute-start | bytes 589832 | tf_op jit(solution)/shard_map/core_gather/ppermute | solution.py:361
  95.1 1.6 %collective-permute-start.12 = (bf16[256,384]{1,0:T(8,128)(2,1)S(1)}, bf16[256,384]{1,0:T(8,128)(2,1)S(1)}, u32[]{:S(2)}, u32[]{:S(2)}) collective-permute-start(bf16[256,384]{1,0:T(8,128)(2,1)S(1)} %collective-permute-done.8.refs_1_), channel_id=1, source_target_pairs={{0,1},{1,0},{2,3},{3,2},{4,5},{5,4},{6,7},{7,6},{8,9},{9,8},{10,11... | collective-permute-start | bytes 589832 | tf_op jit(solution)/shard_map/core_gather/ppermute | solution.py:361
  95.2 1.7 %collective-permute-start.13 = (bf16[256,384]{1,0:T(8,128)(2,1)S(1)}, bf16[256,384]{1,0:T(8,128)(2,1)S(1)}, u32[]{:S(2)}, u32[]{:S(2)}) collective-permute-start(bf16[256,384]{1,0:T(8,128)(2,1)S(1)} %collective-permute-done.9.refs_2_), channel_id=1, source_target_pairs={{0,1},{1,0},{2,3},{3,2},{4,5},{5,4},{6,7},{7,6},{8,9},{9,8},{10,11... | collective-permute-start | bytes 589832 | tf_op jit(solution)/shard_map/core_gather/ppermute | solution.py:361

commit v9 on v6

--- a/solution.py
+++ b/solution.py
@@ -10,7 +10,6 @@
 
 HEADS = 16
 BATCH = 16
-CAP = 4
 EPS = 1e-05
 GELU_C = 0.7978845608028654
 GELU_A = 0.044715
@@ -33,7 +32,7 @@
 NT = ((1,), (1,))
 
 
-def slot_matrix(valid, group, rows_per_block):
+def slot_matrix(valid, group):
     date = iota((8, 256), 1) % 8
     day = iota((8, 256), 0)
     held = valid.astype(F32)
@@ -42,10 +41,10 @@
     own = iota((32, 256), 0) == iota((32, 256), 1) // 16 + group * 16
     keep = jnp.sum(jnp.where(own, keep_all, 0.0), axis=0, keepdims=True)
     rank = jnp.sum(jnp.where(own, rank_all, 0.0), axis=0, keepdims=True)
-    shape = (16 * rows_per_block, 256)
+    shape = (256, 256)
     row, col = iota(shape, 0), iota(shape, 1)
     match = (
-        (row // rows_per_block == col // 16)
+        (row // 16 == col // 16)
         & ((row // 4) % 2 == (col // 8) % 2)
         & (rank == (row % 4).astype(F32))
         & (keep > 0.5)
@@ -53,7 +52,7 @@
     return match.astype(F32)
 
 
-def compact_kernel(feat_hbm, cot_hbm, valid_hbm, send_ref, feat, cot, valid_ref, arrived):
+def compact_kernel(feat_hbm, cot_hbm, valid_hbm, send_ref, match_ref, feat, cot, valid_ref, arrived):
     copies = [
         pltpu.make_async_copy(valid_hbm, valid_ref, arrived.at[0]),
         pltpu.make_async_copy(feat_hbm, feat, arrived.at[1]),
@@ -66,10 +65,11 @@
     is_feat = (iota((256, 1), 0) // 8) % 2 == 0
     picks = []
     for group in range(2):
-        match = slot_matrix(valid, group, 16)
+        match = slot_matrix(valid, group)
         pick_feat = jnp.where(is_feat, match, 0.0).astype(BF16)
         pick_cot = jnp.where(is_feat, 0.0, match).astype(BF16)
         filled = jnp.sum(match, axis=1, keepdims=True) > 0.5
+        match_ref[group] = match.reshape(16, 16, 256)[:, :8].reshape(128, 256).astype(BF16)
         picks.append((pick_feat, pick_cot, is_feat & jnp.logical_not(filled)))
     copies[1].wait()
     copies[2].wait()
@@ -104,20 +104,10 @@
     up_hbm,
     down_hbm,
     grad_ref,
-    terms_ref,
-    gain_first_ref,
-    qkv_ref,
-    out_w_ref,
-    gain_second_ref,
-    up_ref,
-    down_ref,
-    arrived,
-    probs,
-    proj_t,
-    att_t,
-    att_grad_t,
-    proj_grad_t,
+    *rest,
 ):
+    (*sent_refs, gain_first_ref, qkv_ref, out_w_ref, gain_second_ref, up_ref, down_ref) = rest[:14]
+    arrived, probs, proj_t, att_t, att_grad_t, proj_grad_t, terms_ref = rest[14:]
     pairs = (
         (qkv_hbm, qkv_ref),
         (gain_first_hbm, gain_first_ref),
@@ -252,16 +242,17 @@
     slot = iota((256, 256), 0)
     want = slot // 4 % 2 * 128 + slot // 8 * 4 + slot % 4
     grad_ref[...] = dot((iota((256, 256), 1) == want).astype(BF16), grad).astype(BF16)
-
-
-def core_sum_kernel(terms_ref, other_ref, *outs):
-    for slot, out_ref in enumerate(outs):
-        total = terms_ref[0, slot].astype(F32) + other_ref[slot].astype(F32)
-        out_ref[...] = total.astype(BF16)
-
-
-def x_sum_kernel(own_ref, one_ref, two_ref, three_ref, grad_ref, out_ref):
-    total = own_ref[...].astype(F32) + one_ref[...].astype(F32)
+    for at, sent_ref in enumerate(sent_refs):
+        sent_ref[...] = terms_ref[at // 4, at % 4]
+
+
+def core_sum_kernel(mine_ref, other_ref, out_ref):
+    out_ref[...] = (mine_ref[...].astype(F32) + other_ref[...].astype(F32)).astype(BF16)
+
+
+def x_sum_kernel(mine_ref, other_ref, one_ref, two_ref, three_ref, grad_ref, out_ref):
+    total = mine_ref[...].astype(F32) + other_ref[...].astype(F32)
+    total = total + one_ref[...].astype(F32)
     total = total + two_ref[...].astype(F32) + three_ref[...].astype(F32)
     out_ref[:, :, 0:384] = total.astype(BF16).reshape(32, 8, 384)
     out_ref[:, :, 384:640] = grad_ref[...].reshape(32, 8, 256)
@@ -272,15 +263,10 @@
     total_ref[...] = jnp.broadcast_to(total[None], total_ref.shape)
 
 
-def expand_kernel(joint_ref, valid_hbm, out_ref, valid_ref, arrived):
-    copy = pltpu.make_async_copy(valid_hbm, valid_ref, arrived)
-    copy.start()
-    copy.wait()
-    valid = valid_ref[...]
+def expand_kernel(joint_ref, match_ref, out_ref):
     for group in range(2):
-        match = slot_matrix(valid, group, 8).astype(BF16)
         back = joint_ref[group * 16 : group * 16 + 16, :, 384:640].reshape(128, 256)
-        out_ref[pl.ds(group * 256, 256), :] = dot(match, back, TN).astype(BF16)
+        out_ref[pl.ds(group * 256, 256), :] = dot(match_ref[group], back, TN).astype(BF16)
 
 
 def spread_kernel(flip, held_ref, *refs):
@@ -375,9 +361,9 @@
     scale = float(256 * 2 * 256) ** (-0.5)
     dates = ("y", "z")
     with jax.named_scope("compact"):
-        send = run(
+        send, match = run(
             compact_kernel,
-            shape((512, width), BF16),
+            (shape((512, width), BF16), shape((2, 128, 256), BF16)),
             features.reshape(512, width),
             cotangent.reshape(512, width),
             valid_dates.T,
@@ -395,9 +381,9 @@
         )
     piece = shape((256, 384), BF16)
     with jax.named_scope("layer"):
-        grad, terms = run(
+        grad, *terms = run(
             functools.partial(layer_kernel, scale),
-            (shape((256, width), BF16), shape((2, 4, 256, 384), BF16)),
+            (shape((256, width), BF16),) + (piece,) * 8,
             recv.reshape(512, width),
             gain_first.reshape(1, width),
             qkv_weight,
@@ -419,14 +405,15 @@
                 pltpu.VMEM((256, 256), BF16),
                 pltpu.VMEM((256, 256), BF16),
                 pltpu.VMEM((768, 256), BF16),
+                pltpu.VMEM((2, 4, 256, 384), BF16),
             ),
         )
     with jax.named_scope("core_sum"):
-        other = shift(terms[1], "c", 2, 1)
-        slots = run(core_sum_kernel, (piece,) * 4, terms, other)
+        other = {by: shift(terms[4 + by], "c", 2, 1) for by in (3, 1, 2, 0)}
+        slots = {by: run(core_sum_kernel, piece, terms[by], other[by]) for by in (3, 1, 2)}
     with jax.named_scope("x_sum"):
-        got = [shift(slots[by], "x", 4, by) for by in (2, 1, 3)]
-        joint = run(x_sum_kernel, shape((32, 8, 640), BF16), slots[0], *got, grad)
+        got = [shift(slots[by], "x", 4, by) for by in (3, 1, 2)]
+        joint = run(x_sum_kernel, shape((32, 8, 640), BF16), terms[0], other[0], *got, grad)
     with jax.named_scope("yz_sum"):
         joint = lax.all_to_all(joint, dates, split_axis=0, concat_axis=0, tiled=True)
         total = run(yz_sum_kernel, shape((8, 8, 384), BF16), joint)
@@ -440,13 +427,7 @@
         joint, _ = lax.optimization_barrier((joint, mine))
     with jax.named_scope("expand"):
         feature_grad = run(
-            expand_kernel,
-            shape((512, width), BF16),
-            joint,
-            valid_dates.T,
-            held=(1,),
-            scratch=(pltpu.VMEM((8, 32), jnp.int32), pltpu.SemaphoreType.DMA),
-            cost=1000000,
+            expand_kernel, shape((512, width), BF16), joint, match, cost=1000000
         )
     with jax.named_scope("spread"):
         outs = spread(0, mine.reshape(4, 4, 64, 384))

time: 101 us -> 97.7 us (0.967)
  blocking collectives: 64 us -> 62.2 us
    all_to_all x1, blocking collectives: 12.3 us -> 10.8 us  [per_device(): part = lax.all_to_all(total, 'z', split_axis=0, concat_axis=0, tiled=True)]
    pallas_call x6 -> x8, Pallas kernels: 10.5 us -> 9.69 us  [run(): pl.pallas_call(kernel, out_shape=out_shape, in_specs=specs, scratch_shape...]
    ppermute x5 -> x8, waiting for transfers between devices: 9.03 us -> 8.91 us  [shift(): lax.ppermute(array, axis, [(at, (at + by) % size) for at in range(size)])]
    ppermute x5 -> x8, starting transfers between devices: 13.4 us -> 13.4 us  [shift(): lax.ppermute(array, axis, [(at, (at + by) % size) for at in range(size)])]
  transfers between devices with their start and end apart: 5 -> 8, of which waited for: 3 -> 4; matrix products, arithmetic and copies ran while one was open for 0% -> 0% of each run, Pallas kernels for 3% -> 2%
where the time goes in v9:
time: 97.7 us; the launch traced here: 97.4 us
  blocking collectives  62.2 us (64%)
  starting transfers between devices  13.4 us (14%)
  Pallas kernels  12.1 us (12%)
  waiting for transfers between devices  8.91 us (9%)
    all_to_all x1, blocking collectives, per_device(): lax.all_to_all(send.reshape(32, 16, width), dates, split_axis=0, concat_a...  21.5 us
    all_to_all x1, blocking collectives, per_device(): lax.all_to_all(part, ('y', 'x'), split_axis=0, concat_axis=0, tiled=True)  16.1 us
    all_to_all x1, blocking collectives, per_device(): lax.all_to_all(joint, dates, split_axis=0, concat_axis=0, tiled=True)  13.9 us
    ppermute x8, starting transfers between devices, shift(): lax.ppermute(array, axis, [(at, (at + by) % size) for at in range(size)])  13.4 us
    all_to_all x1, blocking collectives, per_device(): part = lax.all_to_all(total, 'z', split_axis=0, concat_axis=0, tiled=True)  10.8 us
    pallas_call x8, Pallas kernels, run(): pl.pallas_call(kernel, out_shape=out_shape, in_specs=specs, scratch_shape...  9.69 us
    ppermute x8, waiting for transfers between devices, shift(): lax.ppermute(array, axis, [(at, (at + by) % size) for at in range(size)])  8.91 us
    pallas_call x2, Pallas kernels, spread(): pl.pallas_call(functools.partial(spread_kernel, flip), out_shape=(shape((...  2.43 us
  transfers between devices with their start and end apart: 8, of which 4 were waited for; matrix products, arithmetic and copies ran while one was open for 0% of the time, Pallas kernels for 2%

profile of v9, /device:TPU:1, one launch (start us, length us, event | category | flops | bytes accessed | tf_op | source)
XLA Modules:
  0.0 97.4 jit_solution(14531547295805038922)
XLA Ops:
  0.6 1.4 %compact.1 = (bf16[512,256]{1,0:T(8,128)(2,1)S(1)}, bf16[2,128,256]{2,1,0:T(8,128)(2,1)S(1)}) custom-call(bf16[512,256]{1,0:T(8,128)(2,1)} %bitcast.15, bf16[512,256]{1,0:T(8,128)(2,1)} %bitcast.16, s32[8,32]{1,0:T(8,128)} %bitcast.19), custom_call_target="tpu_custom_call" | custom-call | tf_op jit(solution)/shard_map/compact/pallas_call | solution.py:333
  2.0 21.5 %all_to_all.20 = bf16[32,16,256]{2,1,0:T(8,128)(2,1)S(1)} all-to-all(bf16[32,16,256]{2,1,0:T(8,128)(2,1)S(1)} %bitcast.14), channel_id=1, replica_groups=mesh['y'=4,'z'=8,'x'=4,'c'=2] {'y','z'}, dimensions={0} | all-to-all | bytes 524288 | tf_op jit(solution)/shard_map/to_owner/all_to_all | solution.py:379
  23.5 7.0 %layer.1 = (bf16[256,256]{1,0:T(8,128)(2,1)S(1)}, bf16[256,384]{1,0:T(8,128)(2,1)S(1)}, bf16[256,384]{1,0:T(8,128)(2,1)S(1)}, bf16[256,384]{1,0:T(8,128)(2,1)S(1...) custom-call(bf16[512,256]{1,0:T(8,128)(2,1)S(1)} %bitcast.12, ...), custom_call_target="tpu_custom_call" | custom-call | tf_op jit(solution)/shard_map/layer/pallas_call | solution.py:333
  30.6 3.8 %collective-permute-start.1 = (bf16[256,384]{1,0:T(8,128)(2,1)S(1)}, bf16[256,384]{1,0:T(8,128)(2,1)S(1)}, u32[]{:S(2)}, u32[]{:S(2)}) collective-permute-start(bf16[256,384]{1,0:T(8,128)(2,1)S(1)} %get-tuple-element.29), channel_id=1, source_target_pairs={{0,1},{1,0},{2,3},{3,2},{4,5},{5,4},{6,7},{7,6},{8,9},{9,8},{10,11... | collective-permute-start | bytes 589832 | tf_op jit(solution)/shard_map/core_sum/ppermute | solution.py:345
  34.4 0.1 collective-permute-start.3
  34.5 0.4 collective-permute-start.5
  34.9 0.1 collective-permute-start
  35.0 0.5 collective-permute-done.1.other_ref
  35.5 2.6 %collective-permute-start.2 = (bf16[256,384]{1,0:T(8,128)(2,1)S(1)}, bf16[256,384]{1,0:T(8,128)(2,1)S(1)}, u32[]{:S(2)}, u32[]{:S(2)}) collective-permute-start(bf16[256,384]{1,0:T(8,128)(2,1)S(1)} %core_sum.3), channel_id=1, source_target_pairs={{0,6},{2,0},{4,2},{6,4},{1,7},{3,1},{5,3},{7,5},{8,14},{10,8},{12,... | collective-permute-start | bytes 589832 | tf_op jit(solution)/shard_map/x_sum/ppermute | solution.py:345
  38.1 0.1 collective-permute-start.4
  38.2 0.1 core_sum.5
  38.3 1.8 %collective-permute-start.6 = (bf16[256,384]{1,0:T(8,128)(2,1)S(1)}, bf16[256,384]{1,0:T(8,128)(2,1)S(1)}, u32[]{:S(2)}, u32[]{:S(2)}) collective-permute-start(bf16[256,384]{1,0:T(8,128)(2,1)S(1)} %core_sum.5), channel_id=1, source_target_pairs={{0,4},{2,6},{4,0},{6,2},{1,5},{3,7},{5,1},{7,3},{8,12},{10,14},{12... | collective-permute-start | bytes 589832 | tf_op jit(solution)/shard_map/x_sum/ppermute | solution.py:345
  40.1 1.9 %collective-permute-done.2.one_ref = bf16[256,384]{1,0:T(8,128)(2,1)S(1)} collective-permute-done((bf16[256,384]{1,0:T(8,128)(2,1)S(1)}, bf16[256,384]{1,0:T(8,128)(2,1)S(1)}, u32[]{:S(2)}, u32[]{:S(2)}) %collective-permute-start.2) | collective-permute-done | bytes 196640 | tf_op jit(solution)/shard_map/x_sum/ppermute | solution.py:345
  42.0 4.2 %collective-permute-done.4.two_ref = bf16[256,384]{1,0:T(8,128)(2,1)S(1)} collective-permute-done((bf16[256,384]{1,0:T(8,128)(2,1)S(1)}, bf16[256,384]{1,0:T(8,128)(2,1)S(1)}, u32[]{:S(2)}, u32[]{:S(2)}) %collective-permute-start.4) | collective-permute-done | bytes 196640 | tf_op jit(solution)/shard_map/x_sum/ppermute | solution.py:345
  46.2 2.4 %collective-permute-done.6.three_ref = bf16[256,384]{1,0:T(8,128)(2,1)S(1)} collective-permute-done((bf16[256,384]{1,0:T(8,128)(2,1)S(1)}, bf16[256,384]{1,0:T(8,128)(2,1)S(1)}, u32[]{:S(2)}, u32[]{:S(2)}) %collective-permute-start.6) | collective-permute-done | bytes 196640 | tf_op jit(solution)/shard_map/x_sum/ppermute | solution.py:345
  48.5 0.1 x_sum.1
  48.7 13.9 %all_to_all.21.joint_ref = bf16[32,8,640]{2,1,0:T(8,128)(2,1)S(1)} all-to-all(bf16[32,8,640]{2,1,0:T(8,128)(2,1)S(1)} %x_sum.1), channel_id=1, replica_groups=mesh['y'=4,'z'=8,'x'=4,'c'=2] {'y','z'}, dimensions={0} | all-to-all | bytes 655360 | tf_op jit(solution)/shard_map/yz_sum/all_to_all | solution.py:418
  62.6 10.8 %all_to_all.22 = bf16[8,8,384]{2,1,0:T(8,128)(2,1)S(1)} all-to-all(bf16[8,8,384]{2,1,0:T(8,128)(2,1)S(1)} %yz_sum.1), channel_id=1, replica_groups=mesh['y'=4,'z'=8,'x'=4,'c'=2] {'z'}, dimensions={0} | all-to-all | bytes 98304 | tf_op jit(solution)/shard_map/z_gather/all_to_all | solution.py:421
  73.3 0.1 broadcast_in_dim.8
  73.4 16.1 %all_to_all.23 = bf16[16,64,384]{2,1,0:T(8,128)(2,1)S(1)} all-to-all(bf16[16,64,384]{2,1,0:T(8,128)(2,1)S(1)} %broadcast_in_dim.8), channel_id=1, replica_groups=mesh['y'=4,'z'=8,'x'=4,'c'=2] {'y','x'}, dimensions={0} | all-to-all | bytes 1572864 | tf_op jit(solution)/shard_map/yx_gather/all_to_all | solution.py:424
  89.5 4.5 %collective-permute-start.7 = (bf16[16,64,384]{2,1,0:T(8,128)(2,1)S(1)}, bf16[16,64,384]{2,1,0:T(8,128)(2,1)S(1)}, u32[]{:S(2)}, u32[]{:S(2)}) collective-permute-start(bf16[16,64,384]{2,1,0:T(8,128)(2,1)S(1)} %all_to_all.23), channel_id=1, source_target_pairs={{0,1},{1,0},{2,3},{3,2},{4,5},{5,4},{6,7},{7,6},{8,9},{9,8},{10,11... | collective-permute-start | bytes 2359304 | tf_op jit(solution)/shard_map/core_gather/ppermute | solution.py:345
  94.0 1.2 %spread.2 = (f32[256,768]{1,0:T(8,128)}, f32[256,256]{1,0:T(8,128)}, f32[256,1024]{1,0:T(8,128)}, f32[1024,256]{1,0:T(8,128)}) custom-call(bf16[4,4,64,384]{3,2,1,0:T(8,128)(2,1)S(1)} %bitcast.11), custom_call_target="tpu_custom_call" | custom-call | bytes 3000000 | tf_op jit(solution)/shard_map/spread/pallas_call | solution.py:302
  95.3 1.0 expand.1
  96.2 1.2 %spread.3 = (f32[256,768]{1,0:T(8,128)}, f32[256,256]{1,0:T(8,128)}, f32[256,1024]{1,0:T(8,128)}, f32[1024,256]{1,0:T(8,128)}) custom-call(bf16[4,4,64,384]{3,2,1,0:T(8,128)(2,1)S(1)} %bitcast.13, f32[256,768]{1,0:T(8,128)} %get-tuple-element.37.refs_0_, ...), custom_call_target="tpu_custom_call", output_to_operand_aliasing={{0}: (1, {}), {1}: (2, {}), {2}: (3, {}), {3}: (4, {})} | custom-call | bytes 3000000 | tf_op jit(solution)/shard_map/spread/pallas_call | solution.py:302
  (7 shorter events, 0.2 us)
Async XLA Ops:
  30.6 4.9 %collective-permute-start.1 = (bf16[256,384]{1,0:T(8,128)(2,1)S(1)}, bf16[256,384]{1,0:T(8,128)(2,1)S(1)}, u32[]{:S(2)}, u32[]{:S(2)}) collective-permute-start(bf16[256,384]{1,0:T(8,128)(2,1)S(1)} %get-tuple-element.29), channel_id=1, source_target_pairs={{0,1},{1,0},{2,3},{3,2},{4,5},{5,4},{6,7},{7,6},{8,9},{9,8},{10,11... | collective-permute-start | bytes 589832 | tf_op jit(solution)/shard_map/core_sum/ppermute | solution.py:345
  34.4 3.7 %collective-permute-start.3 = (bf16[256,384]{1,0:T(8,128)(2,1)S(1)}, bf16[256,384]{1,0:T(8,128)(2,1)S(1)}, u32[]{:S(2)}, u32[]{:S(2)}) collective-permute-start(bf16[256,384]{1,0:T(8,128)(2,1)S(1)} %get-tuple-element.31), channel_id=1, source_target_pairs={{0,1},{1,0},{2,3},{3,2},{4,5},{5,4},{6,7},{7,6},{8,9},{9,8},{10,11... | collective-permute-start | bytes 589832 | tf_op jit(solution)/shard_map/core_sum/ppermute | solution.py:345
  34.5 3.7 %collective-permute-start.5 = (bf16[256,384]{1,0:T(8,128)(2,1)S(1)}, bf16[256,384]{1,0:T(8,128)(2,1)S(1)}, u32[]{:S(2)}, u32[]{:S(2)}) collective-permute-start(bf16[256,384]{1,0:T(8,128)(2,1)S(1)} %get-tuple-element.33), channel_id=1, source_target_pairs={{0,1},{1,0},{2,3},{3,2},{4,5},{5,4},{6,7},{7,6},{8,9},{9,8},{10,11... | collective-permute-start | bytes 589832 | tf_op jit(solution)/shard_map/core_sum/ppermute | solution.py:345
  34.9 5.2 %collective-permute-start = (bf16[256,384]{1,0:T(8,128)(2,1)S(1)}, bf16[256,384]{1,0:T(8,128)(2,1)S(1)}, u32[]{:S(2)}, u32[]{:S(2)}) collective-permute-start(bf16[256,384]{1,0:T(8,128)(2,1)S(1)} %get-tuple-element.27), channel_id=1, source_target_pairs={{0,1},{1,0},{2,3},{3,2},{4,5},{5,4},{6,7},{7,6},{8,9},{9,8},{10,11... | collective-permute-start | bytes 589832 | tf_op jit(solution)/shard_map/core_sum/ppermute | solution.py:345
  35.5 6.5 %collective-permute-start.2 = (bf16[256,384]{1,0:T(8,128)(2,1)S(1)}, bf16[256,384]{1,0:T(8,128)(2,1)S(1)}, u32[]{:S(2)}, u32[]{:S(2)}) collective-permute-start(bf16[256,384]{1,0:T(8,128)(2,1)S(1)} %core_sum.3), channel_id=1, source_target_pairs={{0,6},{2,0},{4,2},{6,4},{1,7},{3,1},{5,3},{7,5},{8,14},{10,8},{12,... | collective-permute-start | bytes 589832 | tf_op jit(solution)/shard_map/x_sum/ppermute | solution.py:345
  38.1 8.0 %collective-permute-start.4 = (bf16[256,384]{1,0:T(8,128)(2,1)S(1)}, bf16[256,384]{1,0:T(8,128)(2,1)S(1)}, u32[]{:S(2)}, u32[]{:S(2)}) collective-permute-start(bf16[256,384]{1,0:T(8,128)(2,1)S(1)} %core_sum.4), channel_id=1, source_target_pairs={{0,2},{2,4},{4,6},{6,0},{1,3},{3,5},{5,7},{7,1},{8,10},{10,12},{12... | collective-permute-start | bytes 589832 | tf_op jit(solution)/shard_map/x_sum/ppermute | solution.py:345
  38.3 10.2 %collective-permute-start.6 = (bf16[256,384]{1,0:T(8,128)(2,1)S(1)}, bf16[256,384]{1,0:T(8,128)(2,1)S(1)}, u32[]{:S(2)}, u32[]{:S(2)}) collective-permute-start(bf16[256,384]{1,0:T(8,128)(2,1)S(1)} %core_sum.5), channel_id=1, source_target_pairs={{0,4},{2,6},{4,0},{6,2},{1,5},{3,7},{5,1},{7,3},{8,12},{10,14},{12... | collective-permute-start | bytes 589832 | tf_op jit(solution)/shard_map/x_sum/ppermute | solution.py:345
  89.5 6.7 %collective-permute-start.7 = (bf16[16,64,384]{2,1,0:T(8,128)(2,1)S(1)}, bf16[16,64,384]{2,1,0:T(8,128)(2,1)S(1)}, u32[]{:S(2)}, u32[]{:S(2)}) collective-permute-start(bf16[16,64,384]{2,1,0:T(8,128)(2,1)S(1)} %all_to_all.23), channel_id=1, source_target_pairs={{0,1},{1,0},{2,3},{3,2},{4,5},{5,4},{6,7},{7,6},{8,9},{9,8},{10,11... | collective-permute-start | bytes 2359304 | tf_op jit(solution)/shard_map/core_gather/ppermute | solution.py:345

commit v10 on v9

--- a/solution.py
+++ b/solution.py
@@ -409,10 +409,10 @@
             ),
         )
     with jax.named_scope("core_sum"):
-        other = {by: shift(terms[4 + by], "c", 2, 1) for by in (3, 1, 2, 0)}
-        slots = {by: run(core_sum_kernel, piece, terms[by], other[by]) for by in (3, 1, 2)}
+        other = {by: shift(terms[4 + by], "c", 2, 1) for by in (2, 1, 3, 0)}
+        slots = {by: run(core_sum_kernel, piece, terms[by], other[by]) for by in (2, 1, 3)}
     with jax.named_scope("x_sum"):
-        got = [shift(slots[by], "x", 4, by) for by in (3, 1, 2)]
+        got = [shift(slots[by], "x", 4, by) for by in (2, 1, 3)]
         joint = run(x_sum_kernel, shape((32, 8, 640), BF16), terms[0], other[0], *got, grad)
     with jax.named_scope("yz_sum"):
         joint = lax.all_to_all(joint, dates, split_axis=0, concat_axis=0, tiled=True)

time: 97.7 us -> 98.1 us (level)
  waiting for transfers between devices: 8.91 us -> 7.26 us
  blocking collectives: 62.2 us -> 63.3 us
  starting transfers between devices: 13.4 us -> 14.4 us
    ppermute x8, waiting for transfers between devices: 8.91 us -> 7.26 us  [shift(): lax.ppermute(array, axis, [(at, (at + by) % size) for at in range(size)])]
    all_to_all x1, blocking collectives: 10.8 us -> 12.3 us  [per_device(): part = lax.all_to_all(total, 'z', split_axis=0, concat_axis=0, tiled=True)]
    ppermute x8, starting transfers between devices: 13.4 us -> 14.4 us  [shift(): lax.ppermute(array, axis, [(at, (at + by) % size) for at in range(size)])]
  transfers between devices with their start and end apart: 8 -> 8, of which waited for: 4 -> 3; matrix products, arithmetic and copies ran while one was open for 0% -> 0% of each run, Pallas kernels for 2% -> 2%
where the time goes in v10:
time: 98.1 us; the launch traced here: 97.8 us
  blocking collectives  63.3 us (65%)
  starting transfers between devices  14.4 us (15%)
  Pallas kernels  12.1 us (12%)
  waiting for transfers between devices  7.26 us (7%)
    all_to_all x1, blocking collectives, per_device(): lax.all_to_all(send.reshape(32, 16, width), dates, split_axis=0, concat_a...  21.5 us
    all_to_all x1, blocking collectives, per_device(): lax.all_to_all(part, ('y', 'x'), split_axis=0, concat_axis=0, tiled=True)  15.3 us
    ppermute x8, starting transfers between devices, shift(): lax.ppermute(array, axis, [(at, (at + by) % size) for at in range(size)])  14.4 us
    all_to_all x1, blocking collectives, per_device(): lax.all_to_all(joint, dates, split_axis=0, concat_axis=0, tiled=True)  14.2 us
    all_to_all x1, blocking collectives, per_device(): part = lax.all_to_all(total, 'z', split_axis=0, concat_axis=0, tiled=True)  12.3 us
    pallas_call x8, Pallas kernels, run(): pl.pallas_call(kernel, out_shape=out_shape, in_specs=specs, scratch_shape...  9.69 us
    ppermute x8, waiting for transfers between devices, shift(): lax.ppermute(array, axis, [(at, (at + by) % size) for at in range(size)])  7.26 us
    pallas_call x2, Pallas kernels, spread(): pl.pallas_call(functools.partial(spread_kernel, flip), out_shape=(shape((...  2.43 us
  transfers between devices with their start and end apart: 8, of which 3 were waited for; matrix products, arithmetic and copies ran while one was open for 0% of the time, Pallas kernels for 2%

profile of v10, /device:TPU:1, one launch (start us, length us, event | category | flops | bytes accessed | tf_op | source)
XLA Modules:
  0.0 97.8 jit_solution(16948187221232273642)
XLA Ops:
  0.6 1.4 %compact.1 = (bf16[512,256]{1,0:T(8,128)(2,1)S(1)}, bf16[2,128,256]{2,1,0:T(8,128)(2,1)S(1)}) custom-call(bf16[512,256]{1,0:T(8,128)(2,1)} %bitcast.15, bf16[512,256]{1,0:T(8,128)(2,1)} %bitcast.16, s32[8,32]{1,0:T(8,128)} %bitcast.19), custom_call_target="tpu_custom_call" | custom-call | tf_op jit(solution)/shard_map/compact/pallas_call | solution.py:333
  2.0 21.5 %all_to_all.20 = bf16[32,16,256]{2,1,0:T(8,128)(2,1)S(1)} all-to-all(bf16[32,16,256]{2,1,0:T(8,128)(2,1)S(1)} %bitcast.14), channel_id=1, replica_groups=mesh['y'=4,'z'=8,'x'=4,'c'=2] {'y','z'}, dimensions={0} | all-to-all | bytes 524288 | tf_op jit(solution)/shard_map/to_owner/all_to_all | solution.py:379
  23.5 7.0 %layer.1 = (bf16[256,256]{1,0:T(8,128)(2,1)S(1)}, bf16[256,384]{1,0:T(8,128)(2,1)S(1)}, bf16[256,384]{1,0:T(8,128)(2,1)S(1)}, bf16[256,384]{1,0:T(8,128)(2,1)S(1...) custom-call(bf16[512,256]{1,0:T(8,128)(2,1)S(1)} %bitcast.12, ...), custom_call_target="tpu_custom_call" | custom-call | tf_op jit(solution)/shard_map/layer/pallas_call | solution.py:333
  30.6 3.8 %collective-permute-start.1 = (bf16[256,384]{1,0:T(8,128)(2,1)S(1)}, bf16[256,384]{1,0:T(8,128)(2,1)S(1)}, u32[]{:S(2)}, u32[]{:S(2)}) collective-permute-start(bf16[256,384]{1,0:T(8,128)(2,1)S(1)} %get-tuple-element.29), channel_id=1, source_target_pairs={{0,1},{1,0},{2,3},{3,2},{4,5},{5,4},{6,7},{7,6},{8,9},{9,8},{10,11... | collective-permute-start | bytes 589832 | tf_op jit(solution)/shard_map/core_sum/ppermute | solution.py:345
  34.4 0.1 collective-permute-start.3
  34.5 0.4 collective-permute-start.5
  34.9 0.1 collective-permute-start
  35.0 0.5 collective-permute-done.1.other_ref
  35.5 0.1 core_sum.3
  35.5 2.8 %collective-permute-start.2 = (bf16[256,384]{1,0:T(8,128)(2,1)S(1)}, bf16[256,384]{1,0:T(8,128)(2,1)S(1)}, u32[]{:S(2)}, u32[]{:S(2)}) collective-permute-start(bf16[256,384]{1,0:T(8,128)(2,1)S(1)} %core_sum.3), channel_id=1, source_target_pairs={{0,4},{2,6},{4,0},{6,2},{1,5},{3,7},{5,1},{7,3},{8,12},{10,14},{12... | collective-permute-start | bytes 589832 | tf_op jit(solution)/shard_map/x_sum/ppermute | solution.py:345
  38.4 0.1 core_sum.4
  38.4 0.4 collective-permute-start.4
  38.9 2.4 %collective-permute-start.6 = (bf16[256,384]{1,0:T(8,128)(2,1)S(1)}, bf16[256,384]{1,0:T(8,128)(2,1)S(1)}, u32[]{:S(2)}, u32[]{:S(2)}) collective-permute-start(bf16[256,384]{1,0:T(8,128)(2,1)S(1)} %core_sum.5), channel_id=1, source_target_pairs={{0,6},{2,0},{4,2},{6,4},{1,7},{3,1},{5,3},{7,5},{8,14},{10,8},{12,... | collective-permute-start | bytes 589832 | tf_op jit(solution)/shard_map/x_sum/ppermute | solution.py:345
  41.3 1.9 %collective-permute-done.2.one_ref = bf16[256,384]{1,0:T(8,128)(2,1)S(1)} collective-permute-done((bf16[256,384]{1,0:T(8,128)(2,1)S(1)}, bf16[256,384]{1,0:T(8,128)(2,1)S(1)}, u32[]{:S(2)}, u32[]{:S(2)}) %collective-permute-start.2) | collective-permute-done | bytes 196640 | tf_op jit(solution)/shard_map/x_sum/ppermute | solution.py:345
  43.2 4.9 %collective-permute-done.4.two_ref = bf16[256,384]{1,0:T(8,128)(2,1)S(1)} collective-permute-done((bf16[256,384]{1,0:T(8,128)(2,1)S(1)}, bf16[256,384]{1,0:T(8,128)(2,1)S(1)}, u32[]{:S(2)}, u32[]{:S(2)}) %collective-permute-start.4) | collective-permute-done | bytes 196640 | tf_op jit(solution)/shard_map/x_sum/ppermute | solution.py:345
  48.1 0.1 x_sum.1
  48.2 14.2 %all_to_all.21.joint_ref = bf16[32,8,640]{2,1,0:T(8,128)(2,1)S(1)} all-to-all(bf16[32,8,640]{2,1,0:T(8,128)(2,1)S(1)} %x_sum.1), channel_id=1, replica_groups=mesh['y'=4,'z'=8,'x'=4,'c'=2] {'y','z'}, dimensions={0} | all-to-all | bytes 655360 | tf_op jit(solution)/shard_map/yz_sum/all_to_all | solution.py:418
  62.4 12.3 %all_to_all.22 = bf16[8,8,384]{2,1,0:T(8,128)(2,1)S(1)} all-to-all(bf16[8,8,384]{2,1,0:T(8,128)(2,1)S(1)} %yz_sum.1), channel_id=1, replica_groups=mesh['y'=4,'z'=8,'x'=4,'c'=2] {'z'}, dimensions={0} | all-to-all | bytes 98304 | tf_op jit(solution)/shard_map/z_gather/all_to_all | solution.py:421
  74.8 0.1 broadcast_in_dim.8
  74.9 15.3 %all_to_all.23 = bf16[16,64,384]{2,1,0:T(8,128)(2,1)S(1)} all-to-all(bf16[16,64,384]{2,1,0:T(8,128)(2,1)S(1)} %broadcast_in_dim.8), channel_id=1, replica_groups=mesh['y'=4,'z'=8,'x'=4,'c'=2] {'y','x'}, dimensions={0} | all-to-all | bytes 1572864 | tf_op jit(solution)/shard_map/yx_gather/all_to_all | solution.py:424
  90.1 4.3 %collective-permute-start.7 = (bf16[16,64,384]{2,1,0:T(8,128)(2,1)S(1)}, bf16[16,64,384]{2,1,0:T(8,128)(2,1)S(1)}, u32[]{:S(2)}, u32[]{:S(2)}) collective-permute-start(bf16[16,64,384]{2,1,0:T(8,128)(2,1)S(1)} %all_to_all.23), channel_id=1, source_target_pairs={{0,1},{1,0},{2,3},{3,2},{4,5},{5,4},{6,7},{7,6},{8,9},{9,8},{10,11... | collective-permute-start | bytes 2359304 | tf_op jit(solution)/shard_map/core_gather/ppermute | solution.py:345
  94.4 1.2 %spread.2 = (f32[256,768]{1,0:T(8,128)}, f32[256,256]{1,0:T(8,128)}, f32[256,1024]{1,0:T(8,128)}, f32[1024,256]{1,0:T(8,128)}) custom-call(bf16[4,4,64,384]{3,2,1,0:T(8,128)(2,1)S(1)} %bitcast.11), custom_call_target="tpu_custom_call" | custom-call | bytes 3000000 | tf_op jit(solution)/shard_map/spread/pallas_call | solution.py:302
  95.7 1.0 expand.1
  96.6 1.2 %spread.3 = (f32[256,768]{1,0:T(8,128)}, f32[256,256]{1,0:T(8,128)}, f32[256,1024]{1,0:T(8,128)}, f32[1024,256]{1,0:T(8,128)}) custom-call(bf16[4,4,64,384]{3,2,1,0:T(8,128)(2,1)S(1)} %bitcast.13, f32[256,768]{1,0:T(8,128)} %get-tuple-element.37.refs_0_, ...), custom_call_target="tpu_custom_call", output_to_operand_aliasing={{0}: (1, {}), {1}: (2, {}), {2}: (3, {}), {3}: (4, {})} | custom-call | bytes 3000000 | tf_op jit(solution)/shard_map/spread/pallas_call | solution.py:302
  (7 shorter events, 0.1 us)
Async XLA Ops:
  30.6 4.9 %collective-permute-start.1 = (bf16[256,384]{1,0:T(8,128)(2,1)S(1)}, bf16[256,384]{1,0:T(8,128)(2,1)S(1)}, u32[]{:S(2)}, u32[]{:S(2)}) collective-permute-start(bf16[256,384]{1,0:T(8,128)(2,1)S(1)} %get-tuple-element.29), channel_id=1, source_target_pairs={{0,1},{1,0},{2,3},{3,2},{4,5},{5,4},{6,7},{7,6},{8,9},{9,8},{10,11... | collective-permute-start | bytes 589832 | tf_op jit(solution)/shard_map/core_sum/ppermute | solution.py:345
  34.4 4.0 %collective-permute-start.3 = (bf16[256,384]{1,0:T(8,128)(2,1)S(1)}, bf16[256,384]{1,0:T(8,128)(2,1)S(1)}, u32[]{:S(2)}, u32[]{:S(2)}) collective-permute-start(bf16[256,384]{1,0:T(8,128)(2,1)S(1)} %get-tuple-element.31), channel_id=1, source_target_pairs={{0,1},{1,0},{2,3},{3,2},{4,5},{5,4},{6,7},{7,6},{8,9},{9,8},{10,11... | collective-permute-start | bytes 589832 | tf_op jit(solution)/shard_map/core_sum/ppermute | solution.py:345
  34.5 4.3 %collective-permute-start.5 = (bf16[256,384]{1,0:T(8,128)(2,1)S(1)}, bf16[256,384]{1,0:T(8,128)(2,1)S(1)}, u32[]{:S(2)}, u32[]{:S(2)}) collective-permute-start(bf16[256,384]{1,0:T(8,128)(2,1)S(1)} %get-tuple-element.33), channel_id=1, source_target_pairs={{0,1},{1,0},{2,3},{3,2},{4,5},{5,4},{6,7},{7,6},{8,9},{9,8},{10,11... | collective-permute-start | bytes 589832 | tf_op jit(solution)/shard_map/core_sum/ppermute | solution.py:345
  34.9 6.4 %collective-permute-start = (bf16[256,384]{1,0:T(8,128)(2,1)S(1)}, bf16[256,384]{1,0:T(8,128)(2,1)S(1)}, u32[]{:S(2)}, u32[]{:S(2)}) collective-permute-start(bf16[256,384]{1,0:T(8,128)(2,1)S(1)} %get-tuple-element.27), channel_id=1, source_target_pairs={{0,1},{1,0},{2,3},{3,2},{4,5},{5,4},{6,7},{7,6},{8,9},{9,8},{10,11... | collective-permute-start | bytes 589832 | tf_op jit(solution)/shard_map/core_sum/ppermute | solution.py:345
  35.5 7.7 %collective-permute-start.2 = (bf16[256,384]{1,0:T(8,128)(2,1)S(1)}, bf16[256,384]{1,0:T(8,128)(2,1)S(1)}, u32[]{:S(2)}, u32[]{:S(2)}) collective-permute-start(bf16[256,384]{1,0:T(8,128)(2,1)S(1)} %core_sum.3), channel_id=1, source_target_pairs={{0,4},{2,6},{4,0},{6,2},{1,5},{3,7},{5,1},{7,3},{8,12},{10,14},{12... | collective-permute-start | bytes 589832 | tf_op jit(solution)/shard_map/x_sum/ppermute | solution.py:345
  38.4 9.7 %collective-permute-start.4 = (bf16[256,384]{1,0:T(8,128)(2,1)S(1)}, bf16[256,384]{1,0:T(8,128)(2,1)S(1)}, u32[]{:S(2)}, u32[]{:S(2)}) collective-permute-start(bf16[256,384]{1,0:T(8,128)(2,1)S(1)} %core_sum.4), channel_id=1, source_target_pairs={{0,2},{2,4},{4,6},{6,0},{1,3},{3,5},{5,7},{7,1},{8,10},{10,12},{12... | collective-permute-start | bytes 589832 | tf_op jit(solution)/shard_map/x_sum/ppermute | solution.py:345
  38.9 9.2 %collective-permute-start.6 = (bf16[256,384]{1,0:T(8,128)(2,1)S(1)}, bf16[256,384]{1,0:T(8,128)(2,1)S(1)}, u32[]{:S(2)}, u32[]{:S(2)}) collective-permute-start(bf16[256,384]{1,0:T(8,128)(2,1)S(1)} %core_sum.5), channel_id=1, source_target_pairs={{0,6},{2,0},{4,2},{6,4},{1,7},{3,1},{5,3},{7,5},{8,14},{10,8},{12,... | collective-permute-start | bytes 589832 | tf_op jit(solution)/shard_map/x_sum/ppermute | solution.py:345
  90.1 6.5 %collective-permute-start.7 = (bf16[16,64,384]{2,1,0:T(8,128)(2,1)S(1)}, bf16[16,64,384]{2,1,0:T(8,128)(2,1)S(1)}, u32[]{:S(2)}, u32[]{:S(2)}) collective-permute-start(bf16[16,64,384]{2,1,0:T(8,128)(2,1)S(1)} %all_to_all.23), channel_id=1, source_target_pairs={{0,1},{1,0},{2,3},{3,2},{4,5},{5,4},{6,7},{7,6},{8,9},{9,8},{10,11... | collective-permute-start | bytes 2359304 | tf_op jit(solution)/shard_map/core_gather/ppermute | solution.py:345
